TPU v7x, 512 devices: a whole 4x8x8 slice. The times are simulated.
512 devices in a mesh: seq: 64 (over x, z_hi, y), ch: 8 (over z_lo, core).
Axes of the slice: x: 4, y: 8, z: 8 (z_hi: 2, z_lo: 4; z = z_hi * 4 + z_lo), core: 2. Of those that a mesh axis runs over, the one named last changes fastest.
Arguments:
- values: bfloat16 [16384, 4096], P('seq', 'ch'), may hold values from -6 to 6
- gate_in: bfloat16 [16384, 4096], P('seq', 'ch'), may hold values from -6 to 6
- gate_out: bfloat16 [16384, 4096], P('seq', 'ch'), may hold values from -6 to 6
- out_grad: bfloat16 [16384, 4096], P('seq', 'ch'), may hold values from -6 to 6
- out_proj: bfloat16 [4096, 4096], P('ch', 'seq'), may hold values from -0.09375 to 0.09375
- amplitude: float32 [8, 512, 16], P('ch', 'seq'), may hold values from -4 to 4
- decay_rate: float32 [8, 512, 16], P('ch', 'seq'), may hold values from 1.5258789e-05 to 0.033333335
- skip_gain: float32 [8, 512], P('ch', 'seq'), may hold values from -6 to 6
Outputs:
- gate_in_grad: bfloat16 [16384, 4096], P('seq', 'ch')
- gate_out_grad: bfloat16 [16384, 4096], P('seq', 'ch')
- values_grad: bfloat16 [16384, 4096], P('seq', 'ch')
- amplitude_grad: float32 [8, 512, 16], P('ch', 'seq')
- rate_grad: float32 [8, 512, 16], P('ch', 'seq')
- skip_grad: float32 [8, 512], P('ch', 'seq')
All inputs are finite; a program needn't handle non-finite values.
Results may differ from a plain program's by a relative error of at most 0.017.
Values may be sent and summed in bfloat16 or wider, within the bound.
No kernel may reach another device: no remote copies, remote signals or barrier semaphores. Data moves between devices by JAX's collectives and lax.ppermute only.
A program may use at most 64 MiB of HBM per device.

v0:
```python
import functools

import jax
import jax.numpy as jnp
from jax import lax
from jax.experimental import pallas as pl
from jax.experimental.pallas import tpu as pltpu
from jax.sharding import Mesh
from jax.sharding import PartitionSpec as P

SEQ_AXES = ("x", "zh", "y")
CH_AXES = ("zl", "core")
LANES = 128
MODES = 16
GROUP = 8
PARAMS = 2 * MODES + 1
VMEM = 48 * 1024 * 1024


def split_exact(x):
    high = lax.reduce_precision(x, 8, 7)
    rest = x - high
    middle = lax.reduce_precision(rest, 8, 7)
    return [part.astype(jnp.bfloat16) for part in (high, middle, rest - middle)]


def to_steps(dst, x, half):
    for h in range(2):
        for q in range(4):
            dst[pl.ds(h * 4 + q, half, stride=8), :] = x[
                h * half : (h + 1) * half, q * LANES : (q + 1) * LANES
            ]


def mode_tables(table, rows, d_ref, c_ref, half_ref):
    for q in range(4):
        flipped = table[q * LANES : (q + 1) * LANES, :].T
        rate = flipped[MODES : 2 * MODES]
        for h in range(2):
            at = pl.ds(h * 4 + q, MODES, stride=8)
            c_ref[at, :] = flipped[:MODES]
            d_ref[at, :] = jnp.exp(-rate)
            half_ref[at, :] = jnp.exp(-float(rows) * rate)


def local_kernel(
    steps,
    half,
    grad_ref,
    proj_ref,
    values_ref,
    gate_in_ref,
    gate_out_ref,
    gated_ref,
    table_ref,
    state_ref,
    edge_ref,
    acc,
    v_rows,
    g_rows,
    d_ref,
    c_ref,
    half_ref,
    halves,
    packed,
):
    step = pl.program_id(0)
    depth = grad_ref.shape[1]

    part = jnp.dot(grad_ref[...], proj_ref[0, :depth, :], preferred_element_type=jnp.float32)

    @pl.when(step == 0)
    def _():
        acc[...] = part

    @pl.when(step > 0)
    def _():
        acc[...] += part

    params = proj_ref[0, depth:, :].astype(jnp.float32)
    for j in range(4):
        for lane in range(4):
            piece = params[8 * j : 8 * j + 8, lane * LANES : (lane + 1) * LANES]
            piece = (
                piece
                + pltpu.roll(piece, LANES - PARAMS, 1)
                + pltpu.roll(piece, LANES - 2 * PARAMS, 1)
            )
            at = pl.multiple_of(step * 128 + 8 * (4 * j + lane), 8)
            table_ref[pl.ds(at, 8), :] = piece

    @pl.when(step == steps - 1)
    def _():
        gated = acc[...].astype(jnp.bfloat16)
        gated_ref[...] = gated
        mixed_grad = (
            (gated.astype(jnp.float32) * gate_out_ref[...].astype(jnp.float32))
            .astype(jnp.bfloat16)
            .astype(jnp.float32)
        )
        mixed_values = (
            (gate_in_ref[...].astype(jnp.float32) * values_ref[...].astype(jnp.float32))
            .astype(jnp.bfloat16)
            .astype(jnp.float32)
        )
        to_steps(g_rows, mixed_grad, half)
        to_steps(v_rows, mixed_values, half)
        mode_tables(table_ref, half, d_ref, c_ref, half_ref)
        zero = jnp.zeros((8, LANES), jnp.float32)

        for first in range(0, MODES, GROUP):
            decay = [d_ref[8 * (first + m) : 8 * (first + m) + 8, :] for m in range(GROUP)]

            def forward(t, carry):
                s, u, z, f, skip = carry
                at = pl.multiple_of(t * 8, 8)
                v = v_rows[pl.ds(at, 8), :]
                g = g_rows[pl.ds(at, 8), :]
                u = [decay[m] * (u[m] + s[m]) for m in range(GROUP)]
                s = [decay[m] * s[m] + v for m in range(GROUP)]
                z = [z[m] + g * s[m] for m in range(GROUP)]
                f = [f[m] + g * u[m] for m in range(GROUP)]
                return s, u, z, f, skip + g * v

            blank = [zero] * GROUP
            s, u, z, f, skip = lax.fori_loop(
                0, half, forward, (blank, blank, blank, blank, zero), unroll=4
            )

            def backward(i, carry):
                w, x = carry
                at = pl.multiple_of((half - 1 - i) * 8, 8)
                g = g_rows[pl.ds(at, 8), :]
                x = [decay[m] * (x[m] + w[m]) for m in range(GROUP)]
                w = [decay[m] * w[m] + g for m in range(GROUP)]
                return w, x

            w, x = lax.fori_loop(0, half, backward, (blank, blank), unroll=4)
            for a, arrays in enumerate((s, u, w, x, z, f)):
                for m in range(GROUP):
                    halves[a, first + m] = arrays[m]

        low = [halves[a, :, 0:4, :] for a in range(6)]
        high = [halves[a, :, 4:8, :] for a in range(6)]
        d = d_ref[...].reshape(MODES, 8, LANES)[:, 0:4, :]
        power = half_ref[...].reshape(MODES, 8, LANES)[:, 0:4, :]
        span = float(half)
        s0, u0, w0, x0, z0, f0 = low
        s1, u1, w1, x1, z1, f1 = high
        edge_ref[0] = s0
        edge_ref[1] = w1
        both = (
            power * s0 + s1,
            power * (u0 + span * s0) + u1,
            w0 + power * w1,
            x0 + power * (x1 + span * w1),
            z0 + z1 + s0 * (d * w1),
            f0 + f1 + d * (u0 * w1 + s0 * (x1 + w1)),
        )
        packed[...] = jnp.zeros_like(packed)
        for a in range(6):
            for m in range(MODES):
                packed[pl.ds((a * MODES + m) * 4, 4), :] = both[a][m]
        packed[pl.ds(6 * MODES * 4, 4), :] = skip[0:4] + skip[4:8]
        for q in range(4):
            state_ref[q * LANES : (q + 1) * LANES, :] = packed[pl.ds(q, LANES, stride=4), :].T


def chain_kernel(chunks, span, own_ref, state_ref, back_ref, amp_ref, rate_ref, skip_ref):
    weight = own_ref[0]
    rate = own_ref[1]
    gain = own_ref[2]
    d = jnp.exp(-rate)
    power = jnp.exp(-span * rate)
    zero = jnp.zeros((8, LANES), jnp.float32)
    lane = lax.broadcasted_iota(jnp.int32, (8, LANES), 1)

    def chunk(c):
        tile = state_ref[pl.ds(pl.multiple_of(c * 8, 8), 8), :]
        return [tile] + [pltpu.roll(tile, LANES - MODES * a, 1) for a in range(1, 7)]

    def forward(c, carry):
        s_in, u_in, z_sum, f_sum, skip_sum = carry
        s, u, w, x, z, f, skip = chunk(c)
        back_ref[pl.ds(pl.multiple_of(c * 8, 8), 8), :] = s_in
        z_sum = z_sum + z + s_in * (d * w)
        f_sum = f_sum + f + d * (u_in * w + s_in * (x + w))
        u_in = power * (u_in + span * s_in) + u
        s_in = power * s_in + s
        return s_in, u_in, z_sum, f_sum, skip_sum + skip

    _, _, zeroth, first_moment, skip_sum = lax.fori_loop(0, chunks, forward, (zero,) * 5)

    def backward(i, r_in):
        c = chunks - 1 - i
        at = pl.ds(pl.multiple_of(c * 8, 8), 8)
        w = pltpu.roll(state_ref[at, :], LANES - 2 * MODES, 1)
        back_ref[at, :] = jnp.where(lane < MODES, back_ref[at, :], pltpu.roll(r_in, MODES, 1))
        return w + power * r_in

    lax.fori_loop(0, chunks, backward, zero)
    amp_grad = gain * zeroth
    rate_grad = rate * weight * (jnp.exp(-2.0 * rate) / gain * zeroth - gain * first_moment)
    amp_ref[0] = amp_grad[:, :MODES]
    rate_ref[0] = rate_grad[:, :MODES]
    skip_ref[...] = skip_sum[:, 0:1]


def final_kernel(
    half,
    table_ref,
    edge_ref,
    carry_ref,
    gated_ref,
    values_ref,
    gate_in_ref,
    gate_out_ref,
    gate_in_grad_ref,
    gate_out_grad_ref,
    values_grad_ref,
    v_rows,
    g_rows,
    d_ref,
    c_ref,
    half_ref,
    s_ref,
    w_ref,
    skip_ref,
):
    gated = gated_ref[...].astype(jnp.float32)
    values = values_ref[...].astype(jnp.float32)
    gate_in = gate_in_ref[...].astype(jnp.float32)
    mixed_grad = (
        (gated * gate_out_ref[...].astype(jnp.float32)).astype(jnp.bfloat16).astype(jnp.float32)
    )
    mixed_values = (gate_in * values).astype(jnp.bfloat16).astype(jnp.float32)
    to_steps(g_rows, mixed_grad, half)
    to_steps(v_rows, mixed_values, half)
    mode_tables(table_ref, half, d_ref, c_ref, half_ref)
    for q in range(4):
        flipped = carry_ref[q * LANES : (q + 1) * LANES, :].T
        for h in range(2):
            at = pl.ds(h * 4 + q, MODES, stride=8)
            s_ref[at, :] = flipped[:MODES]
            w_ref[at, :] = flipped[MODES : 2 * MODES]
        gain_row = table_ref[q * LANES : (q + 1) * LANES, :].T[2 * MODES : 2 * MODES + 1]
        for h in range(2):
            skip_ref[h * 4 + q : h * 4 + q + 1, :] = gain_row
    for m in range(MODES):
        low = pl.ds(8 * m, 4)
        high = pl.ds(8 * m + 4, 4)
        s_ref[high, :] = half_ref[high, :] * s_ref[high, :] + edge_ref[0, m]
        w_ref[low, :] = half_ref[low, :] * w_ref[low, :] + edge_ref[1, m]
    decay = [d_ref[8 * m : 8 * m + 8, :] for m in range(MODES)]
    weight = [c_ref[8 * m : 8 * m + 8, :] for m in range(MODES)]
    skip = skip_ref[...]

    def total(terms):
        while len(terms) > 1:
            terms = [a + b for a, b in zip(terms[::2], terms[1::2])]
        return terms[0]

    def make(rows, reverse):
        def body(i, state):
            t = half - 1 - i if reverse else i
            at = pl.ds(pl.multiple_of(t * 8, 8), 8)
            inp = rows[at, :]
            state = [decay[m] * state[m] + inp for m in range(MODES)]
            rows[at, :] = total([weight[m] * state[m] for m in range(MODES)]) + skip * inp
            return state

        return body

    lax.fori_loop(
        0, half, make(v_rows, False), [s_ref[8 * m : 8 * m + 8, :] for m in range(MODES)], unroll=4
    )
    lax.fori_loop(
        0, half, make(g_rows, True), [w_ref[8 * m : 8 * m + 8, :] for m in range(MODES)], unroll=4
    )
    for h in range(2):
        for q in range(4):
            at = pl.ds(h * 4 + q, half, stride=8)
            rows = slice(h * half, (h + 1) * half)
            cols = slice(q * LANES, (q + 1) * LANES)
            filtered = v_rows[at, :].astype(jnp.bfloat16).astype(jnp.float32)
            back = g_rows[at, :].astype(jnp.bfloat16).astype(jnp.float32)
            gate_out_grad_ref[rows, cols] = (gated[rows, cols] * filtered).astype(jnp.bfloat16)
            gate_in_grad_ref[rows, cols] = (back * values[rows, cols]).astype(jnp.bfloat16)
            values_grad_ref[rows, cols] = (back * gate_in[rows, cols]).astype(jnp.bfloat16)


def whole(*shape):
    return pl.BlockSpec(shape, lambda *_: (0,) * len(shape))


def per_device(sizes, values, gate_in, gate_out, out_grad, out_proj, amplitude, decay_rate, skip_gain):
    rows, cols = values.shape
    half = rows // 2
    nx, nzh, ny = (sizes[a] for a in SEQ_AXES)
    chunks = nx * nzh * ny
    pencil = amplitude.shape[1]
    depth = out_proj.shape[1]

    whole_grad = lax.all_gather(out_grad, CH_AXES, axis=1, tiled=True)

    amp = amplitude.reshape(pencil, MODES)
    rate = decay_rate.reshape(pencil, MODES)
    gain = jnp.sqrt(-jnp.expm1(-2.0 * rate))
    mine = jnp.concatenate([amp * gain, rate, skip_gain.reshape(pencil, 1)], axis=1)
    tile = jnp.concatenate(
        split_exact(mine) + [jnp.zeros((pencil, cols - 3 * PARAMS), jnp.bfloat16)], axis=1
    )
    block = jnp.concatenate([out_proj.T, tile], axis=0)
    height = depth + pencil
    block = lax.all_gather(block, "zh", axis=0)
    block = lax.all_to_all(
        jnp.broadcast_to(block[None], (ny, nzh, height, cols)), "y", 0, 0, tiled=True
    )
    proj = block[:, :, :depth].transpose(1, 0, 2, 3).reshape(nzh * ny * depth, cols)
    tables = (
        block[:, :, depth:, :LANES]
        .reshape(ny // 4, 4, nzh, pencil, LANES)
        .transpose(2, 0, 3, 1, 4)
        .reshape(nzh * ny * pencil // 4, 4 * LANES)
    )
    block = jnp.concatenate([proj, tables], axis=0)
    block = lax.all_to_all(jnp.broadcast_to(block[None], (nx,) + block.shape), "x", 0, 0, tiled=True)

    group_depth = nzh * ny * depth
    f32 = jnp.float32
    gated, table, state, edge = pl.pallas_call(
        functools.partial(local_kernel, nx, half),
        grid=(nx,),
        in_specs=[
            pl.BlockSpec((rows, group_depth), lambda i: (0, i)),
            pl.BlockSpec((1,) + block.shape[1:], lambda i: (i, 0, 0)),
            whole(rows, cols),
            whole(rows, cols),
            whole(rows, cols),
        ],
        out_specs=[
            whole(rows, cols),
            whole(cols, LANES),
            whole(cols, LANES),
            whole(2, MODES, 4, LANES),
        ],
        out_shape=[
            jax.ShapeDtypeStruct((rows, cols), jnp.bfloat16),
            jax.ShapeDtypeStruct((cols, LANES), f32),
            jax.ShapeDtypeStruct((cols, LANES), f32),
            jax.ShapeDtypeStruct((2, MODES, 4, LANES), f32),
        ],
        scratch_shapes=[
            pltpu.VMEM((rows, cols), f32),
            pltpu.VMEM((half * 8, LANES), f32),
            pltpu.VMEM((half * 8, LANES), f32),
            pltpu.VMEM((MODES * 8, LANES), f32),
            pltpu.VMEM((MODES * 8, LANES), f32),
            pltpu.VMEM((MODES * 8, LANES), f32),
            pltpu.VMEM((6, MODES, 8, LANES), f32),
            pltpu.VMEM((4 * LANES, LANES), f32),
        ],
        compiler_params=pltpu.CompilerParams(vmem_limit_bytes=VMEM),
        name="project_and_scan",
    )(whole_grad, block, values, gate_in, gate_out)

    state = lax.all_to_all(state, SEQ_AXES, 0, 0, tiled=True)

    own = jnp.pad(jnp.stack([amp, rate, gain]), ((0, 0), (0, 0), (0, LANES - MODES)))
    carry, amplitude_grad, rate_grad, skip_grad = pl.pallas_call(
        functools.partial(chain_kernel, chunks, float(rows)),
        out_shape=[
            jax.ShapeDtypeStruct((cols, LANES), f32),
            jax.ShapeDtypeStruct((1, pencil, MODES), f32),
            jax.ShapeDtypeStruct((1, pencil, MODES), f32),
            jax.ShapeDtypeStruct((pencil, 1), f32),
        ],
        compiler_params=pltpu.CompilerParams(vmem_limit_bytes=VMEM),
        name="chain_chunks",
    )(own, state)

    carry = lax.all_to_all(carry, SEQ_AXES, 0, 0, tiled=True)

    gate_in_grad, gate_out_grad, values_grad = pl.pallas_call(
        functools.partial(final_kernel, half),
        out_shape=[jax.ShapeDtypeStruct((rows, cols), jnp.bfloat16)] * 3,
        scratch_shapes=[
            pltpu.VMEM((half * 8, LANES), f32),
            pltpu.VMEM((half * 8, LANES), f32),
            pltpu.VMEM((MODES * 8, LANES), f32),
            pltpu.VMEM((MODES * 8, LANES), f32),
            pltpu.VMEM((MODES * 8, LANES), f32),
            pltpu.VMEM((MODES * 8, LANES), f32),
            pltpu.VMEM((MODES * 8, LANES), f32),
            pltpu.VMEM((8, LANES), f32),
        ],
        compiler_params=pltpu.CompilerParams(vmem_limit_bytes=VMEM),
        name="final_scan",
    )(table, edge, carry, gated, values, gate_in, gate_out)

    return (
        gate_in_grad,
        gate_out_grad,
        values_grad,
        amplitude_grad,
        rate_grad,
        skip_grad.reshape(1, pencil),
    )


def solution(mesh):
    fine = Mesh(mesh.devices.reshape(4, 2, 8, 4, 2), SEQ_AXES + CH_AXES)
    grid = P(SEQ_AXES, CH_AXES)
    proj = P(CH_AXES, SEQ_AXES)
    modes = P(CH_AXES, SEQ_AXES, None)
    return jax.shard_map(
        functools.partial(per_device, dict(fine.shape)),
        mesh=fine,
        in_specs=(grid, grid, grid, grid, proj, modes, modes, proj),
        out_specs=(grid, grid, grid, modes, modes, proj),
        check_vma=False,
    )
```

profile of v0, /device:TPU:128, one launch (start us, length us, event | category | flops | bytes accessed | tf_op | source)
XLA Modules:
  0.0 199.7 jit_solution(2240458821882851124)
XLA Ops:
  7.2 0.7 copy.18
  7.9 0.7 bitcast_multiply_fusion
  8.6 0.8 reduce-precision_convert_fusion.1
  9.4 0.9 maximum_maximum_fusion
  10.3 11.0 %all-gather = bf16[144,512]{1,0:T(8,128)(2,1)S(1)} all-gather(bf16[72,512]{1,0:T(8,128)(2,1)S(1)} %maximum_maximum_fusion), channel_id=2, replica_groups=mesh['x'=4,'zh'=2,'y'=8,'zl'=4,'core'=2] {'zh'}, dimensions={0}, use_global_device_ids=true | all-gather | bytes 221184 | tf_op jit(solution)/shard_map/all_gather | solution.py:315
  21.3 1.2 broadcast_in_dim.7
  22.5 7.9 %all-to-all-start = ((bf16[8,2,72,512]{3,2,1,0:T(8,128)(2,1)}), bf16[8,2,72,512]{3,2,1,0:T(8,128)(2,1)S(1)}, u32[]{:S(2)}, u32[]{:S(2)}) async-start(bf16[8,2,72,512]{3,2,1,0:T(8,128)(2,1)} %broadcast_in_dim.7), calls=%async_computation | async-start | bytes 2359296 | tf_op jit(solution)/shard_map/all_to_all | solution.py:316
  30.4 0.0 all-gather.3.cloned.1.call-start
  30.4 0.7 all-gather.3.cloned.1.call-update
  31.1 31.0 %all-to-all-done = bf16[8,2,72,512]{3,2,1,0:T(8,128)(2,1)S(1)} async-done(((bf16[8,2,72,512]{3,2,1,0:T(8,128)(2,1)}), bf16[8,2,72,512]{3,2,1,0:T(8,128)(2,1)S(1)}, u32[]{:S(2)}, u32[]{:S(2)}) %all-to-all-start) | async-done | bytes 1179680 | tf_op jit(solution)/shard_map/all_to_all | solution.py:316
  62.0 0.1 slice.8
  62.2 0.1 copy.21
  62.3 0.1 pad_maximum_fusion
  62.3 2.4 %broadcast_in_dim.8 = bf16[4,1056,512]{2,1,0:T(8,128)(2,1)} broadcast(bf16[1056,512]{1,0:T(8,128)(2,1)S(1)} %pad_maximum_fusion), dimensions={1,2} | broadcast | bytes 5406720 | tf_op jit(solution)/shard_map/broadcast_in_dim | solution.py:327
  64.7 0.0 copy-start.1
  64.7 0.0 copy-start.2
  64.7 0.0 copy-start.3
  64.7 0.0 copy-start.4
  64.7 0.0 copy-start.5
  64.8 5.0 %all-to-all-start.1 = ((bf16[4,1056,512]{2,1,0:T(8,128)(2,1)}), bf16[4,1056,512]{2,1,0:T(8,128)(2,1)}, u32[]{:S(2)}, u32[]{:S(2)}) async-start(bf16[4,1056,512]{2,1,0:T(8,128)(2,1)} %broadcast_in_dim.8), calls=%async_computation.1 | async-start | bytes 8650752 | tf_op jit(solution)/shard_map/all_to_all | solution.py:327
  69.8 2.6 %all-gather.3.cloned.1.call-done.grad_ref = bf16[256,4096]{1,0:T(8,128)(2,1)} async-done(((bf16[256,512]{1,0:T(8,128)(2,1)}), bf16[256,4096]{1,0:T(8,128)(2,1)}) %all-gather.3.cloned.1.call-update) | async-done | bytes 2097168 | tf_op jit(solution)/shard_map/all_gather | solution.py:304
  72.3 48.2 %all-to-all-done.1.proj_ref = bf16[4,1056,512]{2,1,0:T(8,128)(2,1)} async-done(((bf16[4,1056,512]{2,1,0:T(8,128)(2,1)}), bf16[4,1056,512]{2,1,0:T(8,128)(2,1)}, u32[]{:S(2)}, u32[]{:S(2)}) %all-to-all-start.1) | async-done | bytes 4325408 | tf_op jit(solution)/shard_map/all_to_all | solution.py:327
  120.5 0.0 copy-done.1
  120.5 0.0 copy-done.2
  120.5 0.0 copy-done.3
  120.5 0.0 copy-start
  120.5 1.6 copy-done
  122.1 10.3 %project_and_scan.1 = (bf16[256,512]{1,0:T(8,128)(2,1)S(1)}, f32[512,128]{1,0:T(8,128)S(1)}, f32[512,128]{1,0:T(8,128)}, f32[2,16,4,128]{3,2,1,0:T(4,128)S(1)}) custom-call(bf16[256,4096]{1,0:T(8,128)(2,1)S(1)} %copy-done, bf16[4,1056,512]{2,1,0:T(8,128)(2,1)} %all-to-all-done.1.proj_ref, bf16[256,512]{1,0:T(8,128)(2,1)S(1)} %copy-done.1, ...), custom_call_target="tpu_custom_call" | custom-call | tf_op jit(solution)/shard_map/project_and_scan/pallas_call | solution.py:331
  132.4 7.8 %all-to-all-start.2 = ((f32[64,8,128]{2,1,0:T(8,128)}), f32[64,8,128]{2,1,0:T(8,128)S(1)}, u32[]{:S(2)}, u32[]{:S(2)}) async-start(f32[64,8,128]{2,1,0:T(8,128)} %bitcast.10), calls=%async_computation.2 | async-start | bytes 524288 | tf_op jit(solution)/shard_map/all_to_all | solution.py:367
  140.3 0.0 copy-done.4
  140.3 0.0 copy-done.5
  140.3 16.8 %all-to-all-done.2 = f32[64,8,128]{2,1,0:T(8,128)S(1)} async-done(((f32[64,8,128]{2,1,0:T(8,128)}), f32[64,8,128]{2,1,0:T(8,128)S(1)}, u32[]{:S(2)}, u32[]{:S(2)}) %all-to-all-start.2) | async-done | bytes 262176 | tf_op jit(solution)/shard_map/all_to_all | solution.py:367
  157.1 10.2 %chain_chunks.1 = (f32[512,128]{1,0:T(8,128)}, f32[1,8,16]{2,1,0:T(8,128)}, f32[1,8,16]{2,1,0:T(8,128)}, f32[8,1]{1,0:T(8,128)S(1)}) custom-call(f32[3,8,128]{2,1,0:T(8,128)S(1)} %select_maximum_fusion.own_ref, f32[512,128]{1,0:T(8,128)S(1)} %bitcast.20), custom_call_target="tpu_custom_call" | custom-call | tf_op jit(solution)/shard_map/chain_chunks/pallas_call | solution.py:370
  167.3 4.6 %all-to-all-start.3 = ((f32[64,8,128]{2,1,0:T(8,128)}), f32[64,8,128]{2,1,0:T(8,128)S(1)}, u32[]{:S(2)}, u32[]{:S(2)}) async-start(f32[64,8,128]{2,1,0:T(8,128)} %bitcast.12), calls=%async_computation.3 | async-start | bytes 524288 | tf_op jit(solution)/shard_map/all_to_all | solution.py:382
  171.9 0.6 reduce
  172.6 15.8 %all-to-all-done.3 = f32[64,8,128]{2,1,0:T(8,128)S(1)} async-done(((f32[64,8,128]{2,1,0:T(8,128)}), f32[64,8,128]{2,1,0:T(8,128)S(1)}, u32[]{:S(2)}, u32[]{:S(2)}) %all-to-all-start.3) | async-done | bytes 262176 | tf_op jit(solution)/shard_map/all_to_all | solution.py:382
  188.4 4.4 %final_scan.1 = (bf16[256,512]{1,0:T(8,128)(2,1)}, bf16[256,512]{1,0:T(8,128)(2,1)}, bf16[256,512]{1,0:T(8,128)(2,1)}) custom-call(f32[512,128]{1,0:T(8,128)S(1)} %get-tuple-element.17.table_ref, f32[2,16,4,128]{3,2,1,0:T(4,128)S(1)} %get-tuple-element.18.edge_ref, f32[512,128]{1,0:T(8,128)S(1)} %bitcast.19, ...), custom_call_target="tpu_custom_call" | custom-call | tf_op jit(solution)/shard_map/final_scan/pallas_call | solution.py:384
  (6 shorter events, 0.0 us)
Async XLA Ops:
  22.5 39.6 %all-to-all-start = ((bf16[8,2,72,512]{3,2,1,0:T(8,128)(2,1)}), bf16[8,2,72,512]{3,2,1,0:T(8,128)(2,1)S(1)}, u32[]{:S(2)}, u32[]{:S(2)}) async-start(bf16[8,2,72,512]{3,2,1,0:T(8,128)(2,1)} %broadcast_in_dim.7), calls=%async_computation | async-start | bytes 2359296 | tf_op jit(solution)/shard_map/all_to_all | solution.py:316
  30.4 42.0 %all-gather.3.cloned.1.call-start = ((), (), s32[]{:S(2)}) async-start(), calls=%async_computation.4 | async-start | bytes 2359296 | tf_op jit(solution)/shard_map/all_gather | solution.py:304
  64.7 55.8 %copy-start.1 = (bf16[256,512]{1,0:T(8,128)(2,1)S(1)}, bf16[256,512]{1,0:T(8,128)(2,1)}, u32[]{:S(2)}) copy-start(bf16[256,512]{1,0:T(8,128)(2,1)} %values_ref.3) | copy-start | bytes 786436
  64.7 55.8 %copy-start.2 = (bf16[256,512]{1,0:T(8,128)(2,1)S(1)}, bf16[256,512]{1,0:T(8,128)(2,1)}, u32[]{:S(2)}) copy-start(bf16[256,512]{1,0:T(8,128)(2,1)} %gate_in_ref.3) | copy-start | bytes 786436
  64.7 55.8 %copy-start.3 = (bf16[256,512]{1,0:T(8,128)(2,1)S(1)}, bf16[256,512]{1,0:T(8,128)(2,1)}, u32[]{:S(2)}) copy-start(bf16[256,512]{1,0:T(8,128)(2,1)} %gate_out_ref.3) | copy-start | bytes 786436
  64.7 75.6 %copy-start.4 = (f32[1,8,16]{2,1,0:T(8,128)S(1)}, f32[1,8,16]{2,1,0:T(8,128)}, u32[]{:S(2)}) copy-start(f32[1,8,16]{2,1,0:T(8,128)} %param.14) | copy-start | bytes 1540
  64.7 75.6 %copy-start.5 = (f32[1,8,16]{2,1,0:T(8,128)S(1)}, f32[1,8,16]{2,1,0:T(8,128)}, u32[]{:S(2)}) copy-start(f32[1,8,16]{2,1,0:T(8,128)} %param.13) | copy-start | bytes 1540
  64.8 55.8 %all-to-all-start.1 = ((bf16[4,1056,512]{2,1,0:T(8,128)(2,1)}), bf16[4,1056,512]{2,1,0:T(8,128)(2,1)}, u32[]{:S(2)}, u32[]{:S(2)}) async-start(bf16[4,1056,512]{2,1,0:T(8,128)(2,1)} %broadcast_in_dim.8), calls=%async_computation.1 | async-start | bytes 8650752 | tf_op jit(solution)/shard_map/all_to_all | solution.py:327
  120.5 1.6 copy-start
  132.4 24.7 %all-to-all-start.2 = ((f32[64,8,128]{2,1,0:T(8,128)}), f32[64,8,128]{2,1,0:T(8,128)S(1)}, u32[]{:S(2)}, u32[]{:S(2)}) async-start(f32[64,8,128]{2,1,0:T(8,128)} %bitcast.10), calls=%async_computation.2 | async-start | bytes 524288 | tf_op jit(solution)/shard_map/all_to_all | solution.py:367
  167.3 21.1 %all-to-all-start.3 = ((f32[64,8,128]{2,1,0:T(8,128)}), f32[64,8,128]{2,1,0:T(8,128)S(1)}, u32[]{:S(2)}, u32[]{:S(2)}) async-start(f32[64,8,128]{2,1,0:T(8,128)} %bitcast.12), calls=%async_computation.3 | async-start | bytes 524288 | tf_op jit(solution)/shard_map/all_to_all | solution.py:382
Sparse Core Ops, SparseCore 0:
  33.3 39.0 all-gather.2
where the time goes:
time: 200 us
  waiting for transfers between devices  115 us (58%)
  starting transfers between devices  25.4 us (13%)
  Pallas kernels  24.9 us (12%)
  between operations  14.2 us (7%)
  blocking collectives  11 us (6%)
  local copies, waits for them, and re-layouts  6.07 us (3%)
  other arithmetic  3.14 us (2%)
    all_to_all x1, waiting for transfers between devices, per_device(): lax.all_to_all(jnp.broadcast_to(block[None], (nx,) + block.shape), 'x', 0...  48.2 us
    all_to_all x1, waiting for transfers between devices, per_device(): lax.all_to_all(jnp.broadcast_to(block[None], (ny, nzh, height, cols)), 'y...  31 us
    all_to_all x1, waiting for transfers between devices, per_device(): state = lax.all_to_all(state, SEQ_AXES, 0, 0, tiled=True)  16.8 us
    all_to_all x1, waiting for transfers between devices, per_device(): carry = lax.all_to_all(carry, SEQ_AXES, 0, 0, tiled=True)  15.8 us
    all_gather x1, blocking collectives, per_device(): block = lax.all_gather(block, 'zh', axis=0)  11 us
    pallas_call x1, Pallas kernels, per_device(): pl.pallas_call(functools.partial(local_kernel, nx, half), grid=(nx,), in_...  10.3 us
    pallas_call x1, Pallas kernels, per_device(): pl.pallas_call(functools.partial(chain_kernel, chunks, float(rows)), out_...  10.2 us
    all_to_all x1, starting transfers between devices, per_device(): lax.all_to_all(jnp.broadcast_to(block[None], (ny, nzh, height, cols)), 'y...  7.89 us
  transfers between devices with their start and end apart: 5, of which 5 were waited for; matrix products, arithmetic and copies ran while one was open for 2% of the time, Pallas kernels for 0%

commit v1 on v0

v1 whole, which is shorter than its diff:
```python
import functools

import jax
import jax.numpy as jnp
from jax import lax
from jax.experimental import pallas as pl
from jax.experimental.pallas import tpu as pltpu
from jax.sharding import Mesh
from jax.sharding import PartitionSpec as P

SEQ_AXES = ("x", "zh", "y")
CH_AXES = ("zl", "core")
LANES = 128
MODES = 16
GROUP = 8
PARAMS = 2 * MODES + 1
VMEM = 48 * 1024 * 1024


def to_steps(dst, x, half):
    for h in range(2):
        for q in range(4):
            dst[pl.ds(h * 4 + q, half, stride=8), :] = x[
                h * half : (h + 1) * half, q * LANES : (q + 1) * LANES
            ]


def steps_at(t):
    return pl.ds(pl.multiple_of(t * 8, 8), 8)


def mode_at(m):
    return slice(8 * m, 8 * m + 8)


def value_kernel(half, table_ref, values_ref, gate_in_ref, tables_ref, skip_ref, v_rows, ends_ref):
    for q in range(4):
        flipped = table_ref[q * LANES : (q + 1) * LANES, :].T
        rate = flipped[MODES : 2 * MODES]
        for h in range(2):
            at = pl.ds(h * 4 + q, MODES, stride=8)
            tables_ref[0, at, :] = flipped[:MODES]
            tables_ref[1, at, :] = jnp.exp(-rate)
            tables_ref[2, at, :] = jnp.exp(-float(half) * rate)
            skip_ref[h * 4 + q : h * 4 + q + 1, :] = flipped[2 * MODES : 2 * MODES + 1]
    mixed_values = (
        (gate_in_ref[...].astype(jnp.float32) * values_ref[...].astype(jnp.float32))
        .astype(jnp.bfloat16)
        .astype(jnp.float32)
    )
    to_steps(v_rows, mixed_values, half)
    zero = jnp.zeros((8, LANES), jnp.float32)
    decay = [tables_ref[1, mode_at(m), :] for m in range(MODES)]

    def forward(t, carry):
        s, u = carry
        v = v_rows[steps_at(t), :]
        u = [decay[m] * (u[m] + s[m]) for m in range(MODES)]
        s = [decay[m] * s[m] + v for m in range(MODES)]
        return s, u

    s, u = lax.fori_loop(0, half, forward, ([zero] * MODES, [zero] * MODES), unroll=4)
    for m in range(MODES):
        ends_ref[0, m] = s[m]
        ends_ref[1, m] = u[m]


def product_kernel(core_ref, own_ref, other_ref, proj_ref, out_ref):
    core = core_ref[0]
    pieces, _, depth, cols = proj_ref.shape
    own = proj_ref[:, pl.ds(core, 1)].reshape(pieces * depth, cols)
    other = proj_ref[:, pl.ds(1 - core, 1)].reshape(pieces * depth, cols)
    total = jnp.dot(own_ref[0], own, preferred_element_type=jnp.float32)
    total += jnp.dot(other_ref[0], other, preferred_element_type=jnp.float32)
    out_ref[0] = total.astype(jnp.bfloat16)


def gradient_kernel(
    half,
    parts_ref,
    gate_out_ref,
    tables_ref,
    v_rows,
    ends_ref,
    gated_ref,
    g_rows,
    state_ref,
    edge_ref,
    halves,
    packed,
):
    gated = parts_ref[0].astype(jnp.float32)
    for k in range(1, parts_ref.shape[0]):
        gated += parts_ref[k].astype(jnp.float32)
    gated = gated.astype(jnp.bfloat16)
    gated_ref[...] = gated
    mixed_grad = (
        (gated.astype(jnp.float32) * gate_out_ref[...].astype(jnp.float32))
        .astype(jnp.bfloat16)
        .astype(jnp.float32)
    )
    to_steps(g_rows, mixed_grad, half)
    zero = jnp.zeros((8, LANES), jnp.float32)
    blank = [zero] * GROUP

    for first in range(0, MODES, GROUP):
        decay = [tables_ref[1, mode_at(first + m), :] for m in range(GROUP)]

        def backward(i, carry):
            w, x, z, f, skip = carry
            at = steps_at(half - 1 - i)
            g = g_rows[at, :]
            v = v_rows[at, :]
            x = [decay[m] * (x[m] + w[m]) for m in range(GROUP)]
            w = [decay[m] * w[m] + g for m in range(GROUP)]
            z = [z[m] + v * w[m] for m in range(GROUP)]
            f = [f[m] + v * x[m] for m in range(GROUP)]
            return w, x, z, f, skip + g * v

        w, x, z, f, skip = lax.fori_loop(
            0, half, backward, (blank, blank, blank, blank, zero), unroll=4
        )
        for a, arrays in enumerate((w, x, z, f)):
            for m in range(GROUP):
                halves[a, first + m] = arrays[m]

    s0, u0 = (ends_ref[a, :, 0:4, :] for a in range(2))
    s1, u1 = (ends_ref[a, :, 4:8, :] for a in range(2))
    w0, x0, z0, f0 = (halves[a, :, 0:4, :] for a in range(4))
    w1, x1, z1, f1 = (halves[a, :, 4:8, :] for a in range(4))
    d = tables_ref[1].reshape(MODES, 8, LANES)[:, 0:4, :]
    power = tables_ref[2].reshape(MODES, 8, LANES)[:, 0:4, :]
    span = float(half)
    edge_ref[0] = s0
    edge_ref[1] = w1
    both = (
        power * s0 + s1,
        power * (u0 + span * s0) + u1,
        w0 + power * w1,
        x0 + power * (x1 + span * w1),
        z0 + z1 + s0 * (d * w1),
        f0 + f1 + d * (u0 * w1 + s0 * (x1 + w1)),
    )
    packed[...] = jnp.zeros_like(packed)
    for a in range(6):
        for m in range(MODES):
            packed[pl.ds((a * MODES + m) * 4, 4), :] = both[a][m]
    packed[pl.ds(6 * MODES * 4, 4), :] = skip[0:4] + skip[4:8]
    for q in range(4):
        state_ref[q * LANES : (q + 1) * LANES, :] = packed[pl.ds(q, LANES, stride=4), :].T


def chain_kernel(
    chunks, span, own_ref, state_ref, back_ref, amp_ref, rate_ref, skip_ref, parts, s_rows, r_rows
):
    weight = own_ref[0]
    rate = own_ref[1]
    gain = own_ref[2]
    d = jnp.exp(-rate)
    power = jnp.exp(-span * rate)
    zero = jnp.zeros((8, LANES), jnp.float32)
    state = state_ref[...]
    for a in range(1, 7):
        parts[a - 1] = pltpu.roll(state, LANES - MODES * a, 1)

    def step(c, carry):
        s_in, u_in, z_sum, f_sum, skip_sum, r_in = carry
        at = steps_at(c)
        s = state_ref[at, :]
        u, w, x, z, f, skip = (parts[a, at, :] for a in range(6))
        s_rows[at, :] = s_in
        z_sum = z_sum + z + s_in * (d * w)
        f_sum = f_sum + f + d * (u_in * w + s_in * (x + w))
        u_in = power * (u_in + span * s_in) + u
        s_in = power * s_in + s
        last = steps_at(chunks - 1 - c)
        r_rows[last, :] = r_in
        r_in = parts[1, last, :] + power * r_in
        return s_in, u_in, z_sum, f_sum, skip_sum + skip, r_in

    _, _, zeroth, first_moment, skip_sum, _ = lax.fori_loop(
        0, chunks, step, (zero,) * 6, unroll=8
    )
    lane = lax.broadcasted_iota(jnp.int32, back_ref.shape, 1)
    back_ref[...] = jnp.where(lane < MODES, s_rows[...], pltpu.roll(r_rows[...], MODES, 1))
    amp_grad = gain * zeroth
    rate_grad = rate * weight * (jnp.exp(-2.0 * rate) / gain * zeroth - gain * first_moment)
    amp_ref[0] = amp_grad[:, :MODES]
    rate_ref[0] = rate_grad[:, :MODES]
    skip_ref[...] = skip_sum[:, 0:1]


def final_kernel(
    half,
    tables_ref,
    skip_ref,
    edge_ref,
    carry_ref,
    v_rows,
    g_rows,
    gated_ref,
    values_ref,
    gate_in_ref,
    gate_in_grad_ref,
    gate_out_grad_ref,
    values_grad_ref,
    s_ref,
    w_ref,
    filtered_rows,
    back_rows,
):
    for q in range(4):
        flipped = carry_ref[q * LANES : (q + 1) * LANES, :].T
        for h in range(2):
            at = pl.ds(h * 4 + q, MODES, stride=8)
            s_ref[at, :] = flipped[:MODES]
            w_ref[at, :] = flipped[MODES : 2 * MODES]
    for m in range(MODES):
        low = pl.ds(8 * m, 4)
        high = pl.ds(8 * m + 4, 4)
        s_ref[high, :] = tables_ref[2, high, :] * s_ref[high, :] + edge_ref[0, m]
        w_ref[low, :] = tables_ref[2, low, :] * w_ref[low, :] + edge_ref[1, m]
    weight = [tables_ref[0, mode_at(m), :] for m in range(MODES)]
    decay = [tables_ref[1, mode_at(m), :] for m in range(MODES)]
    skip = skip_ref[...]

    def total(terms):
        while len(terms) > 1:
            terms = [a + b for a, b in zip(terms[::2], terms[1::2])]
        return terms[0]

    def make(rows, out, reverse):
        def body(i, state):
            at = steps_at(half - 1 - i if reverse else i)
            inp = rows[at, :]
            state = [decay[m] * state[m] + inp for m in range(MODES)]
            out[at, :] = total([weight[m] * state[m] for m in range(MODES)]) + skip * inp
            return state

        return body

    for rows, out, ref, reverse in (
        (v_rows, filtered_rows, s_ref, False),
        (g_rows, back_rows, w_ref, True),
    ):
        lax.fori_loop(
            0, half, make(rows, out, reverse), [ref[mode_at(m), :] for m in range(MODES)], unroll=4
        )
    for h in range(2):
        for q in range(4):
            at = pl.ds(h * 4 + q, half, stride=8)
            rows = slice(h * half, (h + 1) * half)
            cols = slice(q * LANES, (q + 1) * LANES)
            filtered = filtered_rows[at, :].astype(jnp.bfloat16).astype(jnp.float32)
            back = back_rows[at, :].astype(jnp.bfloat16).astype(jnp.float32)
            gated = gated_ref[rows, cols].astype(jnp.float32)
            values = values_ref[rows, cols].astype(jnp.float32)
            gate_in = gate_in_ref[rows, cols].astype(jnp.float32)
            gate_out_grad_ref[rows, cols] = (gated * filtered).astype(jnp.bfloat16)
            gate_in_grad_ref[rows, cols] = (back * values).astype(jnp.bfloat16)
            values_grad_ref[rows, cols] = (back * gate_in).astype(jnp.bfloat16)


def whole(*shape):
    return pl.BlockSpec(shape, lambda *_: (0,) * len(shape))


def call(kernel, out_shape, scratch, name, **more):
    return pl.pallas_call(
        kernel,
        out_shape=out_shape,
        scratch_shapes=[pltpu.VMEM(shape, jnp.float32) for shape in scratch],
        compiler_params=pltpu.CompilerParams(vmem_limit_bytes=VMEM),
        name=name,
        **more,
    )


def repeated(x, times):
    return jnp.broadcast_to(x[None], (times,) + x.shape)


def per_device(sizes, values, gate_in, gate_out, out_grad, out_proj, amplitude, decay_rate, skip_gain):
    rows, cols = values.shape
    half = rows // 2
    nx, nzh, ny = (sizes[a] for a in SEQ_AXES)
    chunks = nx * nzh * ny
    pencil = amplitude.shape[1]
    f32, bf16 = jnp.float32, jnp.bfloat16
    shape = jax.ShapeDtypeStruct
    exchange = functools.partial(lax.all_to_all, split_axis=0, concat_axis=0, tiled=True)

    columns = exchange(repeated(out_grad, nx), "zl")
    proj = exchange(repeated(out_proj.T, nzh), "zh")
    proj = exchange(repeated(proj, ny), "y")
    own = exchange(columns, "x")
    other = lax.ppermute(own, "core", [(0, 1), (1, 0)])
    core = lax.axis_index("core").astype(jnp.int32).reshape(1)
    parts = pl.pallas_call(
        product_kernel,
        grid=(nx,),
        in_specs=[
            pl.BlockSpec(memory_space=pltpu.SMEM),
            pl.BlockSpec((1, rows, cols), lambda i: (i, 0, 0)),
            pl.BlockSpec((1, rows, cols), lambda i: (i, 0, 0)),
            whole(*proj.shape),
        ],
        out_specs=pl.BlockSpec((1, rows, cols), lambda i: (i, 0, 0)),
        out_shape=shape((nx, rows, cols), bf16),
        compiler_params=pltpu.CompilerParams(vmem_limit_bytes=VMEM),
        name="partial_products",
    )(core, own, other, proj)
    parts = exchange(parts, "x")

    amp = amplitude.reshape(pencil, MODES)
    rate = decay_rate.reshape(pencil, MODES)
    gain = jnp.sqrt(-jnp.expm1(-2.0 * rate))
    mine = jnp.concatenate([amp * gain, rate, skip_gain.reshape(pencil, 1)], axis=1)
    mine = jnp.pad(mine, ((0, 0), (0, LANES - PARAMS)))
    table = exchange(repeated(mine, chunks), SEQ_AXES).reshape(cols, LANES)
    tables, skip, v_rows, ends = call(
        functools.partial(value_kernel, half),
        [
            shape((3, MODES * 8, LANES), f32),
            shape((8, LANES), f32),
            shape((half * 8, LANES), f32),
            shape((2, MODES, 8, LANES), f32),
        ],
        [],
        "value_scan",
    )(table, values, gate_in)

    gated, g_rows, state, edge = call(
        functools.partial(gradient_kernel, half),
        [
            shape((rows, cols), bf16),
            shape((half * 8, LANES), f32),
            shape((cols, LANES), f32),
            shape((2, MODES, 4, LANES), f32),
        ],
        [(4, MODES, 8, LANES), (4 * LANES, LANES)],
        "gradient_scan",
    )(parts, gate_out, tables, v_rows, ends)

    state = exchange(state, SEQ_AXES)
    own_modes = jnp.pad(jnp.stack([amp, rate, gain]), ((0, 0), (0, 0), (0, LANES - MODES)))
    carry, amplitude_grad, rate_grad, skip_grad = call(
        functools.partial(chain_kernel, chunks, float(rows)),
        [
            shape((cols, LANES), f32),
            shape((1, pencil, MODES), f32),
            shape((1, pencil, MODES), f32),
            shape((pencil, 1), f32),
        ],
        [(6, cols, LANES), (cols, LANES), (cols, LANES)],
        "chain_chunks",
    )(own_modes, state)
    carry = exchange(carry, SEQ_AXES)

    gate_in_grad, gate_out_grad, values_grad = call(
        functools.partial(final_kernel, half),
        [shape((rows, cols), bf16)] * 3,
        [(MODES * 8, LANES), (MODES * 8, LANES), (half * 8, LANES), (half * 8, LANES)],
        "final_scan",
    )(tables, skip, edge, carry, v_rows, g_rows, gated, values, gate_in)

    return (
        gate_in_grad,
        gate_out_grad,
        values_grad,
        amplitude_grad,
        rate_grad,
        skip_grad.reshape(1, pencil),
    )


def solution(mesh):
    fine = Mesh(mesh.devices.reshape(4, 2, 8, 4, 2), SEQ_AXES + CH_AXES)
    grid = P(SEQ_AXES, CH_AXES)
    proj = P(CH_AXES, SEQ_AXES)
    modes = P(CH_AXES, SEQ_AXES, None)
    return jax.shard_map(
        functools.partial(per_device, dict(fine.shape)),
        mesh=fine,
        in_specs=(grid, grid, grid, grid, proj, modes, modes, proj),
        out_specs=(grid, grid, grid, modes, modes, proj),
        check_vma=False,
    )
```

time: 200 us -> 188 us (0.940)
  the two profiles are of different devices: /device:TPU:128 before, /device:TPU:8 now
where the time goes in v1:
time: 188 us
  waiting for transfers between devices  75.9 us (40%)
  blocking collectives  65 us (35%)
  starting transfers between devices  28.7 us (15%)
  Pallas kernels  13 us (7%)
  local copies, waits for them, and re-layouts  3.59 us (2%)
    all_to_all x1, blocking collectives, per_device(): columns = exchange(repeated(out_grad, nx), 'zl')  27.8 us
    all_to_all x1, waiting for transfers between devices, per_device(): proj = exchange(repeated(proj, ny), 'y')  22.5 us
    all_to_all x1, blocking collectives, per_device(): proj = exchange(repeated(out_proj.T, nzh), 'zh')  19.4 us
    all_to_all x1, blocking collectives, per_device(): own = exchange(columns, 'x')  17.8 us
    all_to_all x1, waiting for transfers between devices, per_device(): state = exchange(state, SEQ_AXES)  15.7 us
    all_to_all x1, waiting for transfers between devices, per_device(): carry = exchange(carry, SEQ_AXES)  15.1 us
    all_to_all x1, waiting for transfers between devices, per_device(): table = exchange(repeated(mine, chunks), SEQ_AXES).reshape(cols, LANES)  13 us
    all_to_all x1, waiting for transfers between devices, per_device(): parts = exchange(parts, 'x')  9.72 us
  transfers between devices with their start and end apart: 6, of which 5 were waited for; matrix products, arithmetic and copies ran while one was open for 1% of the time, Pallas kernels for 2%

profile of v1, /device:TPU:8, one launch (start us, length us, event | category | flops | bytes accessed | tf_op | source)
XLA Modules:
  0.0 187.7 jit_solution(368592892087378035)
XLA Ops:
  0.6 0.0 copy-start.4
  0.6 0.9 broadcast_in_dim.10
  1.5 19.4 %all_to_all.52 = bf16[2,64,512]{2,1,0:T(8,128)(2,1)S(1)} all-to-all(bf16[2,64,512]{2,1,0:T(8,128)(2,1)S(1)} %broadcast_in_dim.10), channel_id=1, replica_groups=mesh['x'=4,'zh'=2,'y'=8,'zl'=4,'core'=2] {'zh'}, dimensions={0} | all-to-all | bytes 262144 | tf_op jit(solution)/shard_map/all_to_all | solution.py:294
  21.0 0.0 copy-done.4
  21.0 0.1 broadcast_in_dim.9
  21.0 27.8 %all_to_all.53 = bf16[4,256,512]{2,1,0:T(8,128)(2,1)S(1)} all-to-all(bf16[4,256,512]{2,1,0:T(8,128)(2,1)S(1)} %broadcast_in_dim.9), channel_id=1, replica_groups=mesh['x'=4,'zh'=2,'y'=8,'zl'=4,'core'=2] {'zl'}, dimensions={0} | all-to-all | bytes 2097152 | tf_op jit(solution)/shard_map/all_to_all | solution.py:293
  48.8 17.8 %all_to_all.54.own_ref = bf16[4,256,512]{2,1,0:T(8,128)(2,1)S(1)} all-to-all(bf16[4,256,512]{2,1,0:T(8,128)(2,1)S(1)} %all_to_all.53), channel_id=1, replica_groups=mesh['x'=4,'zh'=2,'y'=8,'zl'=4,'core'=2] {'x'}, dimensions={0} | all-to-all | bytes 2097152 | tf_op jit(solution)/shard_map/all_to_all | solution.py:296
  66.6 1.1 broadcast_in_dim.11
  67.7 0.0 copy-start.7
  67.7 0.0 copy-start.6
  67.7 7.7 %all-to-all-start.4 = ((bf16[8,2,64,512]{3,2,1,0:T(8,128)(2,1)}), bf16[8,2,64,512]{3,2,1,0:T(8,128)(2,1)S(1)}, u32[]{:S(2)}, u32[]{:S(2)}) async-start(bf16[8,2,64,512]{3,2,1,0:T(8,128)(2,1)} %broadcast_in_dim.11), calls=%async_computation.4 | async-start | bytes 2097152 | tf_op jit(solution)/shard_map/all_to_all | solution.py:295
  75.4 0.0 copy-start.5
  75.4 2.0 %collective-permute-start = (bf16[4,256,512]{2,1,0:T(8,128)(2,1)S(1)}, bf16[4,256,512]{2,1,0:T(8,128)(2,1)S(1)}, u32[]{:S(2)}, u32[]{:S(2)}) collective-permute-start(bf16[4,256,512]{2,1,0:T(8,128)(2,1)S(1)} %all_to_all.54.own_ref), channel_id=1, source_target_pairs={{0,1},{1,0},{2,3},{3,2},{4,5},{5,4},{6,7},{7,6},{8,9},{9,8},{10,11... | collective-permute-start | bytes 3145736 | tf_op jit(solution)/shard_map/ppermute | solution.py:297
  77.4 0.0 copy-done.7
  77.5 0.1 copy.15
  77.5 0.0 copy-done.6
  77.5 0.0 copy-done.5
  77.6 0.1 select_maximum_fusion.2
  77.6 22.5 %all-to-all-done.4.proj_ref = bf16[8,2,64,512]{3,2,1,0:T(8,128)(2,1)S(1)} async-done(((bf16[8,2,64,512]{3,2,1,0:T(8,128)(2,1)}), bf16[8,2,64,512]{3,2,1,0:T(8,128)(2,1)S(1)}, u32[]{:S(2)}, u32[]{:S(2)}) %all-to-all-start.4) | async-done | bytes 1048608 | tf_op jit(solution)/shard_map/all_to_all | solution.py:295
  100.1 0.7 broadcast_in_dim.8
  100.8 5.5 %all-to-all-start = ((f32[64,8,128]{2,1,0:T(8,128)}), f32[64,8,128]{2,1,0:T(8,128)S(1)}, u32[]{:S(2)}, u32[]{:S(2)}) async-start(f32[64,8,128]{2,1,0:T(8,128)} %broadcast_in_dim.8), calls=%async_computation | async-start | bytes 524288 | tf_op jit(solution)/shard_map/all_to_all | solution.py:320
  106.4 0.0 collective-permute-done.other_ref
  106.4 2.7 %partial_products.1 = bf16[4,256,512]{2,1,0:T(8,128)(2,1)} custom-call(s32[1]{0:T(128)} %bitcast.4.core_ref, bf16[4,256,512]{2,1,0:T(8,128)(2,1)S(1)} %all_to_all.54.own_ref, bf16[4,256,512]{2,1,0:T(8,128)(2,1)S(1)} %collective-permute-done.other_ref, bf16[8,2,64,512]{3,2,1,0:T(8,128)(2,1)S(1)} %all-to-all-done.4.proj_ref), custom_call_target="tpu_custom_call" | custom-call | tf_op jit(solution)/shard_map/partial_products/pallas_call | solution.py:299
  109.1 0.0 copy-start
  109.1 0.0 copy-start.1
  109.1 13.0 %all-to-all-done = f32[64,8,128]{2,1,0:T(8,128)S(1)} async-done(((f32[64,8,128]{2,1,0:T(8,128)}), f32[64,8,128]{2,1,0:T(8,128)S(1)}, u32[]{:S(2)}, u32[]{:S(2)}) %all-to-all-start) | async-done | bytes 262176 | tf_op jit(solution)/shard_map/all_to_all | solution.py:320
  122.1 3.5 %all-to-all-start.5 = ((bf16[4,256,512]{2,1,0:T(8,128)(2,1)}), bf16[4,256,512]{2,1,0:T(8,128)(2,1)S(1)}, u32[]{:S(2)}, u32[]{:S(2)}) async-start(bf16[4,256,512]{2,1,0:T(8,128)(2,1)} %partial_products.1), calls=%async_computation.5 | async-start | bytes 2097152 | tf_op jit(solution)/shard_map/all_to_all | solution.py:313
  125.7 0.0 copy-done
  125.7 0.0 copy-done.1
  125.7 0.0 copy-start.2
  125.7 1.6 value_scan.1
  127.3 9.7 %all-to-all-done.5.parts_ref = bf16[4,256,512]{2,1,0:T(8,128)(2,1)S(1)} async-done(((bf16[4,256,512]{2,1,0:T(8,128)(2,1)}), bf16[4,256,512]{2,1,0:T(8,128)(2,1)S(1)}, u32[]{:S(2)}, u32[]{:S(2)}) %all-to-all-start.5) | async-done | bytes 1048608 | tf_op jit(solution)/shard_map/all_to_all | solution.py:313
  137.0 0.0 copy-done.2
  137.0 3.3 %gradient_scan.1 = (bf16[256,512]{1,0:T(8,128)(2,1)S(1)}, f32[1024,128]{1,0:T(8,128)S(1)}, f32[512,128]{1,0:T(8,128)S(1)}, f32[2,16,4,128]{3,2,1,0:T(4,128)S(1)}) custom-call(bf16[4,256,512]{2,1,0:T(8,128)(2,1)S(1)} %all-to-all-done.5.parts_ref, bf16[256,512]{1,0:T(8,128)(2,1)S(1)} %copy-done.2, f32[3,128,128]{2,1,0:T(8,128)S(1)} %get-tuple-element.21.tables_ref, ...), custom_call_target="tpu_custom_call" | custom-call | tf_op jit(solution)/shard_map/gradient_scan/pallas_call | solution.py:333
  140.3 0.0 copy-start.3
  140.3 0.7 copy-done.3
  141.0 4.9 %all-to-all-start.6 = ((f32[64,8,128]{2,1,0:T(8,128)}), f32[64,8,128]{2,1,0:T(8,128)S(1)}, u32[]{:S(2)}, u32[]{:S(2)}) async-start(f32[64,8,128]{2,1,0:T(8,128)} %bitcast.16), calls=%async_computation.6 | async-start | bytes 524288 | tf_op jit(solution)/shard_map/all_to_all | solution.py:345
  146.0 15.7 %all-to-all-done.6 = f32[64,8,128]{2,1,0:T(8,128)S(1)} async-done(((f32[64,8,128]{2,1,0:T(8,128)}), f32[64,8,128]{2,1,0:T(8,128)S(1)}, u32[]{:S(2)}, u32[]{:S(2)}) %all-to-all-start.6) | async-done | bytes 262176 | tf_op jit(solution)/shard_map/all_to_all | solution.py:345
  161.7 1.6 chain_chunks.1
  163.3 5.0 %all-to-all-start.7 = ((f32[64,8,128]{2,1,0:T(8,128)}), f32[64,8,128]{2,1,0:T(8,128)S(1)}, u32[]{:S(2)}, u32[]{:S(2)}) async-start(f32[64,8,128]{2,1,0:T(8,128)} %bitcast.8), calls=%async_computation.7 | async-start | bytes 524288 | tf_op jit(solution)/shard_map/all_to_all | solution.py:358
  168.3 0.6 reduce
  168.9 15.1 %all-to-all-done.7 = f32[64,8,128]{2,1,0:T(8,128)S(1)} async-done(((f32[64,8,128]{2,1,0:T(8,128)}), f32[64,8,128]{2,1,0:T(8,128)S(1)}, u32[]{:S(2)}, u32[]{:S(2)}) %all-to-all-start.7) | async-done | bytes 262176 | tf_op jit(solution)/shard_map/all_to_all | solution.py:358
  184.0 3.7 %final_scan.1 = (bf16[256,512]{1,0:T(8,128)(2,1)}, bf16[256,512]{1,0:T(8,128)(2,1)}, bf16[256,512]{1,0:T(8,128)(2,1)}) custom-call(f32[3,128,128]{2,1,0:T(8,128)S(1)} %get-tuple-element.21.tables_ref, f32[8,128]{1,0:T(8,128)S(1)} %get-tuple-element.22.skip_ref, f32[2,16,4,128]{3,2,1,0:T(4,128)S(1)} %get-tuple-element.25.edge_ref, f32[512,128]{1,0:T(8,128)S(1)} %bitcast.14, ...), custom_call_target="tpu_custom_call" | custom-call | tf_op jit(solution)/shard_map/final_scan/pallas_call | solution.py:360
  (3 shorter events, 0.0 us)
Async XLA Ops:
  0.6 20.3 %copy-start.4 = (bf16[256,512]{1,0:T(8,128)(2,1)S(1)}, bf16[256,512]{1,0:T(8,128)(2,1)}, u32[]{:S(2)}) copy-start(bf16[256,512]{1,0:T(8,128)(2,1)} %param.11) | copy-start | bytes 786436
  67.7 9.7 %copy-start.7 = (f32[1,8]{1,0:T(1,128)S(1)}, f32[1,8]{1,0:T(1,128)}, u32[]{:S(2)}) copy-start(f32[1,8]{1,0:T(1,128)} %param.15) | copy-start | bytes 100
  67.7 9.8 %copy-start.6 = (f32[1,8,16]{2,1,0:T(8,128)S(1)}, f32[1,8,16]{2,1,0:T(8,128)}, u32[]{:S(2)}) copy-start(f32[1,8,16]{2,1,0:T(8,128)} %param.13) | copy-start | bytes 1540
  67.7 32.4 %all-to-all-start.4 = ((bf16[8,2,64,512]{3,2,1,0:T(8,128)(2,1)}), bf16[8,2,64,512]{3,2,1,0:T(8,128)(2,1)S(1)}, u32[]{:S(2)}, u32[]{:S(2)}) async-start(bf16[8,2,64,512]{3,2,1,0:T(8,128)(2,1)} %broadcast_in_dim.11), calls=%async_computation.4 | async-start | bytes 2097152 | tf_op jit(solution)/shard_map/all_to_all | solution.py:295
  75.4 2.1 %copy-start.5 = (f32[1,8,16]{2,1,0:T(8,128)S(1)}, f32[1,8,16]{2,1,0:T(8,128)}, u32[]{:S(2)}) copy-start(f32[1,8,16]{2,1,0:T(8,128)} %param.14) | copy-start | bytes 1540
  75.4 31.0 %collective-permute-start = (bf16[4,256,512]{2,1,0:T(8,128)(2,1)S(1)}, bf16[4,256,512]{2,1,0:T(8,128)(2,1)S(1)}, u32[]{:S(2)}, u32[]{:S(2)}) collective-permute-start(bf16[4,256,512]{2,1,0:T(8,128)(2,1)S(1)} %all_to_all.54.own_ref), channel_id=1, source_target_pairs={{0,1},{1,0},{2,3},{3,2},{4,5},{5,4},{6,7},{7,6},{8,9},{9,8},{10,11... | collective-permute-start | bytes 3145736 | tf_op jit(solution)/shard_map/ppermute | solution.py:297
  100.8 21.3 %all-to-all-start = ((f32[64,8,128]{2,1,0:T(8,128)}), f32[64,8,128]{2,1,0:T(8,128)S(1)}, u32[]{:S(2)}, u32[]{:S(2)}) async-start(f32[64,8,128]{2,1,0:T(8,128)} %broadcast_in_dim.8), calls=%async_computation | async-start | bytes 524288 | tf_op jit(solution)/shard_map/all_to_all | solution.py:320
  109.1 16.5 %copy-start = (bf16[256,512]{1,0:T(8,128)(2,1)S(1)}, bf16[256,512]{1,0:T(8,128)(2,1)}, u32[]{:S(2)}) copy-start(bf16[256,512]{1,0:T(8,128)(2,1)} %values_ref.3) | copy-start | bytes 786436
  109.1 16.5 %copy-start.1 = (bf16[256,512]{1,0:T(8,128)(2,1)S(1)}, bf16[256,512]{1,0:T(8,128)(2,1)}, u32[]{:S(2)}) copy-start(bf16[256,512]{1,0:T(8,128)(2,1)} %gate_in_ref.3) | copy-start | bytes 786436
  122.1 14.9 %all-to-all-start.5 = ((bf16[4,256,512]{2,1,0:T(8,128)(2,1)}), bf16[4,256,512]{2,1,0:T(8,128)(2,1)S(1)}, u32[]{:S(2)}, u32[]{:S(2)}) async-start(bf16[4,256,512]{2,1,0:T(8,128)(2,1)} %partial_products.1), calls=%async_computation.5 | async-start | bytes 2097152 | tf_op jit(solution)/shard_map/all_to_all | solution.py:313
  125.7 11.3 %copy-start.2 = (bf16[256,512]{1,0:T(8,128)(2,1)S(1)}, bf16[256,512]{1,0:T(8,128)(2,1)}, u32[]{:S(2)}) copy-start(bf16[256,512]{1,0:T(8,128)(2,1)} %gate_out_ref.1) | copy-start | bytes 786436
  140.3 0.7 copy-start.3
  141.0 20.7 %all-to-all-start.6 = ((f32[64,8,128]{2,1,0:T(8,128)}), f32[64,8,128]{2,1,0:T(8,128)S(1)}, u32[]{:S(2)}, u32[]{:S(2)}) async-start(f32[64,8,128]{2,1,0:T(8,128)} %bitcast.16), calls=%async_computation.6 | async-start | bytes 524288 | tf_op jit(solution)/shard_map/all_to_all | solution.py:345
  163.3 20.7 %all-to-all-start.7 = ((f32[64,8,128]{2,1,0:T(8,128)}), f32[64,8,128]{2,1,0:T(8,128)S(1)}, u32[]{:S(2)}, u32[]{:S(2)}) async-start(f32[64,8,128]{2,1,0:T(8,128)} %bitcast.8), calls=%async_computation.7 | async-start | bytes 524288 | tf_op jit(solution)/shard_map/all_to_all | solution.py:358

commit v2 on v1

v2 whole, which is shorter than its diff:
```python
import functools

import jax
import jax.numpy as jnp
from jax import lax
from jax.experimental import pallas as pl
from jax.experimental.pallas import tpu as pltpu
from jax.sharding import Mesh
from jax.sharding import PartitionSpec as P

SEQ_AXES = ("x", "zh", "y")
CH_AXES = ("zl", "core")
LANES = 128
MODES = 16
GROUP = 8
PARAMS = 2 * MODES + 1
VMEM = 48 * 1024 * 1024


def split_exact(x):
    high = lax.reduce_precision(x, 8, 7)
    rest = x - high
    middle = lax.reduce_precision(rest, 8, 7)
    return [part.astype(jnp.bfloat16) for part in (high, middle, rest - middle)]


def to_steps(dst, x, half):
    for h in range(2):
        for q in range(4):
            dst[pl.ds(h * 4 + q, half, stride=8), :] = x[
                h * half : (h + 1) * half, q * LANES : (q + 1) * LANES
            ]


def steps_at(t):
    return pl.ds(pl.multiple_of(t * 8, 8), 8)


def mode_at(m):
    return slice(8 * m, 8 * m + 8)


def product_kernel(place_ref, own_ref, other_ref, proj_ref, out_ref):
    core = place_ref[0]
    ring, pair, height, cols = proj_ref.shape
    depth = height - 8
    rows = own_ref.shape[1]
    count = ring * pair

    def rows_of(c):
        return proj_ref[:, pl.ds(c, 1), 0:depth, :].reshape(ring * depth, cols)

    total = jnp.dot(own_ref[0], rows_of(core), preferred_element_type=jnp.float32)
    total += jnp.dot(other_ref[0], rows_of(1 - core), preferred_element_type=jnp.float32)
    out_ref[0, 0:rows, :] = total.astype(jnp.bfloat16)
    pieces = [proj_ref[j % ring, j // ring, :, 0:LANES].astype(jnp.float32)[depth:] for j in range(count)]
    params = [jnp.concatenate(pieces[j : j + 4], axis=1) for j in range(0, count, 4)]
    out_ref[0, rows:, :] = jnp.concatenate(params, axis=0).astype(jnp.bfloat16)


def local_kernel(
    half,
    place_ref,
    parts_ref,
    values_ref,
    gate_in_ref,
    gate_out_ref,
    gated_ref,
    tables_ref,
    skip_ref,
    v_rows,
    g_rows,
    send_ref,
    edge_ref,
    rate_ref,
    own_table_ref,
    table,
    halves,
    packed,
    state,
):
    sources = parts_ref.shape[0]
    rows = 2 * half
    for k in range(sources):
        params = parts_ref[k, rows:, :].astype(jnp.float32)
        for j in range(16):
            piece = params[8 * (j // 4) : 8 * (j // 4) + 8, (j % 4) * LANES : (j % 4 + 1) * LANES]
            piece = (
                piece
                + pltpu.roll(piece, LANES - PARAMS, 1)
                + pltpu.roll(piece, LANES - 2 * PARAMS, 1)
            )
            table[128 * k + 8 * j : 128 * k + 8 * j + 8, :] = piece
    for q in range(4):
        flipped = table[q * LANES : (q + 1) * LANES, :].T
        rate = flipped[MODES : 2 * MODES]
        rate_ref[pl.ds(q, MODES, stride=4), :] = rate
        for h in range(2):
            at = pl.ds(h * 4 + q, MODES, stride=8)
            tables_ref[0, at, :] = flipped[:MODES]
            tables_ref[1, at, :] = jnp.exp(-rate)
            tables_ref[2, at, :] = jnp.exp(-float(half) * rate)
            skip_ref[h * 4 + q : h * 4 + q + 1, :] = flipped[2 * MODES : 2 * MODES + 1]
    mixed_values = (
        (gate_in_ref[...].astype(jnp.float32) * values_ref[...].astype(jnp.float32))
        .astype(jnp.bfloat16)
        .astype(jnp.float32)
    )
    to_steps(v_rows, mixed_values, half)
    gated = parts_ref[0, 0:rows, :].astype(jnp.float32)
    for k in range(1, sources):
        gated += parts_ref[k, 0:rows, :].astype(jnp.float32)
    gated = gated.astype(jnp.bfloat16)
    gated_ref[...] = gated
    mixed_grad = (
        (gated.astype(jnp.float32) * gate_out_ref[...].astype(jnp.float32))
        .astype(jnp.bfloat16)
        .astype(jnp.float32)
    )
    to_steps(g_rows, mixed_grad, half)
    zero = jnp.zeros((8, LANES), jnp.float32)
    decay = [tables_ref[1, mode_at(m), :] for m in range(MODES)]

    def forward(t, carry):
        s, u = carry
        v = v_rows[steps_at(t), :]
        u = [decay[m] * (u[m] + s[m]) for m in range(MODES)]
        s = [decay[m] * s[m] + v for m in range(MODES)]
        return s, u

    s, u = lax.fori_loop(0, half, forward, ([zero] * MODES, [zero] * MODES), unroll=4)
    for a, arrays in enumerate((s, u)):
        for m in range(MODES):
            halves[a, m] = arrays[m]

    blank = [zero] * GROUP
    for first in range(0, MODES, GROUP):
        decay = [tables_ref[1, mode_at(first + m), :] for m in range(GROUP)]

        def backward(i, carry):
            w, x, z, f, skip = carry
            at = steps_at(half - 1 - i)
            g = g_rows[at, :]
            v = v_rows[at, :]
            x = [decay[m] * (x[m] + w[m]) for m in range(GROUP)]
            w = [decay[m] * w[m] + g for m in range(GROUP)]
            z = [z[m] + v * w[m] for m in range(GROUP)]
            f = [f[m] + v * x[m] for m in range(GROUP)]
            return w, x, z, f, skip + g * v

        w, x, z, f, skip = lax.fori_loop(
            0, half, backward, (blank, blank, blank, blank, zero), unroll=4
        )
        for a, arrays in enumerate((w, x, z, f)):
            for m in range(GROUP):
                halves[2 + a, first + m] = arrays[m]

    s0, u0, w0, x0, z0, f0 = (halves[a, :, 0:4, :] for a in range(6))
    s1, u1, w1, x1, z1, f1 = (halves[a, :, 4:8, :] for a in range(6))
    d = tables_ref[1].reshape(MODES, 8, LANES)[:, 0:4, :]
    power = tables_ref[2].reshape(MODES, 8, LANES)[:, 0:4, :]
    span = float(half)
    edge_ref[0] = s0
    edge_ref[1] = w1
    both = (
        power * s0 + s1,
        power * (u0 + span * s0) + u1,
        w0 + power * w1,
        x0 + power * (x1 + span * w1),
        z0 + z1 + s0 * (d * w1),
        f0 + f1 + d * (u0 * w1 + s0 * (x1 + w1)),
    )
    packed[...] = jnp.zeros_like(packed)
    for a in range(6):
        for m in range(MODES):
            packed[pl.ds((a * MODES + m) * 4, 4), :] = both[a][m]
    packed[pl.ds(6 * MODES * 4, 4), :] = skip[0:4] + skip[4:8]
    for q in range(4):
        state[q * LANES : (q + 1) * LANES, :] = packed[pl.ds(q, LANES, stride=4), :].T
    peers = send_ref.shape[0]
    groups = packed.shape[0] // (8 * peers)
    every = jnp.concatenate(
        [packed[0 : 4 * MODES, :], packed[8 * MODES : 12 * MODES, :]], axis=0
    ).astype(jnp.bfloat16)
    for y in range(peers):
        send_ref[y, 0 : 8 * MODES, :] = every
        mine = jnp.concatenate(
            [state[8 * (peers * g + y) : 8 * (peers * g + y) + 8, :] for g in range(groups)], axis=0
        )
        high = mine.astype(jnp.bfloat16)
        low = (mine - high.astype(jnp.float32)).astype(jnp.bfloat16)
        send_ref[y, 8 * MODES : 8 * MODES + 8 * groups, :] = high
        send_ref[y, 8 * MODES + 8 * groups :, :] = low
    for g in range(groups):
        at = pl.multiple_of(8 * (peers * g + place_ref[1]), 8)
        own_table_ref[8 * g : 8 * g + 8, :] = table[pl.ds(at, 8), :]


def chained(chunks, rate, span):
    d = jnp.exp(-rate)
    power = jnp.exp(-span * rate)
    parts = [
        [c] + [pltpu.roll(c, LANES - MODES * a, 1) for a in range(1, 7)] for c in chunks
    ]
    s_in, u_in, w_in, x_in, z_sum, f_sum, skip_sum = (jnp.zeros_like(chunks[0]),) * 7
    for s, u, w, x, z, f, skip in parts:
        z_sum = z_sum + z + s_in * (d * w)
        f_sum = f_sum + f + d * (u_in * w + s_in * (x + w))
        u_in = power * (u_in + span * s_in) + u
        s_in = power * s_in + s
        skip_sum = skip_sum + skip
    for _, _, w, x, _, _, _ in parts[::-1]:
        x_in = x + power * (x_in + span * w_in)
        w_in = w + power * w_in
    return s_in, u_in, w_in, x_in, z_sum, f_sum, skip_sum


def neighbours(s, w, power, index):
    count = len(s)
    before = after = total = rest = jnp.zeros_like(s[0])
    for c in range(count):
        before = jnp.where(index == c, total, before)
        total = power * total + s[c]
    for c in range(count - 1, -1, -1):
        after = jnp.where(index == c, rest, after)
        rest = power * rest + w[c]
    return before, after, total, rest


def group_kernel(span, place_ref, recv_ref, rate_ref, own_table_ref, send_ref, near_ref):
    peers = recv_ref.shape[0]
    groups = send_ref.shape[0]
    many = 4 * MODES
    s = [recv_ref[c, 0:many, :].astype(jnp.float32) for c in range(peers)]
    w = [recv_ref[c, many : 2 * many, :].astype(jnp.float32) for c in range(peers)]
    power = jnp.exp(-span * rate_ref[...])
    before, after, total, rest = neighbours(s, w, power, place_ref[1])
    near_ref[0] = before
    near_ref[1] = after
    every = jnp.concatenate([total, rest], axis=0).astype(jnp.bfloat16)
    high = slice(2 * many, 2 * many + 8 * groups)
    low = slice(2 * many + 8 * groups, 2 * many + 16 * groups)
    sums = [
        recv_ref[c, high, :].astype(jnp.float32) + recv_ref[c, low, :].astype(jnp.float32)
        for c in range(peers)
    ]
    rate = pltpu.roll(own_table_ref[...], LANES - MODES, 1)
    lane = lax.broadcasted_iota(jnp.int32, rate.shape, 1)
    rate = jnp.where(lane < MODES, rate, 0.0)
    packed = jnp.zeros_like(rate)
    for a, part in enumerate(chained(sums, rate, span)):
        packed += pltpu.roll(jnp.where(lane < MODES, part, 0.0), MODES * a, 1)
    first = packed.astype(jnp.bfloat16).astype(jnp.float32)
    second = packed - first
    for g in range(groups):
        send_ref[g, 0 : 2 * many, :] = every
        at = slice(8 * g, 8 * g + 8)
        send_ref[g, 2 * many :, :] = jnp.concatenate([first[at], second[at]], axis=0).astype(
            jnp.bfloat16
        )


def final_kernel(
    half,
    ring,
    place_ref,
    own_ref,
    recv_ref,
    near_ref,
    rate_ref,
    tables_ref,
    skip_ref,
    edge_ref,
    v_rows,
    g_rows,
    gated_ref,
    values_ref,
    gate_in_ref,
    gate_in_grad_ref,
    gate_out_grad_ref,
    values_grad_ref,
    amp_ref,
    rate_grad_ref,
    skip_grad_ref,
    s_ref,
    w_ref,
    filtered_rows,
    back_rows,
):
    groups = recv_ref.shape[0]
    many = 4 * MODES
    span = 2.0 * half
    s = [recv_ref[g, 0:many, :].astype(jnp.float32) for g in range(groups)]
    w = [recv_ref[g, many : 2 * many, :].astype(jnp.float32) for g in range(groups)]
    rate = rate_ref[...]
    before, after, _, _ = neighbours(s, w, jnp.exp(-(span * ring) * rate), place_ref[2])
    y = place_ref[1].astype(jnp.float32)
    s_in = near_ref[0] + jnp.exp(-(span * y) * rate) * before
    w_in = near_ref[1] + jnp.exp(-(span * (ring - 1.0 - y)) * rate) * after
    for m in range(MODES):
        low = pl.ds(8 * m, 4)
        high = pl.ds(8 * m + 4, 4)
        at = slice(4 * m, 4 * m + 4)
        s_ref[low, :] = s_in[at]
        s_ref[high, :] = tables_ref[2, high, :] * s_in[at] + edge_ref[0, m]
        w_ref[low, :] = tables_ref[2, low, :] * w_in[at] + edge_ref[1, m]
        w_ref[high, :] = w_in[at]
    weight = [tables_ref[0, mode_at(m), :] for m in range(MODES)]
    decay = [tables_ref[1, mode_at(m), :] for m in range(MODES)]
    skip = skip_ref[...]

    def total(terms):
        while len(terms) > 1:
            terms = [a + b for a, b in zip(terms[::2], terms[1::2])]
        return terms[0]

    def make(rows, out, reverse):
        def body(i, state):
            at = steps_at(half - 1 - i if reverse else i)
            inp = rows[at, :]
            state = [decay[m] * state[m] + inp for m in range(MODES)]
            out[at, :] = total([weight[m] * state[m] for m in range(MODES)]) + skip * inp
            return state

        return body

    for rows, out, ref, reverse in (
        (v_rows, filtered_rows, s_ref, False),
        (g_rows, back_rows, w_ref, True),
    ):
        lax.fori_loop(
            0, half, make(rows, out, reverse), [ref[mode_at(m), :] for m in range(MODES)], unroll=4
        )
    for h in range(2):
        for q in range(4):
            at = pl.ds(h * 4 + q, half, stride=8)
            rows = slice(h * half, (h + 1) * half)
            cols = slice(q * LANES, (q + 1) * LANES)
            filtered = filtered_rows[at, :].astype(jnp.bfloat16).astype(jnp.float32)
            back = back_rows[at, :].astype(jnp.bfloat16).astype(jnp.float32)
            gated = gated_ref[rows, cols].astype(jnp.float32)
            values = values_ref[rows, cols].astype(jnp.float32)
            gate_in = gate_in_ref[rows, cols].astype(jnp.float32)
            gate_out_grad_ref[rows, cols] = (gated * filtered).astype(jnp.bfloat16)
            gate_in_grad_ref[rows, cols] = (back * values).astype(jnp.bfloat16)
            values_grad_ref[rows, cols] = (back * gate_in).astype(jnp.bfloat16)

    sums = [recv_ref[g, 2 * many :, :].astype(jnp.float32) for g in range(groups)]
    own_weight, own_rate, gain = (own_ref[a] for a in range(3))
    done = chained([x[0:8] + x[8:16] for x in sums], own_rate, span * ring)
    zeroth, first_moment = done[4], done[5]
    amp_grad = gain * zeroth
    rate_grad = own_rate * own_weight * (
        jnp.exp(-2.0 * own_rate) / gain * zeroth - gain * first_moment
    )
    amp_ref[0] = amp_grad[:, :MODES]
    rate_grad_ref[0] = rate_grad[:, :MODES]
    skip_grad_ref[...] = done[6][:, 0:1]


def whole(*shape):
    return pl.BlockSpec(shape, lambda *_: (0,) * len(shape))


def call(kernel, out_shape, scratch, name, **more):
    return pl.pallas_call(
        kernel,
        out_shape=out_shape,
        scratch_shapes=[pltpu.VMEM(shape, jnp.float32) for shape in scratch],
        compiler_params=pltpu.CompilerParams(vmem_limit_bytes=VMEM),
        name=name,
        **more,
    )


def repeated(x, times):
    return jnp.broadcast_to(x[None], (times,) + x.shape)


def per_device(sizes, values, gate_in, gate_out, out_grad, out_proj, amplitude, decay_rate, skip_gain):
    rows, cols = values.shape
    half = rows // 2
    nx, nzh, ny = (sizes[a] for a in SEQ_AXES)
    chunks = nx * nzh * ny
    pencil = amplitude.shape[1]
    f32, bf16 = jnp.float32, jnp.bfloat16
    shape = jax.ShapeDtypeStruct
    exchange = functools.partial(lax.all_to_all, split_axis=0, concat_axis=0, tiled=True)

    amp = amplitude.reshape(pencil, MODES)
    rate = decay_rate.reshape(pencil, MODES)
    gain = jnp.sqrt(-jnp.expm1(-2.0 * rate))
    mine = jnp.concatenate([amp * gain, rate, skip_gain.reshape(pencil, 1)], axis=1)
    tile = jnp.concatenate(
        split_exact(mine) + [jnp.zeros((pencil, cols - 3 * PARAMS), bf16)], axis=1
    )
    block = jnp.concatenate([out_proj.T, tile], axis=0)
    there = lax.ppermute(block, "zh", [(0, 1), (1, 0)])
    zh = lax.axis_index("zh")
    block = jnp.stack([jnp.where(zh == 0, block, there), jnp.where(zh == 0, there, block)])
    proj = exchange(repeated(block, ny), "y")

    tiles = []
    for k in range(nx):
        moves = [(a * nx + b, b * nx + (a + k) % nx) for a in range(nx) for b in range(nx)]
        tiles.append(lax.ppermute(out_grad, ("x", "zl"), moves))
    own = jnp.stack(tiles)
    other = lax.ppermute(own, "core", [(0, 1), (1, 0)])
    place = jnp.stack(
        [lax.axis_index("core"), lax.axis_index("y"), lax.axis_index(("x", "zh")), lax.axis_index("zl")]
    ).astype(jnp.int32)
    height = rows + nzh * ny * pencil // 4
    parts = pl.pallas_call(
        product_kernel,
        grid_spec=pltpu.PrefetchScalarGridSpec(
            num_scalar_prefetch=1,
            grid=(nx,),
            in_specs=[
                pl.BlockSpec((1, rows, cols), lambda k, place: (k, 0, 0)),
                pl.BlockSpec((1, rows, cols), lambda k, place: (k, 0, 0)),
                whole(*proj.shape),
            ],
            out_specs=pl.BlockSpec(
                (1, height, cols), lambda k, place: (lax.rem(place[3] + nx - k, nx), 0, 0)
            ),
        ),
        out_shape=shape((nx, height, cols), bf16),
        compiler_params=pltpu.CompilerParams(vmem_limit_bytes=VMEM),
        name="partial_products",
    )(place, own, other, proj)
    parts = exchange(parts, "x")

    smem = pl.BlockSpec(memory_space=pltpu.SMEM)
    vmem = pl.BlockSpec(memory_space=pltpu.VMEM)
    many = 4 * MODES
    groups = nx * nzh
    gated, tables, skip, v_rows, g_rows, send, edge, rates, own_table = call(
        functools.partial(local_kernel, half),
        [
            shape((rows, cols), bf16),
            shape((3, MODES * 8, LANES), f32),
            shape((8, LANES), f32),
            shape((half * 8, LANES), f32),
            shape((half * 8, LANES), f32),
            shape((ny, 2 * many + 16 * groups, LANES), bf16),
            shape((2, MODES, 4, LANES), f32),
            shape((many, LANES), f32),
            shape((8 * groups, LANES), f32),
        ],
        [(cols, LANES), (6, MODES, 8, LANES), (4 * LANES, LANES), (cols, LANES)],
        "local_scans",
        in_specs=[smem] + [vmem] * 4,
    )(place, parts, values, gate_in, gate_out)

    recv = exchange(send, "y")
    send, near = call(
        functools.partial(group_kernel, float(rows)),
        [shape((groups, 2 * many + 16, LANES), bf16), shape((2, many, LANES), f32)],
        [],
        "chain_ring",
        in_specs=[smem] + [vmem] * 3,
    )(place, recv, rates, own_table)

    recv = exchange(send, ("x", "zh"))
    own_modes = jnp.pad(jnp.stack([amp, rate, gain]), ((0, 0), (0, 0), (0, LANES - MODES)))
    gate_in_grad, gate_out_grad, values_grad, amplitude_grad, rate_grad, skip_grad = call(
        functools.partial(final_kernel, half, float(ny)),
        [shape((rows, cols), bf16)] * 3
        + [shape((1, pencil, MODES), f32)] * 2
        + [shape((pencil, 1), f32)],
        [(MODES * 8, LANES), (MODES * 8, LANES), (half * 8, LANES), (half * 8, LANES)],
        "final_scan",
        in_specs=[smem] + [vmem] * 12,
    )(
        place,
        own_modes,
        recv,
        near,
        rates,
        tables,
        skip,
        edge,
        v_rows,
        g_rows,
        gated,
        values,
        gate_in,
    )

    return (
        gate_in_grad,
        gate_out_grad,
        values_grad,
        amplitude_grad,
        rate_grad,
        skip_grad.reshape(1, pencil),
    )


def solution(mesh):
    fine = Mesh(mesh.devices.reshape(4, 2, 8, 4, 2), SEQ_AXES + CH_AXES)
    grid = P(SEQ_AXES, CH_AXES)
    proj = P(CH_AXES, SEQ_AXES)
    modes = P(CH_AXES, SEQ_AXES, None)
    return jax.shard_map(
        functools.partial(per_device, dict(fine.shape)),
        mesh=fine,
        in_specs=(grid, grid, grid, grid, proj, modes, modes, proj),
        out_specs=(grid, grid, grid, modes, modes, proj),
        check_vma=False,
    )
```

time: 188 us -> 144 us (0.77)
  the two profiles are of different devices: /device:TPU:8 before, /device:TPU:64 now
where the time goes in v2:
time: 144 us; the launch traced here: 143 us
  blocking collectives  46 us (32%)
  starting transfers between devices  43.5 us (30%)
  waiting for transfers between devices  32.4 us (22%)
  Pallas kernels  14.3 us (10%)
  other arithmetic  4.21 us (3%)
  local copies, waits for them, and re-layouts  1.93 us (1%)
    all_to_all x1, blocking collectives, per_device(): recv = exchange(send, 'y')  23.1 us
    all_to_all x1, blocking collectives, per_device(): parts = exchange(parts, 'x')  22.9 us
    ppermute x4, starting transfers between devices, per_device(): tiles.append(lax.ppermute(out_grad, ('x', 'zl'), moves))  16.8 us
    ppermute x4, waiting for transfers between devices, per_device(): tiles.append(lax.ppermute(out_grad, ('x', 'zl'), moves))  16.3 us
    all_to_all x1, waiting for transfers between devices, per_device(): recv = exchange(send, ('x', 'zh'))  11.3 us
    ppermute x1, starting transfers between devices, per_device(): there = lax.ppermute(block, 'zh', [(0, 1), (1, 0)])  10 us
    all_to_all x1, starting transfers between devices, per_device(): recv = exchange(send, ('x', 'zh'))  7.54 us
    all_to_all x1, starting transfers between devices, per_device(): proj = exchange(repeated(block, ny), 'y')  7.23 us
  transfers between devices with their start and end apart: 8, of which 5 were waited for; matrix products, arithmetic and copies ran while one was open for 0% of the time, Pallas kernels for 0%

profile of v2, /device:TPU:64, one launch (start us, length us, event | category | flops | bytes accessed | tf_op | source)
XLA Modules:
  0.0 143.2 jit_solution(14122554644511578517)
XLA Ops:
  0.6 0.7 copy.15
  1.4 0.7 bitcast_multiply_fusion
  2.1 0.8 reduce-precision_convert_fusion.1
  2.9 0.9 maximum_maximum_fusion
  3.8 10.0 %collective-permute-start.5 = (bf16[72,512]{1,0:T(8,128)(2,1)S(1)}, bf16[72,512]{1,0:T(8,128)(2,1)S(1)}, u32[]{:S(2)}, u32[]{:S(2)}) collective-permute-start(bf16[72,512]{1,0:T(8,128)(2,1)S(1)} %maximum_maximum_fusion), channel_id=1, source_target_pairs={{0,64},{64,0},{1,65},{65,1},{2,66},{66,2},{3,67},{67,3},{4,68},{68... | collective-permute-start | bytes 221192 | tf_op jit(solution)/shard_map/ppermute | solution.py:398
  13.8 2.3 %collective-permute-done.5 = bf16[72,512]{1,0:T(8,128)(2,1)S(1)} collective-permute-done((bf16[72,512]{1,0:T(8,128)(2,1)S(1)}, bf16[72,512]{1,0:T(8,128)(2,1)S(1)}, u32[]{:S(2)}, u32[]{:S(2)}) %collective-permute-start.5) | collective-permute-done | bytes 73760 | tf_op jit(solution)/shard_map/ppermute | solution.py:398
  16.1 0.9 select_bitcast_fusion.1
  17.1 1.2 broadcast_in_dim.10
  18.2 0.0 copy-start.5
  18.2 7.2 %all-to-all-start = ((bf16[8,2,72,512]{3,2,1,0:T(8,128)(2,1)}), bf16[8,2,72,512]{3,2,1,0:T(8,128)(2,1)S(1)}, u32[]{:S(2)}, u32[]{:S(2)}) async-start(bf16[8,2,72,512]{3,2,1,0:T(8,128)(2,1)} %broadcast_in_dim.10), calls=%async_computation | async-start | bytes 2359296 | tf_op jit(solution)/shard_map/all_to_all | solution.py:401
  25.5 0.0 copy-done.5
  25.5 4.4 %collective-permute-start = (bf16[256,512]{1,0:T(8,128)(2,1)S(1)}, bf16[256,512]{1,0:T(8,128)(2,1)S(1)}, u32[]{:S(2)}, u32[]{:S(2)}) collective-permute-start(bf16[256,512]{1,0:T(8,128)(2,1)S(1)} %copy-done.5), channel_id=1, source_target_pairs={{0,0},{2,128},{4,256},{6,384},{128,2},{130,130},{132,258},{134,386... | collective-permute-start | bytes 786440 | tf_op jit(solution)/shard_map/ppermute | solution.py:406
  29.9 1.9 %collective-permute-start.1 = (bf16[256,512]{1,0:T(8,128)(2,1)S(1)}, bf16[256,512]{1,0:T(8,128)(2,1)S(1)}, u32[]{:S(2)}, u32[]{:S(2)}) collective-permute-start(bf16[256,512]{1,0:T(8,128)(2,1)S(1)} %copy-done.5), channel_id=1, source_target_pairs={{0,2},{2,130},{4,258},{6,386},{128,4},{130,132},{132,260},{134,388... | collective-permute-start | bytes 786440 | tf_op jit(solution)/shard_map/ppermute | solution.py:406
  31.8 3.6 %collective-permute-start.2 = (bf16[256,512]{1,0:T(8,128)(2,1)S(1)}, bf16[256,512]{1,0:T(8,128)(2,1)S(1)}, u32[]{:S(2)}, u32[]{:S(2)}) collective-permute-start(bf16[256,512]{1,0:T(8,128)(2,1)S(1)} %copy-done.5), channel_id=1, source_target_pairs={{0,4},{2,132},{4,260},{6,388},{128,6},{130,134},{132,262},{134,390... | collective-permute-start | bytes 786440 | tf_op jit(solution)/shard_map/ppermute | solution.py:406
  35.5 6.8 %collective-permute-start.3 = (bf16[256,512]{1,0:T(8,128)(2,1)S(1)}, bf16[256,512]{1,0:T(8,128)(2,1)S(1)}, u32[]{:S(2)}, u32[]{:S(2)}) collective-permute-start(bf16[256,512]{1,0:T(8,128)(2,1)S(1)} %copy-done.5), channel_id=1, source_target_pairs={{0,6},{2,134},{4,262},{6,390},{128,0},{130,128},{132,256},{134,384... | collective-permute-start | bytes 786440 | tf_op jit(solution)/shard_map/ppermute | solution.py:406
  42.3 0.0 collective-permute-done
  42.3 0.0 collective-permute-done.1
  42.3 11.1 %collective-permute-done.2 = bf16[256,512]{1,0:T(8,128)(2,1)S(1)} collective-permute-done((bf16[256,512]{1,0:T(8,128)(2,1)S(1)}, bf16[256,512]{1,0:T(8,128)(2,1)S(1)}, u32[]{:S(2)}, u32[]{:S(2)}) %collective-permute-start.2) | collective-permute-done | bytes 262176 | tf_op jit(solution)/shard_map/ppermute | solution.py:406
  53.4 5.1 %collective-permute-done.3 = bf16[256,512]{1,0:T(8,128)(2,1)S(1)} collective-permute-done((bf16[256,512]{1,0:T(8,128)(2,1)S(1)}, bf16[256,512]{1,0:T(8,128)(2,1)S(1)}, u32[]{:S(2)}, u32[]{:S(2)}) %collective-permute-start.3) | collective-permute-done | bytes 262176 | tf_op jit(solution)/shard_map/ppermute | solution.py:406
  58.6 0.1 pad_maximum_fusion.own_ref
  58.7 1.9 %collective-permute-start.4 = (bf16[4,256,512]{2,1,0:T(8,128)(2,1)S(1)}, bf16[4,256,512]{2,1,0:T(8,128)(2,1)S(1)}, u32[]{:S(2)}, u32[]{:S(2)}) collective-permute-start(bf16[4,256,512]{2,1,0:T(8,128)(2,1)S(1)} %pad_maximum_fusion.own_ref), channel_id=1, source_target_pairs={{0,1},{1,0},{2,3},{3,2},{4,5},{5,4},{6,7},{7,6},{8,9},{9,8},{10,11... | collective-permute-start | bytes 3145736 | tf_op jit(solution)/shard_map/ppermute | solution.py:408
  60.7 0.1 pad_add_fusion.place_ref
  60.7 2.5 %collective-permute-done.4.other_ref = bf16[4,256,512]{2,1,0:T(8,128)(2,1)S(1)} collective-permute-done((bf16[4,256,512]{2,1,0:T(8,128)(2,1)S(1)}, bf16[4,256,512]{2,1,0:T(8,128)(2,1)S(1)}, u32[]{:S(2)}, u32[]{:S(2)}) %collective-permute-start.4) | collective-permute-done | bytes 1048608 | tf_op jit(solution)/shard_map/ppermute | solution.py:408
  63.3 0.0 all-to-all-done.proj_ref
  63.3 2.3 %partial_products.1 = bf16[4,288,512]{2,1,0:T(8,128)(2,1)S(1)} custom-call(s32[4]{0:T(128)S(1)} %pad_add_fusion.place_ref, bf16[4,256,512]{2,1,0:T(8,128)(2,1)S(1)} %pad_maximum_fusion.own_ref, bf16[4,256,512]{2,1,0:T(8,128)(2,1)S(1)} %collective-permute-done.4.other_ref, bf16[8,2,72,512]{3,2,1,0:T(8,128)(2,1)S(1)} %all-to-all-done.proj_ref), custom_call_target="tpu_custom_call" | custom-call | tf_op jit(solution)/shard_map/partial_products/pallas_call | solution.py:413
  65.6 0.0 copy-start
  65.6 0.0 copy-start.1
  65.6 0.0 copy-start.2
  65.7 22.9 %all_to_all.20.parts_ref = bf16[4,288,512]{2,1,0:T(8,128)(2,1)S(1)} all-to-all(bf16[4,288,512]{2,1,0:T(8,128)(2,1)S(1)} %partial_products.1), channel_id=1, replica_groups=mesh['x'=4,'zh'=2,'y'=8,'zl'=4,'core'=2] {'x'}, dimensions={0} | all-to-all | bytes 2359296 | tf_op jit(solution)/shard_map/all_to_all | solution.py:431
  88.6 0.0 copy-done
  88.6 0.0 copy-done.1
  88.6 0.0 copy-done.2
  88.6 5.7 %local_scans.1 = (bf16[256,512]{1,0:T(8,128)(2,1)S(1)}, f32[3,128,128]{2,1,0:T(8,128)S(1)}, f32[8,128]{1,0:T(8,128)S(1)}, f32[1024,128]{1,0:T(8,128)S(1)}, f32[1...) custom-call(s32[4]{0:T(128)S(1)} %pad_add_fusion.place_ref, ...), custom_call_target="tpu_custom_call" | custom-call | tf_op jit(solution)/shard_map/local_scans/pallas_call | solution.py:437
  94.3 0.0 copy-start.3
  94.3 0.0 copy-start.4
  94.3 23.1 %all_to_all.21.recv_ref = bf16[8,256,128]{2,1,0:T(8,128)(2,1)S(1)} all-to-all(bf16[8,256,128]{2,1,0:T(8,128)(2,1)S(1)} %get-tuple-element.23), channel_id=1, replica_groups=mesh['x'=4,'zh'=2,'y'=8,'zl'=4,'core'=2] {'y'}, dimensions={0} | all-to-all | bytes 1048576 | tf_op jit(solution)/shard_map/all_to_all | solution.py:455
  117.4 1.9 %chain_ring.1 = (bf16[8,144,128]{2,1,0:T(8,128)(2,1)}, f32[2,64,128]{2,1,0:T(8,128)S(1)}) custom-call(s32[4]{0:T(128)S(1)} %pad_add_fusion.place_ref, bf16[8,256,128]{2,1,0:T(8,128)(2,1)S(1)} %all_to_all.21.recv_ref, f32[64,128]{1,0:T(8,128)S(1)} %get-tuple-element.24.rate_ref, f32[64,128]{1,0:T(8,128)S(1)} %get-tuple-element.25.own_table_ref), custom_call_target="tpu_custom_call" | custom-call | tf_op jit(solution)/shard_map/chain_ring/pallas_call | solution.py:456
  119.3 7.5 %all-to-all-start.3 = ((bf16[8,144,128]{2,1,0:T(8,128)(2,1)}), bf16[8,144,128]{2,1,0:T(8,128)(2,1)S(1)}, u32[]{:S(2)}, u32[]{:S(2)}) async-start(bf16[8,144,128]{2,1,0:T(8,128)(2,1)} %get-tuple-element.26), calls=%async_computation.3 | async-start | bytes 589824 | tf_op jit(solution)/shard_map/all_to_all | solution.py:464
  126.8 0.0 copy-done.3
  126.8 0.0 copy-done.4
  126.9 11.3 %all-to-all-done.3.recv_ref = bf16[8,144,128]{2,1,0:T(8,128)(2,1)S(1)} async-done(((bf16[8,144,128]{2,1,0:T(8,128)(2,1)}), bf16[8,144,128]{2,1,0:T(8,128)(2,1)S(1)}, u32[]{:S(2)}, u32[]{:S(2)}) %all-to-all-start.3) | async-done | bytes 294944 | tf_op jit(solution)/shard_map/all_to_all | solution.py:464
  138.2 4.4 %final_scan.1 = (bf16[256,512]{1,0:T(8,128)(2,1)}, bf16[256,512]{1,0:T(8,128)(2,1)}, bf16[256,512]{1,0:T(8,128)(2,1)}, f32[1,8,16]{2,1,0:T(8,128)}, f32[1,8,16]{2,1,0:T(8,128)}, /*index=5*/f32[8,1]{1,0:T(8,128)S(1)}) custom-call(s32[4]{0:T(128)S(1)} %pad_add_fusion.place_ref, f32[3,8,128]{2,1,0:T(8,128)S(1)} %select_maximum_fusion.own_ref, ...), custom_call_target="tpu_custom_call" | custom-call | tf_op jit(solution)/shard_map/final_scan/pallas_call | solution.py:466
  142.6 0.6 reduce
  (5 shorter events, 0.1 us)
Async XLA Ops:
  3.8 12.3 %collective-permute-start.5 = (bf16[72,512]{1,0:T(8,128)(2,1)S(1)}, bf16[72,512]{1,0:T(8,128)(2,1)S(1)}, u32[]{:S(2)}, u32[]{:S(2)}) collective-permute-start(bf16[72,512]{1,0:T(8,128)(2,1)S(1)} %maximum_maximum_fusion), channel_id=1, source_target_pairs={{0,64},{64,0},{1,65},{65,1},{2,66},{66,2},{3,67},{67,3},{4,68},{68... | collective-permute-start | bytes 221192 | tf_op jit(solution)/shard_map/ppermute | solution.py:398
  18.2 7.2 %copy-start.5 = (bf16[256,512]{1,0:T(8,128)(2,1)S(1)}, bf16[256,512]{1,0:T(8,128)(2,1)}, u32[]{:S(2)}) copy-start(bf16[256,512]{1,0:T(8,128)(2,1)} %param.11) | copy-start | bytes 786436
  18.2 45.1 %all-to-all-start = ((bf16[8,2,72,512]{3,2,1,0:T(8,128)(2,1)}), bf16[8,2,72,512]{3,2,1,0:T(8,128)(2,1)S(1)}, u32[]{:S(2)}, u32[]{:S(2)}) async-start(bf16[8,2,72,512]{3,2,1,0:T(8,128)(2,1)} %broadcast_in_dim.10), calls=%async_computation | async-start | bytes 2359296 | tf_op jit(solution)/shard_map/all_to_all | solution.py:401
  25.5 16.8 %collective-permute-start = (bf16[256,512]{1,0:T(8,128)(2,1)S(1)}, bf16[256,512]{1,0:T(8,128)(2,1)S(1)}, u32[]{:S(2)}, u32[]{:S(2)}) collective-permute-start(bf16[256,512]{1,0:T(8,128)(2,1)S(1)} %copy-done.5), channel_id=1, source_target_pairs={{0,0},{2,128},{4,256},{6,384},{128,2},{130,130},{132,258},{134,386... | collective-permute-start | bytes 786440 | tf_op jit(solution)/shard_map/ppermute | solution.py:406
  29.9 12.4 %collective-permute-start.1 = (bf16[256,512]{1,0:T(8,128)(2,1)S(1)}, bf16[256,512]{1,0:T(8,128)(2,1)S(1)}, u32[]{:S(2)}, u32[]{:S(2)}) collective-permute-start(bf16[256,512]{1,0:T(8,128)(2,1)S(1)} %copy-done.5), channel_id=1, source_target_pairs={{0,2},{2,130},{4,258},{6,386},{128,4},{130,132},{132,260},{134,388... | collective-permute-start | bytes 786440 | tf_op jit(solution)/shard_map/ppermute | solution.py:406
  31.8 21.6 %collective-permute-start.2 = (bf16[256,512]{1,0:T(8,128)(2,1)S(1)}, bf16[256,512]{1,0:T(8,128)(2,1)S(1)}, u32[]{:S(2)}, u32[]{:S(2)}) collective-permute-start(bf16[256,512]{1,0:T(8,128)(2,1)S(1)} %copy-done.5), channel_id=1, source_target_pairs={{0,4},{2,132},{4,260},{6,388},{128,6},{130,134},{132,262},{134,390... | collective-permute-start | bytes 786440 | tf_op jit(solution)/shard_map/ppermute | solution.py:406
  35.5 23.1 %collective-permute-start.3 = (bf16[256,512]{1,0:T(8,128)(2,1)S(1)}, bf16[256,512]{1,0:T(8,128)(2,1)S(1)}, u32[]{:S(2)}, u32[]{:S(2)}) collective-permute-start(bf16[256,512]{1,0:T(8,128)(2,1)S(1)} %copy-done.5), channel_id=1, source_target_pairs={{0,6},{2,134},{4,262},{6,390},{128,0},{130,128},{132,256},{134,384... | collective-permute-start | bytes 786440 | tf_op jit(solution)/shard_map/ppermute | solution.py:406
  58.7 4.6 %collective-permute-start.4 = (bf16[4,256,512]{2,1,0:T(8,128)(2,1)S(1)}, bf16[4,256,512]{2,1,0:T(8,128)(2,1)S(1)}, u32[]{:S(2)}, u32[]{:S(2)}) collective-permute-start(bf16[4,256,512]{2,1,0:T(8,128)(2,1)S(1)} %pad_maximum_fusion.own_ref), channel_id=1, source_target_pairs={{0,1},{1,0},{2,3},{3,2},{4,5},{5,4},{6,7},{7,6},{8,9},{9,8},{10,11... | collective-permute-start | bytes 3145736 | tf_op jit(solution)/shard_map/ppermute | solution.py:408
  65.6 22.9 %copy-start = (bf16[256,512]{1,0:T(8,128)(2,1)S(1)}, bf16[256,512]{1,0:T(8,128)(2,1)}, u32[]{:S(2)}) copy-start(bf16[256,512]{1,0:T(8,128)(2,1)} %values_ref.3) | copy-start | bytes 786436
  65.6 22.9 %copy-start.1 = (bf16[256,512]{1,0:T(8,128)(2,1)S(1)}, bf16[256,512]{1,0:T(8,128)(2,1)}, u32[]{:S(2)}) copy-start(bf16[256,512]{1,0:T(8,128)(2,1)} %gate_in_ref.3) | copy-start | bytes 786436
  65.6 22.9 %copy-start.2 = (bf16[256,512]{1,0:T(8,128)(2,1)S(1)}, bf16[256,512]{1,0:T(8,128)(2,1)}, u32[]{:S(2)}) copy-start(bf16[256,512]{1,0:T(8,128)(2,1)} %gate_out_ref.1) | copy-start | bytes 786436
  94.3 32.5 %copy-start.3 = (f32[1,8,16]{2,1,0:T(8,128)S(1)}, f32[1,8,16]{2,1,0:T(8,128)}, u32[]{:S(2)}) copy-start(f32[1,8,16]{2,1,0:T(8,128)} %param.14) | copy-start | bytes 1540
  94.3 32.6 %copy-start.4 = (f32[1,8,16]{2,1,0:T(8,128)S(1)}, f32[1,8,16]{2,1,0:T(8,128)}, u32[]{:S(2)}) copy-start(f32[1,8,16]{2,1,0:T(8,128)} %param.13) | copy-start | bytes 1540
  119.3 18.9 %all-to-all-start.3 = ((bf16[8,144,128]{2,1,0:T(8,128)(2,1)}), bf16[8,144,128]{2,1,0:T(8,128)(2,1)S(1)}, u32[]{:S(2)}, u32[]{:S(2)}) async-start(bf16[8,144,128]{2,1,0:T(8,128)(2,1)} %get-tuple-element.26), calls=%async_computation.3 | async-start | bytes 589824 | tf_op jit(solution)/shard_map/all_to_all | solution.py:464

commit v3 on v2

--- a/solution.py
+++ b/solution.py
@@ -17,11 +17,57 @@
 VMEM = 48 * 1024 * 1024
 
 
-def split_exact(x):
-    high = lax.reduce_precision(x, 8, 7)
+def pack_kernel(*refs):
+    sources, (block_ref, own_ref), fetched, tile, sems = refs[:4], refs[4:6], refs[6:10], *refs[10:]
+    copies = [
+        pltpu.make_async_copy(src, dst, sems.at[i])
+        for i, (src, dst) in enumerate(zip(sources, fetched))
+    ]
+    for copy in copies:
+        copy.start()
+    for copy in copies:
+        copy.wait()
+    proj_ref, amp_ref, rate_ref, skip_ref = fetched
+    pencil = amp_ref.shape[0]
+    rate = rate_ref[...]
+    y = 2.0 * rate
+    series = jnp.ones_like(y)
+    for n in range(10, 1, -1):
+        series = 1.0 - y * (1.0 / n) * series
+    gain = jnp.sqrt(jnp.where(y < 0.5, y * series, 1.0 - jnp.exp(-y)))
+    own_ref[...] = jnp.zeros_like(own_ref)
+    own_ref[0, :, 0:MODES] = amp_ref[...]
+    own_ref[1, :, 0:MODES] = rate
+    own_ref[2, :, 0:MODES] = gain
+    row = lax.broadcasted_iota(jnp.int32, (pencil, pencil), 0)
+    col = lax.broadcasted_iota(jnp.int32, (pencil, pencil), 1)
+    skip = jnp.sum(jnp.where(row == col, skip_ref[...], 0.0), axis=1, keepdims=True)
+    tile[...] = jnp.zeros_like(tile)
+    tile[:, 0:MODES] = amp_ref[...] * gain
+    tile[:, MODES : 2 * MODES] = rate
+    tile[:, 2 * MODES : 2 * MODES + 1] = skip
+    x = tile[...]
+    high = x.astype(jnp.bfloat16).astype(jnp.float32)
     rest = x - high
-    middle = lax.reduce_precision(rest, 8, 7)
-    return [part.astype(jnp.bfloat16) for part in (high, middle, rest - middle)]
+    middle = rest.astype(jnp.bfloat16).astype(jnp.float32)
+    x = high + pltpu.roll(middle, PARAMS, 1) + pltpu.roll(rest - middle, 2 * PARAMS, 1)
+    blank = jnp.zeros((pencil, block_ref.shape[1] - LANES), jnp.float32)
+    block = jnp.concatenate(
+        [proj_ref[...].astype(jnp.float32), jnp.concatenate([x, blank], axis=1)], axis=0
+    ).astype(jnp.bfloat16)
+    block_ref[...] = block
+
+
+def spread_kernel(place_ref, block_ref, far_ref, tile_ref, repeated_ref):
+    del tile_ref
+    zh = lax.rem(place_ref[2], 2)
+    here = block_ref[...]
+    there = far_ref[...]
+    low = jnp.where(zh == 0, here, there)
+    high = jnp.where(zh == 0, there, here)
+    for k in range(repeated_ref.shape[0]):
+        repeated_ref[k, 0] = low
+        repeated_ref[k, 1] = high
 
 
 def to_steps(dst, x, half):
@@ -40,22 +86,48 @@
     return slice(8 * m, 8 * m + 8)
 
 
-def product_kernel(place_ref, own_ref, other_ref, proj_ref, out_ref):
+def product_kernel(place_ref, mine0_ref, mine1_ref, theirs0_ref, theirs1_ref, proj_ref, out_ref):
     core = place_ref[0]
     ring, pair, height, cols = proj_ref.shape
     depth = height - 8
-    rows = own_ref.shape[1]
+    rows = mine0_ref.shape[1]
     count = ring * pair
 
     def rows_of(c):
         return proj_ref[:, pl.ds(c, 1), 0:depth, :].reshape(ring * depth, cols)
 
-    total = jnp.dot(own_ref[0], rows_of(core), preferred_element_type=jnp.float32)
-    total += jnp.dot(other_ref[0], rows_of(1 - core), preferred_element_type=jnp.float32)
-    out_ref[0, 0:rows, :] = total.astype(jnp.bfloat16)
-    pieces = [proj_ref[j % ring, j // ring, :, 0:LANES].astype(jnp.float32)[depth:] for j in range(count)]
+    for k, tile_ref in enumerate((mine0_ref, mine1_ref, theirs0_ref, theirs1_ref)):
+        first = core if k < 2 else 1 - core
+
+        @pl.when(pl.program_id(0) == k)
+        def _():
+            total = jnp.dot(tile_ref[0], rows_of(first), preferred_element_type=jnp.float32)
+            total += jnp.dot(tile_ref[1], rows_of(1 - first), preferred_element_type=jnp.float32)
+            out_ref[0, 0:rows, :] = total.astype(jnp.bfloat16)
+
+    pieces = [
+        proj_ref[j % ring, j // ring, :, 0:LANES].astype(jnp.float32)[depth:] for j in range(count)
+    ]
     params = [jnp.concatenate(pieces[j : j + 4], axis=1) for j in range(0, count, 4)]
     out_ref[0, rows:, :] = jnp.concatenate(params, axis=0).astype(jnp.bfloat16)
+
+
+def two_terms(x, pad):
+    high = x.astype(jnp.bfloat16).astype(jnp.float32)
+    return jnp.concatenate([high, x - high] + [jnp.zeros_like(x)] * pad, axis=0).astype(jnp.bfloat16)
+
+
+def pack_sums(x):
+    lane = lax.broadcasted_iota(jnp.int32, x.shape, 1)
+    high = x.astype(jnp.bfloat16).astype(jnp.float32)
+    rest = pltpu.roll(x - high, 2 * MODES, 1)
+    return jnp.where(lane < 6 * MODES, high, rest).astype(jnp.bfloat16)
+
+
+def unpack_sums(x):
+    lane = lax.broadcasted_iota(jnp.int32, x.shape, 1)
+    rest = pltpu.roll(x, LANES - 2 * MODES, 1)
+    return x + jnp.where((lane >= 4 * MODES) & (lane < 6 * MODES), rest, 0.0)
 
 
 def local_kernel(
@@ -182,15 +254,14 @@
     every = jnp.concatenate(
         [packed[0 : 4 * MODES, :], packed[8 * MODES : 12 * MODES, :]], axis=0
     ).astype(jnp.bfloat16)
+    skips = two_terms(packed[24 * MODES : 24 * MODES + 4, :], 2)
     for y in range(peers):
         send_ref[y, 0 : 8 * MODES, :] = every
         mine = jnp.concatenate(
             [state[8 * (peers * g + y) : 8 * (peers * g + y) + 8, :] for g in range(groups)], axis=0
         )
-        high = mine.astype(jnp.bfloat16)
-        low = (mine - high.astype(jnp.float32)).astype(jnp.bfloat16)
-        send_ref[y, 8 * MODES : 8 * MODES + 8 * groups, :] = high
-        send_ref[y, 8 * MODES + 8 * groups :, :] = low
+        send_ref[y, 8 * MODES : 8 * MODES + 8 * groups, :] = pack_sums(mine)
+        send_ref[y, 8 * MODES + 8 * groups :, :] = skips
     for g in range(groups):
         at = pl.multiple_of(8 * (peers * g + place_ref[1]), 8)
         own_table_ref[8 * g : 8 * g + 8, :] = table[pl.ds(at, 8), :]
@@ -200,19 +271,18 @@
     d = jnp.exp(-rate)
     power = jnp.exp(-span * rate)
     parts = [
-        [c] + [pltpu.roll(c, LANES - MODES * a, 1) for a in range(1, 7)] for c in chunks
+        [c] + [pltpu.roll(c, LANES - MODES * a, 1) for a in range(1, 6)] for c in chunks
     ]
-    s_in, u_in, w_in, x_in, z_sum, f_sum, skip_sum = (jnp.zeros_like(chunks[0]),) * 7
-    for s, u, w, x, z, f, skip in parts:
+    s_in, u_in, w_in, x_in, z_sum, f_sum = (jnp.zeros_like(chunks[0]),) * 6
+    for s, u, w, x, z, f in parts:
         z_sum = z_sum + z + s_in * (d * w)
         f_sum = f_sum + f + d * (u_in * w + s_in * (x + w))
         u_in = power * (u_in + span * s_in) + u
         s_in = power * s_in + s
-        skip_sum = skip_sum + skip
-    for _, _, w, x, _, _, _ in parts[::-1]:
+    for _, _, w, x, _, _ in parts[::-1]:
         x_in = x + power * (x_in + span * w_in)
         w_in = w + power * w_in
-    return s_in, u_in, w_in, x_in, z_sum, f_sum, skip_sum
+    return s_in, u_in, w_in, x_in, z_sum, f_sum
 
 
 def neighbours(s, w, power, index):
@@ -238,26 +308,24 @@
     near_ref[0] = before
     near_ref[1] = after
     every = jnp.concatenate([total, rest], axis=0).astype(jnp.bfloat16)
-    high = slice(2 * many, 2 * many + 8 * groups)
-    low = slice(2 * many + 8 * groups, 2 * many + 16 * groups)
-    sums = [
-        recv_ref[c, high, :].astype(jnp.float32) + recv_ref[c, low, :].astype(jnp.float32)
-        for c in range(peers)
-    ]
+    share = slice(2 * many, 2 * many + 8 * groups)
+    sums = [unpack_sums(recv_ref[c, share, :].astype(jnp.float32)) for c in range(peers)]
+    tails = [recv_ref[c, 2 * many + 8 * groups :, :].astype(jnp.float32) for c in range(peers)]
+    skip = sum(tails[1:], tails[0])
+    skip = skip[0:4] + skip[4:8]
     rate = pltpu.roll(own_table_ref[...], LANES - MODES, 1)
     lane = lax.broadcasted_iota(jnp.int32, rate.shape, 1)
     rate = jnp.where(lane < MODES, rate, 0.0)
     packed = jnp.zeros_like(rate)
     for a, part in enumerate(chained(sums, rate, span)):
         packed += pltpu.roll(jnp.where(lane < MODES, part, 0.0), MODES * a, 1)
-    first = packed.astype(jnp.bfloat16).astype(jnp.float32)
-    second = packed - first
+    packed = pack_sums(packed).astype(jnp.float32)
+    skips = two_terms(skip, 0).astype(jnp.float32)
     for g in range(groups):
         send_ref[g, 0 : 2 * many, :] = every
-        at = slice(8 * g, 8 * g + 8)
-        send_ref[g, 2 * many :, :] = jnp.concatenate([first[at], second[at]], axis=0).astype(
-            jnp.bfloat16
-        )
+        send_ref[g, 2 * many :, :] = jnp.concatenate(
+            [packed[8 * g : 8 * g + 8], skips], axis=0
+        ).astype(jnp.bfloat16)
 
 
 def final_kernel(
@@ -347,7 +415,7 @@
 
     sums = [recv_ref[g, 2 * many :, :].astype(jnp.float32) for g in range(groups)]
     own_weight, own_rate, gain = (own_ref[a] for a in range(3))
-    done = chained([x[0:8] + x[8:16] for x in sums], own_rate, span * ring)
+    done = chained([unpack_sums(x[0:8]) for x in sums], own_rate, span * ring)
     zeroth, first_moment = done[4], done[5]
     amp_grad = gain * zeroth
     rate_grad = own_rate * own_weight * (
@@ -355,7 +423,19 @@
     )
     amp_ref[0] = amp_grad[:, :MODES]
     rate_grad_ref[0] = rate_grad[:, :MODES]
-    skip_grad_ref[...] = done[6][:, 0:1]
+    pencil = skip_grad_ref.shape[1]
+    tails = sum([x[8:16] for x in sums[1:]], sums[0][8:16])
+    skip = tails[0:4] + tails[4:8]
+    chunk = place_ref[2] * int(ring) + place_ref[1]
+    row = lax.broadcasted_iota(jnp.int32, skip.shape, 0)
+    lane = lax.broadcasted_iota(jnp.int32, skip.shape, 1)
+    here = (row == chunk // (LANES // pencil)) & (lane // pencil == lax.rem(chunk, LANES // pencil))
+    skip = jnp.sum(jnp.where(here, skip, 0.0), axis=0, keepdims=True)
+    shift = LANES // 2
+    while shift >= pencil:
+        skip += pltpu.roll(skip, shift, 1)
+        shift //= 2
+    skip_grad_ref[...] = skip[:, 0:pencil]
 
 
 def whole(*shape):
@@ -387,51 +467,75 @@
     shape = jax.ShapeDtypeStruct
     exchange = functools.partial(lax.all_to_all, split_axis=0, concat_axis=0, tiled=True)
 
-    amp = amplitude.reshape(pencil, MODES)
-    rate = decay_rate.reshape(pencil, MODES)
-    gain = jnp.sqrt(-jnp.expm1(-2.0 * rate))
-    mine = jnp.concatenate([amp * gain, rate, skip_gain.reshape(pencil, 1)], axis=1)
-    tile = jnp.concatenate(
-        split_exact(mine) + [jnp.zeros((pencil, cols - 3 * PARAMS), bf16)], axis=1
-    )
-    block = jnp.concatenate([out_proj.T, tile], axis=0)
-    there = lax.ppermute(block, "zh", [(0, 1), (1, 0)])
-    zh = lax.axis_index("zh")
-    block = jnp.stack([jnp.where(zh == 0, block, there), jnp.where(zh == 0, there, block)])
-    proj = exchange(repeated(block, ny), "y")
-
-    tiles = []
-    for k in range(nx):
-        moves = [(a * nx + b, b * nx + (a + k) % nx) for a in range(nx) for b in range(nx)]
-        tiles.append(lax.ppermute(out_grad, ("x", "zl"), moves))
-    own = jnp.stack(tiles)
-    other = lax.ppermute(own, "core", [(0, 1), (1, 0)])
+    smem = pl.BlockSpec(memory_space=pltpu.SMEM)
+    vmem = pl.BlockSpec(memory_space=pltpu.VMEM)
+    height = out_proj.shape[1] + pencil
+    operands = (
+        out_proj.T,
+        amplitude.reshape(pencil, MODES),
+        decay_rate.reshape(pencil, MODES),
+        skip_gain,
+    )
+    block, own_modes = pl.pallas_call(
+        pack_kernel,
+        out_shape=[shape((height, cols), bf16), shape((3, pencil, LANES), f32)],
+        in_specs=[pl.BlockSpec(memory_space=pltpu.HBM)] * 4,
+        scratch_shapes=[pltpu.VMEM(x.shape, x.dtype) for x in operands]
+        + [pltpu.VMEM((pencil, LANES), f32), pltpu.SemaphoreType.DMA((4,))],
+        name="pack",
+    )(*operands)
     place = jnp.stack(
-        [lax.axis_index("core"), lax.axis_index("y"), lax.axis_index(("x", "zh")), lax.axis_index("zl")]
+        [lax.axis_index(a) for a in ("core", "y", ("x", "zh"), "zl", "x")]
     ).astype(jnp.int32)
+    swap = [(0, 1), (1, 0)]
+    far = lax.ppermute(block, "zh", swap)
+    other = lax.ppermute(out_grad, "core", swap)
+    tile = jnp.stack([out_grad, other])
+    proj = pl.pallas_call(
+        spread_kernel,
+        grid=(1,),
+        out_shape=shape((ny, nzh, height, cols), bf16),
+        in_specs=[
+            smem,
+            whole(height, cols),
+            whole(height, cols),
+            pl.BlockSpec(memory_space=pl.ANY),
+        ],
+        out_specs=whole(ny, nzh, height, cols),
+        name="spread",
+    )(place, block, far, tile)
+    proj = exchange(proj, "y")
+
+    mine, theirs = [], []
+    for j in range(2):
+        moves = [
+            ((a * nx + b) * 2 + c, (b * nx + (a + 2 * c + j) % nx) * 2 + c)
+            for a in range(nx)
+            for b in range(nx)
+            for c in range(2)
+        ]
+        mine.append(lax.ppermute(tile, ("x", "zl", "core"), moves))
+        theirs.append(lax.ppermute(mine[j], "core", swap))
+
+    def tile_of(k, place):
+        core = jnp.where(k < 2, place[0], 1 - place[0])
+        return (lax.rem(place[3] + 2 * nx - 2 * core - lax.rem(k, 2), nx), 0, 0)
+
     height = rows + nzh * ny * pencil // 4
     parts = pl.pallas_call(
         product_kernel,
         grid_spec=pltpu.PrefetchScalarGridSpec(
             num_scalar_prefetch=1,
             grid=(nx,),
-            in_specs=[
-                pl.BlockSpec((1, rows, cols), lambda k, place: (k, 0, 0)),
-                pl.BlockSpec((1, rows, cols), lambda k, place: (k, 0, 0)),
-                whole(*proj.shape),
-            ],
-            out_specs=pl.BlockSpec(
-                (1, height, cols), lambda k, place: (lax.rem(place[3] + nx - k, nx), 0, 0)
-            ),
+            in_specs=[whole(2, rows, cols)] * 4 + [whole(*proj.shape)],
+            out_specs=pl.BlockSpec((1, height, cols), tile_of),
         ),
         out_shape=shape((nx, height, cols), bf16),
         compiler_params=pltpu.CompilerParams(vmem_limit_bytes=VMEM),
         name="partial_products",
-    )(place, own, other, proj)
+    )(place, *mine, *theirs, proj)
     parts = exchange(parts, "x")
 
-    smem = pl.BlockSpec(memory_space=pltpu.SMEM)
-    vmem = pl.BlockSpec(memory_space=pltpu.VMEM)
     many = 4 * MODES
     groups = nx * nzh
     gated, tables, skip, v_rows, g_rows, send, edge, rates, own_table = call(
@@ -442,7 +546,7 @@
             shape((8, LANES), f32),
             shape((half * 8, LANES), f32),
             shape((half * 8, LANES), f32),
-            shape((ny, 2 * many + 16 * groups, LANES), bf16),
+            shape((ny, 2 * many + 8 * groups + 16, LANES), bf16),
             shape((2, MODES, 4, LANES), f32),
             shape((many, LANES), f32),
             shape((8 * groups, LANES), f32),
@@ -462,12 +566,11 @@
     )(place, recv, rates, own_table)
 
     recv = exchange(send, ("x", "zh"))
-    own_modes = jnp.pad(jnp.stack([amp, rate, gain]), ((0, 0), (0, 0), (0, LANES - MODES)))
     gate_in_grad, gate_out_grad, values_grad, amplitude_grad, rate_grad, skip_grad = call(
         functools.partial(final_kernel, half, float(ny)),
         [shape((rows, cols), bf16)] * 3
         + [shape((1, pencil, MODES), f32)] * 2
-        + [shape((pencil, 1), f32)],
+        + [shape((1, pencil), f32)],
         [(MODES * 8, LANES), (MODES * 8, LANES), (half * 8, LANES), (half * 8, LANES)],
         "final_scan",
         in_specs=[smem] + [vmem] * 12,
@@ -493,7 +596,7 @@
         values_grad,
         amplitude_grad,
         rate_grad,
-        skip_grad.reshape(1, pencil),
+        skip_grad,
     )
 
 

time: 144 us -> 140 us (0.972)
  blocking collectives: 46 us -> 66.2 us
  waiting for transfers between devices: 32.4 us -> 18.2 us
  starting transfers between devices: 43.5 us -> 33.4 us
  Pallas kernels: 14.3 us -> 17.8 us
  other arithmetic: 4.21 us -> 1.8 us
    all_to_all x0 -> x1, blocking collectives: none -> 20.2 us  [per_device(): recv = exchange(send, ('x', 'zh'))]
    all_to_all x2 -> x1, waiting for transfers between devices: 11.3 us -> 0.01 us  [per_device(): proj = exchange(proj, 'y')]
    all_to_all x2 -> x1, starting transfers between devices: 14.8 us -> 7.23 us  [per_device(): proj = exchange(proj, 'y')]
    pallas_call x0 -> x2, Pallas kernels: none -> 3.74 us  [the longest x1 2.06 us: per_device(): pl.pallas_call(spread_kernel, grid=(1,), out_shape=shape((ny, nzh, height...]
    ppermute x6, waiting for transfers between devices: 21.1 us -> 18.2 us  [the longest x2 16 us: per_device(): mine.append(lax.ppermute(tile, ('x', 'zl', 'core'), moves))]
    ppermute x6, starting transfers between devices: 28.7 us -> 26.2 us  [the longest x1 10 us: per_device(): far = lax.ppermute(block, 'zh', swap)]
    all_to_all x1, blocking collectives: 22.9 us -> 24.6 us  [per_device(): parts = exchange(parts, 'x')]
    all_to_all x1, blocking collectives: 23.1 us -> 21.4 us  [per_device(): recv = exchange(send, 'y')]
  transfers between devices with their start and end apart: 8 -> 7, of which waited for: 5 -> 3; matrix products, arithmetic and copies ran while one was open for 0% -> 2% of each run, Pallas kernels for 0% -> 1%
where the time goes in v3:
time: 140 us
  blocking collectives  66.2 us (47%)
  starting transfers between devices  33.4 us (24%)
  waiting for transfers between devices  18.2 us (13%)
  Pallas kernels  17.8 us (13%)
  other arithmetic  1.8 us (1%)
    all_to_all x1, blocking collectives, per_device(): parts = exchange(parts, 'x')  24.6 us
    all_to_all x1, blocking collectives, per_device(): recv = exchange(send, 'y')  21.4 us
    all_to_all x1, blocking collectives, per_device(): recv = exchange(send, ('x', 'zh'))  20.2 us
    ppermute x2, waiting for transfers between devices, per_device(): mine.append(lax.ppermute(tile, ('x', 'zl', 'core'), moves))  16 us
    ppermute x1, starting transfers between devices, per_device(): far = lax.ppermute(block, 'zh', swap)  10 us
    ppermute x2, starting transfers between devices, per_device(): theirs.append(lax.ppermute(mine[j], 'core', swap))  8.81 us
    all_to_all x1, starting transfers between devices, per_device(): proj = exchange(proj, 'y')  7.23 us
    pallas_call x1, Pallas kernels, per_device(): call(functools.partial(local_kernel, half), [shape((rows, cols), bf16), s...  5.8 us
  transfers between devices with their start and end apart: 7, of which 3 were waited for; matrix products, arithmetic and copies ran while one was open for 2% of the time, Pallas kernels for 1%

profile of v3, /device:TPU:64, one launch (start us, length us, event | category | flops | bytes accessed | tf_op | source)
XLA Modules:
  0.0 139.5 jit_solution(10150421457761253227)
XLA Ops:
  0.6 1.9 %collective-permute-start = (bf16[256,512]{1,0:T(8,128)(2,1)}, bf16[256,512]{1,0:T(8,128)(2,1)S(1)}, u32[]{:S(2)}, u32[]{:S(2)}) collective-permute-start(bf16[256,512]{1,0:T(8,128)(2,1)} %param.11), channel_id=1, source_target_pairs={{0,1},{1,0},{2,3},{3,2},{4,5},{5,4},{6,7},{7,6},{8,9},{9,8},{10,11... | collective-permute-start | bytes 786440 | tf_op jit(solution)/shard_map/ppermute | solution.py:492
  2.6 1.7 %pack.1 = (bf16[72,512]{1,0:T(8,128)(2,1)}, f32[3,8,128]{2,1,0:T(8,128)}) custom-call(bf16[64,512]{1,0:T(8,128)(2,1)} %bitcast.12, f32[8,16]{1,0:T(8,128)} %bitcast.13, f32[8,16]{1,0:T(8,128)} %bitcast.14, f32[1,8]{1,0:T(1,128)} %refs_3_.1), custom_call_target="tpu_custom_call" | custom-call | tf_op jit(solution)/shard_map/pack/pallas_call | solution.py:479
  4.3 10.0 %collective-permute-start.5 = (bf16[72,512]{1,0:T(8,128)(2,1)}, bf16[72,512]{1,0:T(8,128)(2,1)S(1)}, u32[]{:S(2)}, u32[]{:S(2)}) collective-permute-start(bf16[72,512]{1,0:T(8,128)(2,1)} %get-tuple-element.20.block_ref), channel_id=1, source_target_pairs={{0,64},{64,0},{1,65},{65,1},{2,66},{66,2},{3,67},{67,3},{4,68},{68... | collective-permute-start | bytes 221192 | tf_op jit(solution)/shard_map/ppermute | solution.py:491
  14.3 0.6 stack.32.place_ref
  14.9 0.0 collective-permute-done
  14.9 1.8 %pad_maximum_fusion.tile_ref = bf16[2,256,512]{2,1,0:T(8,128)(2,1)} fusion(bf16[1,256,512]{2,1,0:T(8,128)(2,1)S(1)} %bitcast.11, bf16[1,256,512]{2,1,0:T(8,128)(2,1)} %bitcast.10), kind=kLoop, calls=%fused_computation | loop fusion | flops 262144 | bytes 1048576 | tf_op jit(solution)/shard_map/stack | solution.py:493
  16.7 0.7 collective-permute-done.5.far_ref
  17.4 0.0 copy-start.6
  17.4 0.6 copy-done.6
  18.0 2.1 %spread.1 = bf16[8,2,72,512]{3,2,1,0:T(8,128)(2,1)} custom-call(s32[5]{0:T(128)} %stack.32.place_ref, bf16[72,512]{1,0:T(8,128)(2,1)} %get-tuple-element.20.block_ref, bf16[72,512]{1,0:T(8,128)(2,1)} %copy-done.6, bf16[2,256,512]{2,1,0:T(8,128)(2,1)} %pad_maximum_fusion.tile_ref), custom_call_target="tpu_custom_call" | custom-call | tf_op jit(solution)/shard_map/spread/pallas_call | solution.py:494
  20.1 0.0 copy-start.5
  20.1 0.0 copy-start.3
  20.1 7.2 %all-to-all-start = ((bf16[8,2,72,512]{3,2,1,0:T(8,128)(2,1)}), bf16[8,2,72,512]{3,2,1,0:T(8,128)(2,1)S(1)}, u32[]{:S(2)}, u32[]{:S(2)}) async-start(bf16[8,2,72,512]{3,2,1,0:T(8,128)(2,1)} %spread.1), calls=%async_computation | async-start | bytes 2359296 | tf_op jit(solution)/shard_map/all_to_all | solution.py:507
  27.3 0.0 copy-done.5
  27.3 3.5 %collective-permute-start.1 = (bf16[2,256,512]{2,1,0:T(8,128)(2,1)S(1)}, bf16[2,256,512]{2,1,0:T(8,128)(2,1)S(1)}, u32[]{:S(2)}, u32[]{:S(2)}) collective-permute-start(bf16[2,256,512]{2,1,0:T(8,128)(2,1)S(1)} %copy-done.5), channel_id=1, source_target_pairs={{0,0},{1,5},{2,128},{3,133},{4,256},{5,261},{6,384},{7,389},{128,2... | collective-permute-start | bytes 1572872 | tf_op jit(solution)/shard_map/ppermute | solution.py:517
  30.8 1.9 %collective-permute-start.2 = (bf16[2,256,512]{2,1,0:T(8,128)(2,1)S(1)}, bf16[2,256,512]{2,1,0:T(8,128)(2,1)S(1)}, u32[]{:S(2)}, u32[]{:S(2)}) collective-permute-start(bf16[2,256,512]{2,1,0:T(8,128)(2,1)S(1)} %copy-done.5), channel_id=1, source_target_pairs={{0,2},{1,7},{2,130},{3,135},{4,258},{5,263},{6,386},{7,391},{128,4... | collective-permute-start | bytes 1572872 | tf_op jit(solution)/shard_map/ppermute | solution.py:517
  32.8 16.0 %collective-permute-done.1.mine0_ref = bf16[2,256,512]{2,1,0:T(8,128)(2,1)S(1)} collective-permute-done((bf16[2,256,512]{2,1,0:T(8,128)(2,1)S(1)}, bf16[2,256,512]{2,1,0:T(8,128)(2,1)S(1)}, u32[]{:S(2)}, u32[]{:S(2)}) %collective-permute-start.1) | collective-permute-done | bytes 524320 | tf_op jit(solution)/shard_map/ppermute | solution.py:517
  48.7 1.9 %collective-permute-start.3 = (bf16[2,256,512]{2,1,0:T(8,128)(2,1)S(1)}, bf16[2,256,512]{2,1,0:T(8,128)(2,1)S(1)}, u32[]{:S(2)}, u32[]{:S(2)}) collective-permute-start(bf16[2,256,512]{2,1,0:T(8,128)(2,1)S(1)} %collective-permute-done.1.mine0_ref), channel_id=1, source_target_pairs={{0,1},{1,0},{2,3},{3,2},{4,5},{5,4},{6,7},{7,6},{8,9},{9,8},{10,11... | collective-permute-start | bytes 1572872 | tf_op jit(solution)/shard_map/ppermute | solution.py:518
  50.7 0.0 collective-permute-done.2.mine1_ref
  50.7 6.9 %collective-permute-start.4 = (bf16[2,256,512]{2,1,0:T(8,128)(2,1)S(1)}, bf16[2,256,512]{2,1,0:T(8,128)(2,1)S(1)}, u32[]{:S(2)}, u32[]{:S(2)}) collective-permute-start(bf16[2,256,512]{2,1,0:T(8,128)(2,1)S(1)} %collective-permute-done.2.mine1_ref), channel_id=1, source_target_pairs={{0,1},{1,0},{2,3},{3,2},{4,5},{5,4},{6,7},{7,6},{8,9},{9,8},{10,11... | collective-permute-start | bytes 1572872 | tf_op jit(solution)/shard_map/ppermute | solution.py:518
  57.6 0.0 collective-permute-done.3.theirs0_ref
  57.6 1.5 %collective-permute-done.4.theirs1_ref = bf16[2,256,512]{2,1,0:T(8,128)(2,1)S(1)} collective-permute-done((bf16[2,256,512]{2,1,0:T(8,128)(2,1)S(1)}, bf16[2,256,512]{2,1,0:T(8,128)(2,1)S(1)}, u32[]{:S(2)}, u32[]{:S(2)}) %collective-permute-start.4) | collective-permute-done | bytes 524320 | tf_op jit(solution)/shard_map/ppermute | solution.py:518
  59.1 0.0 all-to-all-done.proj_ref
  59.1 0.0 copy-done.3
  59.1 2.4 %partial_products.1 = bf16[4,288,512]{2,1,0:T(8,128)(2,1)S(1)} custom-call(s32[5]{0:T(128)S(1)} %copy-done.3, bf16[2,256,512]{2,1,0:T(8,128)(2,1)S(1)} %collective-permute-done.1.mine0_ref, bf16[2,256,512]{2,1,0:T(8,128)(2,1)S(1)} %collective-permute-done.2.mine1_ref, bf16[2,256,512]{2,1,0:T(8,128)(2,1)S(1)} %collective-permute-done.3.theirs0_ref, ...), custom_call_target="tpu_custom_call" | custom-call | tf_op jit(solution)/shard_map/partial_products/pallas_call | solution.py:525
  61.5 0.0 copy-start
  61.6 0.0 copy-start.1
  61.6 0.0 copy-start.2
  61.6 24.6 %all_to_all.20.parts_ref = bf16[4,288,512]{2,1,0:T(8,128)(2,1)S(1)} all-to-all(bf16[4,288,512]{2,1,0:T(8,128)(2,1)S(1)} %partial_products.1), channel_id=1, replica_groups=mesh['x'=4,'zh'=2,'y'=8,'zl'=4,'core'=2] {'x'}, dimensions={0} | all-to-all | bytes 2359296 | tf_op jit(solution)/shard_map/all_to_all | solution.py:537
  86.2 0.0 copy-done
  86.2 0.0 copy-done.1
  86.2 0.0 copy-done.2
  86.2 5.8 %local_scans.1 = (bf16[256,512]{1,0:T(8,128)(2,1)S(1)}, f32[3,128,128]{2,1,0:T(8,128)S(1)}, f32[8,128]{1,0:T(8,128)S(1)}, f32[1024,128]{1,0:T(8,128)S(1)}, f32[1...) custom-call(s32[5]{0:T(128)S(1)} %copy-done.3, ...), custom_call_target="tpu_custom_call" | custom-call | tf_op jit(solution)/shard_map/local_scans/pallas_call | solution.py:541
  92.0 0.0 copy-start.4
  92.0 21.4 %all_to_all.21.recv_ref = bf16[8,208,128]{2,1,0:T(8,128)(2,1)S(1)} all-to-all(bf16[8,208,128]{2,1,0:T(8,128)(2,1)S(1)} %get-tuple-element.21), channel_id=1, replica_groups=mesh['x'=4,'zh'=2,'y'=8,'zl'=4,'core'=2] {'y'}, dimensions={0} | all-to-all | bytes 851968 | tf_op jit(solution)/shard_map/all_to_all | solution.py:559
  113.4 1.2 chain_ring.1
  114.7 20.2 %all_to_all.22.recv_ref = bf16[8,144,128]{2,1,0:T(8,128)(2,1)S(1)} all-to-all(bf16[8,144,128]{2,1,0:T(8,128)(2,1)S(1)} %get-tuple-element.24), channel_id=1, replica_groups=mesh['x'=4,'zh'=2,'y'=8,'zl'=4,'core'=2] {'x','zh'}, dimensions={0} | all-to-all | bytes 589824 | tf_op jit(solution)/shard_map/all_to_all | solution.py:568
  134.9 0.0 copy-done.4
  134.9 4.6 %final_scan.1 = (bf16[256,512]{1,0:T(8,128)(2,1)}, bf16[256,512]{1,0:T(8,128)(2,1)}, bf16[256,512]{1,0:T(8,128)(2,1)}, f32[1,8,16]{2,1,0:T(8,128)}, f32[1,8,16]{2,1,0:T(8,128)}, /*index=5*/f32[1,8]{1,0:T(1,128)}) custom-call(s32[5]{0:T(128)S(1)} %copy-done.3, f32[3,8,128]{2,1,0:T(8,128)S(1)} %copy-done.4, bf16[8,144,128]{2,1,0:T(8,128)(2,1)S(1)} %all_to_all.22.recv_ref, ...), custom_call_target="tpu_custom_call" | custom-call | tf_op jit(solution)/shard_map/final_scan/pallas_call | solution.py:569
Async XLA Ops:
  0.6 14.3 %collective-permute-start = (bf16[256,512]{1,0:T(8,128)(2,1)}, bf16[256,512]{1,0:T(8,128)(2,1)S(1)}, u32[]{:S(2)}, u32[]{:S(2)}) collective-permute-start(bf16[256,512]{1,0:T(8,128)(2,1)} %param.11), channel_id=1, source_target_pairs={{0,1},{1,0},{2,3},{3,2},{4,5},{5,4},{6,7},{7,6},{8,9},{9,8},{10,11... | collective-permute-start | bytes 786440 | tf_op jit(solution)/shard_map/ppermute | solution.py:492
  4.3 13.2 %collective-permute-start.5 = (bf16[72,512]{1,0:T(8,128)(2,1)}, bf16[72,512]{1,0:T(8,128)(2,1)S(1)}, u32[]{:S(2)}, u32[]{:S(2)}) collective-permute-start(bf16[72,512]{1,0:T(8,128)(2,1)} %get-tuple-element.20.block_ref), channel_id=1, source_target_pairs={{0,64},{64,0},{1,65},{65,1},{2,66},{66,2},{3,67},{67,3},{4,68},{68... | collective-permute-start | bytes 221192 | tf_op jit(solution)/shard_map/ppermute | solution.py:491
  17.4 0.6 copy-start.6
  20.1 7.2 %copy-start.5 = (bf16[2,256,512]{2,1,0:T(8,128)(2,1)S(1)}, bf16[2,256,512]{2,1,0:T(8,128)(2,1)}, u32[]{:S(2)}) copy-start(bf16[2,256,512]{2,1,0:T(8,128)(2,1)} %pad_maximum_fusion.tile_ref) | copy-start | bytes 1572868
  20.1 39.0 %copy-start.3 = (s32[5]{0:T(128)S(1)}, s32[5]{0:T(128)}, u32[]{:S(2)}) copy-start(s32[5]{0:T(128)} %stack.32.place_ref) | copy-start | bytes 64
  20.1 39.0 %all-to-all-start = ((bf16[8,2,72,512]{3,2,1,0:T(8,128)(2,1)}), bf16[8,2,72,512]{3,2,1,0:T(8,128)(2,1)S(1)}, u32[]{:S(2)}, u32[]{:S(2)}) async-start(bf16[8,2,72,512]{3,2,1,0:T(8,128)(2,1)} %spread.1), calls=%async_computation | async-start | bytes 2359296 | tf_op jit(solution)/shard_map/all_to_all | solution.py:507
  27.3 21.4 %collective-permute-start.1 = (bf16[2,256,512]{2,1,0:T(8,128)(2,1)S(1)}, bf16[2,256,512]{2,1,0:T(8,128)(2,1)S(1)}, u32[]{:S(2)}, u32[]{:S(2)}) collective-permute-start(bf16[2,256,512]{2,1,0:T(8,128)(2,1)S(1)} %copy-done.5), channel_id=1, source_target_pairs={{0,0},{1,5},{2,128},{3,133},{4,256},{5,261},{6,384},{7,389},{128,2... | collective-permute-start | bytes 1572872 | tf_op jit(solution)/shard_map/ppermute | solution.py:517
  30.8 19.8 %collective-permute-start.2 = (bf16[2,256,512]{2,1,0:T(8,128)(2,1)S(1)}, bf16[2,256,512]{2,1,0:T(8,128)(2,1)S(1)}, u32[]{:S(2)}, u32[]{:S(2)}) collective-permute-start(bf16[2,256,512]{2,1,0:T(8,128)(2,1)S(1)} %copy-done.5), channel_id=1, source_target_pairs={{0,2},{1,7},{2,130},{3,135},{4,258},{5,263},{6,386},{7,391},{128,4... | collective-permute-start | bytes 1572872 | tf_op jit(solution)/shard_map/ppermute | solution.py:517
  48.7 8.8 %collective-permute-start.3 = (bf16[2,256,512]{2,1,0:T(8,128)(2,1)S(1)}, bf16[2,256,512]{2,1,0:T(8,128)(2,1)S(1)}, u32[]{:S(2)}, u32[]{:S(2)}) collective-permute-start(bf16[2,256,512]{2,1,0:T(8,128)(2,1)S(1)} %collective-permute-done.1.mine0_ref), channel_id=1, source_target_pairs={{0,1},{1,0},{2,3},{3,2},{4,5},{5,4},{6,7},{7,6},{8,9},{9,8},{10,11... | collective-permute-start | bytes 1572872 | tf_op jit(solution)/shard_map/ppermute | solution.py:518
  50.7 8.4 %collective-permute-start.4 = (bf16[2,256,512]{2,1,0:T(8,128)(2,1)S(1)}, bf16[2,256,512]{2,1,0:T(8,128)(2,1)S(1)}, u32[]{:S(2)}, u32[]{:S(2)}) collective-permute-start(bf16[2,256,512]{2,1,0:T(8,128)(2,1)S(1)} %collective-permute-done.2.mine1_ref), channel_id=1, source_target_pairs={{0,1},{1,0},{2,3},{3,2},{4,5},{5,4},{6,7},{7,6},{8,9},{9,8},{10,11... | collective-permute-start | bytes 1572872 | tf_op jit(solution)/shard_map/ppermute | solution.py:518
  61.5 24.7 %copy-start = (bf16[256,512]{1,0:T(8,128)(2,1)S(1)}, bf16[256,512]{1,0:T(8,128)(2,1)}, u32[]{:S(2)}) copy-start(bf16[256,512]{1,0:T(8,128)(2,1)} %values_ref.3) | copy-start | bytes 786436
  61.6 24.7 %copy-start.1 = (bf16[256,512]{1,0:T(8,128)(2,1)S(1)}, bf16[256,512]{1,0:T(8,128)(2,1)}, u32[]{:S(2)}) copy-start(bf16[256,512]{1,0:T(8,128)(2,1)} %gate_in_ref.3) | copy-start | bytes 786436
  61.6 24.7 %copy-start.2 = (bf16[256,512]{1,0:T(8,128)(2,1)S(1)}, bf16[256,512]{1,0:T(8,128)(2,1)}, u32[]{:S(2)}) copy-start(bf16[256,512]{1,0:T(8,128)(2,1)} %gate_out_ref.1) | copy-start | bytes 786436
  92.0 42.9 %copy-start.4 = (f32[3,8,128]{2,1,0:T(8,128)S(1)}, f32[3,8,128]{2,1,0:T(8,128)}, u32[]{:S(2)}) copy-start(f32[3,8,128]{2,1,0:T(8,128)} %get-tuple-element.19.own_ref) | copy-start | bytes 36868

commit v4 on v3

--- a/solution.py
+++ b/solution.py
@@ -51,23 +51,43 @@
     rest = x - high
     middle = rest.astype(jnp.bfloat16).astype(jnp.float32)
     x = high + pltpu.roll(middle, PARAMS, 1) + pltpu.roll(rest - middle, 2 * PARAMS, 1)
-    blank = jnp.zeros((pencil, block_ref.shape[1] - LANES), jnp.float32)
-    block = jnp.concatenate(
-        [proj_ref[...].astype(jnp.float32), jnp.concatenate([x, blank], axis=1)], axis=0
+    wide = block_ref.shape[1] // LANES
+    lines = [
+        jnp.concatenate([x[r : r + 1] for r in range(k, k + wide)], axis=1)
+        for k in range(0, pencil, wide)
+    ]
+    blank = jnp.zeros((pencil - len(lines), block_ref.shape[1]), jnp.float32)
+    block_ref[...] = jnp.concatenate(
+        [proj_ref[...].astype(jnp.float32)] + lines + [blank], axis=0
     ).astype(jnp.bfloat16)
-    block_ref[...] = block
 
 
 def spread_kernel(place_ref, block_ref, far_ref, tile_ref, repeated_ref):
     del tile_ref
     zh = lax.rem(place_ref[2], 2)
-    here = block_ref[...]
-    there = far_ref[...]
+    here = block_ref[...].astype(jnp.float32)
+    there = far_ref[...].astype(jnp.float32)
     low = jnp.where(zh == 0, here, there)
     high = jnp.where(zh == 0, there, here)
+    depth = here.shape[0] - 8
+    block = jnp.concatenate(
+        [
+            low[:depth],
+            high[:depth],
+            low[depth : depth + 2],
+            high[depth : depth + 2],
+            jnp.zeros((4, here.shape[1]), jnp.float32),
+        ],
+        axis=0,
+    ).astype(jnp.bfloat16)
     for k in range(repeated_ref.shape[0]):
-        repeated_ref[k, 0] = low
-        repeated_ref[k, 1] = high
+        repeated_ref[k] = block
+
+
+def join_kernel(first_ref, second_ref, *refs):
+    out_ref = refs[-1]
+    out_ref[0] = first_ref[...]
+    out_ref[1] = second_ref[...]
 
 
 def to_steps(dst, x, half):
@@ -86,17 +106,18 @@
     return slice(8 * m, 8 * m + 8)
 
 
-def product_kernel(place_ref, mine0_ref, mine1_ref, theirs0_ref, theirs1_ref, proj_ref, out_ref):
+def product_kernel(place_ref, mine_ref, theirs_ref, proj_ref, out_ref):
     core = place_ref[0]
-    ring, pair, height, cols = proj_ref.shape
-    depth = height - 8
-    rows = mine0_ref.shape[1]
-    count = ring * pair
+    ring, height, cols = proj_ref.shape
+    depth = (height - 8) // 2
+    rows = mine_ref.shape[2]
 
     def rows_of(c):
-        return proj_ref[:, pl.ds(c, 1), 0:depth, :].reshape(ring * depth, cols)
-
-    for k, tile_ref in enumerate((mine0_ref, mine1_ref, theirs0_ref, theirs1_ref)):
+        at = pl.ds(pl.multiple_of(c * depth, depth), depth)
+        return proj_ref[:, at, :].reshape(ring * depth, cols)
+
+    for k in range(4):
+        tile_ref = (mine_ref, theirs_ref)[k // 2].at[k % 2]
         first = core if k < 2 else 1 - core
 
         @pl.when(pl.program_id(0) == k)
@@ -105,10 +126,11 @@
             total += jnp.dot(tile_ref[1], rows_of(1 - first), preferred_element_type=jnp.float32)
             out_ref[0, 0:rows, :] = total.astype(jnp.bfloat16)
 
-    pieces = [
-        proj_ref[j % ring, j // ring, :, 0:LANES].astype(jnp.float32)[depth:] for j in range(count)
+    params = [
+        proj_ref[y].astype(jnp.float32)[2 * depth + 2 * z : 2 * depth + 2 * z + 2]
+        for z in range(2)
+        for y in range(ring)
     ]
-    params = [jnp.concatenate(pieces[j : j + 4], axis=1) for j in range(0, count, 4)]
     out_ref[0, rows:, :] = jnp.concatenate(params, axis=0).astype(jnp.bfloat16)
 
 
@@ -155,14 +177,15 @@
     rows = 2 * half
     for k in range(sources):
         params = parts_ref[k, rows:, :].astype(jnp.float32)
-        for j in range(16):
-            piece = params[8 * (j // 4) : 8 * (j // 4) + 8, (j % 4) * LANES : (j % 4 + 1) * LANES]
-            piece = (
-                piece
-                + pltpu.roll(piece, LANES - PARAMS, 1)
-                + pltpu.roll(piece, LANES - 2 * PARAMS, 1)
-            )
-            table[128 * k + 8 * j : 128 * k + 8 * j + 8, :] = piece
+        for q in range(4):
+            at = pl.ds(128 * k + q, params.shape[0], stride=4)
+            table[at, :] = params[:, q * LANES : (q + 1) * LANES]
+    three = table[...]
+    table[...] = (
+        three
+        + pltpu.roll(three, LANES - PARAMS, 1)
+        + pltpu.roll(three, LANES - 2 * PARAMS, 1)
+    )
     for q in range(4):
         flipped = table[q * LANES : (q + 1) * LANES, :].T
         rate = flipped[MODES : 2 * MODES]
@@ -490,36 +513,50 @@
     swap = [(0, 1), (1, 0)]
     far = lax.ppermute(block, "zh", swap)
     other = lax.ppermute(out_grad, "core", swap)
-    tile = jnp.stack([out_grad, other])
+    tile = call(
+        join_kernel,
+        shape((2, rows, cols), bf16),
+        [],
+        "tile",
+        in_specs=[vmem, vmem, pl.BlockSpec(memory_space=pl.ANY)],
+    )(out_grad, other, block)
+    tall = nzh * out_proj.shape[1] + 8
     proj = pl.pallas_call(
         spread_kernel,
         grid=(1,),
-        out_shape=shape((ny, nzh, height, cols), bf16),
+        out_shape=shape((ny, tall, cols), bf16),
         in_specs=[
             smem,
             whole(height, cols),
             whole(height, cols),
             pl.BlockSpec(memory_space=pl.ANY),
         ],
-        out_specs=whole(ny, nzh, height, cols),
+        out_specs=whole(ny, tall, cols),
         name="spread",
     )(place, block, far, tile)
     proj = exchange(proj, "y")
 
-    mine, theirs = [], []
+    mine = []
     for j in range(2):
         moves = [
-            ((a * nx + b) * 2 + c, (b * nx + (a + 2 * c + j) % nx) * 2 + c)
+            ((a * nx + b) * 2 + c, (b * nx + (a + b + 2 * c + j) % nx) * 2 + c)
             for a in range(nx)
             for b in range(nx)
             for c in range(2)
         ]
         mine.append(lax.ppermute(tile, ("x", "zl", "core"), moves))
-        theirs.append(lax.ppermute(mine[j], "core", swap))
+    mine = call(
+        join_kernel,
+        shape((2, 2, rows, cols), bf16),
+        [],
+        "join",
+        cost_estimate=pl.CostEstimate(flops=4266100000, bytes_accessed=4 * rows * cols * 4, transcendentals=0),
+    )(*mine)
+    theirs = lax.ppermute(mine, "core", swap)
 
     def tile_of(k, place):
         core = jnp.where(k < 2, place[0], 1 - place[0])
-        return (lax.rem(place[3] + 2 * nx - 2 * core - lax.rem(k, 2), nx), 0, 0)
+        return (lax.rem(place[3] - place[4] + 2 * nx - 2 * core - lax.rem(k, 2), nx), 0, 0)
 
     height = rows + nzh * ny * pencil // 4
     parts = pl.pallas_call(
@@ -527,13 +564,13 @@
         grid_spec=pltpu.PrefetchScalarGridSpec(
             num_scalar_prefetch=1,
             grid=(nx,),
-            in_specs=[whole(2, rows, cols)] * 4 + [whole(*proj.shape)],
+            in_specs=[whole(2, 2, rows, cols)] * 2 + [whole(*proj.shape)],
             out_specs=pl.BlockSpec((1, height, cols), tile_of),
         ),
         out_shape=shape((nx, height, cols), bf16),
         compiler_params=pltpu.CompilerParams(vmem_limit_bytes=VMEM),
         name="partial_products",
-    )(place, *mine, *theirs, proj)
+    )(place, mine, theirs, proj)
     parts = exchange(parts, "x")
 
     many = 4 * MODES

time: 140 us -> 134 us (0.957)
  blocking collectives: 66.2 us -> 52.8 us
  waiting for transfers between devices: 18.2 us -> 27.4 us
  starting transfers between devices: 33.4 us -> 30.8 us
  local copies, waits for them, and re-layouts: 1.3 us -> 3.2 us
  other arithmetic: 1.8 us -> 0 us
    all_to_all x1, waiting for transfers between devices: 0.01 us -> 17.5 us  [per_device(): proj = exchange(proj, 'y')]
    ppermute x2, waiting for transfers between devices: 16 us -> 7.59 us  [per_device(): mine.append(lax.ppermute(tile, ('x', 'zl', 'core'), moves))]
    all_to_all x1, blocking collectives: 24.6 us -> 19.6 us  [per_device(): parts = exchange(parts, 'x')]
    ppermute x2 -> x1, starting transfers between devices: 8.81 us -> 4.12 us  [per_device(): theirs = lax.ppermute(mine, 'core', swap)]
    all_to_all x1, blocking collectives: 20.2 us -> 15.8 us  [per_device(): recv = exchange(send, ('x', 'zh'))]
    all_to_all x1, blocking collectives: 21.4 us -> 17.4 us  [per_device(): recv = exchange(send, 'y')]
    ppermute x2, starting transfers between devices: 5.41 us -> 7.69 us  [per_device(): mine.append(lax.ppermute(tile, ('x', 'zl', 'core'), moves))]
    unnamed x14 -> x18, local copies, waits for them, and re-layouts: 0.66 us -> 2.53 us
  transfers between devices with their start and end apart: 7 -> 6, of which waited for: 3 -> 3; matrix products, arithmetic and copies ran while one was open for 2% -> 1% of each run, Pallas kernels for 1% -> 3%
where the time goes in v4:
time: 134 us; the launch traced here: 133 us
  blocking collectives  52.8 us (39%)
  starting transfers between devices  30.8 us (23%)
  waiting for transfers between devices  27.4 us (20%)
  Pallas kernels  18 us (13%)
  local copies, waits for them, and re-layouts  3.2 us (2%)
    all_to_all x1, blocking collectives, per_device(): parts = exchange(parts, 'x')  19.6 us
    all_to_all x1, waiting for transfers between devices, per_device(): proj = exchange(proj, 'y')  17.5 us
    all_to_all x1, blocking collectives, per_device(): recv = exchange(send, 'y')  17.4 us
    all_to_all x1, blocking collectives, per_device(): recv = exchange(send, ('x', 'zh'))  15.8 us
    ppermute x1, starting transfers between devices, per_device(): far = lax.ppermute(block, 'zh', swap)  10 us
    ppermute x2, starting transfers between devices, per_device(): mine.append(lax.ppermute(tile, ('x', 'zl', 'core'), moves))  7.69 us
    ppermute x2, waiting for transfers between devices, per_device(): mine.append(lax.ppermute(tile, ('x', 'zl', 'core'), moves))  7.59 us
    all_to_all x1, starting transfers between devices, per_device(): proj = exchange(proj, 'y')  7.1 us
  transfers between devices with their start and end apart: 6, of which 3 were waited for; matrix products, arithmetic and copies ran while one was open for 1% of the time, Pallas kernels for 3%

profile of v4, /device:TPU:64, one launch (start us, length us, event | category | flops | bytes accessed | tf_op | source)
XLA Modules:
  0.0 133.1 jit_solution(1797659793126673629)
XLA Ops:
  0.6 1.9 %collective-permute-start = (bf16[256,512]{1,0:T(8,128)(2,1)}, bf16[256,512]{1,0:T(8,128)(2,1)S(1)}, u32[]{:S(2)}, u32[]{:S(2)}) collective-permute-start(bf16[256,512]{1,0:T(8,128)(2,1)} %first_ref.1), channel_id=1, source_target_pairs={{0,1},{1,0},{2,3},{3,2},{4,5},{5,4},{6,7},{7,6},{8,9},{9,8},{10,11... | collective-permute-start | bytes 786440 | tf_op jit(solution)/shard_map/ppermute | solution.py:515
  2.6 1.7 %pack.1 = (bf16[72,512]{1,0:T(8,128)(2,1)}, f32[3,8,128]{2,1,0:T(8,128)}) custom-call(bf16[64,512]{1,0:T(8,128)(2,1)} %bitcast.8, f32[8,16]{1,0:T(8,128)} %bitcast.9, f32[8,16]{1,0:T(8,128)} %bitcast.10, f32[1,8]{1,0:T(1,128)} %refs_3_.1), custom_call_target="tpu_custom_call" | custom-call | tf_op jit(solution)/shard_map/pack/pallas_call | solution.py:502
  4.3 10.0 %collective-permute-start.4 = (bf16[72,512]{1,0:T(8,128)(2,1)}, bf16[72,512]{1,0:T(8,128)(2,1)S(1)}, u32[]{:S(2)}, u32[]{:S(2)}) collective-permute-start(bf16[72,512]{1,0:T(8,128)(2,1)} %get-tuple-element.20.refs_0_.block_ref), channel_id=1, source_target_pairs={{0,64},{64,0},{1,65},{65,1},{2,66},{66,2},{3,67},{67,3},{4,68},{68... | collective-permute-start | bytes 221192 | tf_op jit(solution)/shard_map/ppermute | solution.py:514
  14.3 0.0 collective-permute-done.second_ref
  14.3 0.0 copy-start.3
  14.3 0.9 copy-done.3
  15.2 0.0 copy-start.4
  15.2 0.9 copy-done.4
  16.2 0.0 copy-start
  16.2 4.3 %collective-permute-start.2 = (bf16[2,256,512]{2,1,0:T(8,128)(2,1)S(1)}, bf16[2,256,512]{2,1,0:T(8,128)(2,1)S(1)}, u32[]{:S(2)}, u32[]{:S(2)}) collective-permute-start(bf16[2,256,512]{2,1,0:T(8,128)(2,1)S(1)} %tile.1.tile_ref), channel_id=1, source_target_pairs={{0,2},{1,7},{2,132},{3,129},{4,262},{5,259},{6,384},{7,389},{128,4... | collective-permute-start | bytes 1572872 | tf_op jit(solution)/shard_map/ppermute | solution.py:547
  20.5 3.4 %collective-permute-start.1 = (bf16[2,256,512]{2,1,0:T(8,128)(2,1)S(1)}, bf16[2,256,512]{2,1,0:T(8,128)(2,1)S(1)}, u32[]{:S(2)}, u32[]{:S(2)}) collective-permute-start(bf16[2,256,512]{2,1,0:T(8,128)(2,1)S(1)} %tile.1.tile_ref), channel_id=1, source_target_pairs={{0,0},{1,5},{2,130},{3,135},{4,260},{5,257},{6,390},{7,387},{128,2... | collective-permute-start | bytes 1572872 | tf_op jit(solution)/shard_map/ppermute | solution.py:547
  23.9 0.7 stack.23.place_ref
  24.6 0.0 collective-permute-done.4.far_ref
  24.6 0.0 copy-done
  24.6 0.0 copy-start.8
  24.6 0.6 copy-done.8
  25.2 2.0 %spread.1 = bf16[8,136,512]{2,1,0:T(8,128)(2,1)} custom-call(s32[5]{0:T(128)} %stack.23.place_ref, bf16[72,512]{1,0:T(8,128)(2,1)} %get-tuple-element.20.refs_0_.block_ref, bf16[72,512]{1,0:T(8,128)(2,1)} %copy-done.8, bf16[2,256,512]{2,1,0:T(8,128)(2,1)} %copy-done), custom_call_target="tpu_custom_call" | custom-call | tf_op jit(solution)/shard_map/spread/pallas_call | solution.py:524
  27.3 7.1 %all-to-all-start = ((bf16[8,136,512]{2,1,0:T(8,128)(2,1)}), bf16[8,136,512]{2,1,0:T(8,128)(2,1)S(1)}, u32[]{:S(2)}, u32[]{:S(2)}) async-start(bf16[8,136,512]{2,1,0:T(8,128)(2,1)} %spread.1), calls=%async_computation | async-start | bytes 2228224 | tf_op jit(solution)/shard_map/all_to_all | solution.py:537
  34.4 0.0 copy-start.6
  34.4 7.6 %collective-permute-done.2.second_ref = bf16[2,256,512]{2,1,0:T(8,128)(2,1)S(1)} collective-permute-done((bf16[2,256,512]{2,1,0:T(8,128)(2,1)S(1)}, bf16[2,256,512]{2,1,0:T(8,128)(2,1)S(1)}, u32[]{:S(2)}, u32[]{:S(2)}) %collective-permute-start.2) | collective-permute-done | bytes 524320 | tf_op jit(solution)/shard_map/ppermute | solution.py:547
  42.0 0.0 collective-permute-done.1.first_ref
  42.0 0.1 join.1.mine_ref
  42.0 4.1 %collective-permute-start.3 = (bf16[2,2,256,512]{3,2,1,0:T(8,128)(2,1)S(1)}, bf16[2,2,256,512]{3,2,1,0:T(8,128)(2,1)S(1)}, u32[]{:S(2)}, u32[]{:S(2)}) collective-permute-start(bf16[2,2,256,512]{3,2,1,0:T(8,128)(2,1)S(1)} %join.1.mine_ref), channel_id=1, source_target_pairs={{0,1},{1,0},{2,3},{3,2},{4,5},{5,4},{6,7},{7,6},{8,9},{9,8},{10,11... | collective-permute-start | bytes 3145736 | tf_op jit(solution)/shard_map/ppermute | solution.py:555
  46.2 2.3 %collective-permute-done.3.theirs_ref = bf16[2,2,256,512]{3,2,1,0:T(8,128)(2,1)S(1)} collective-permute-done((bf16[2,2,256,512]{3,2,1,0:T(8,128)(2,1)S(1)}, bf16[2,2,256,512]{3,2,1,0:T(8,128)(2,1)S(1)}, u32[]{:S(2)}, u32[]{:S(2)}) %collective-permute-start.3) | collective-permute-done | bytes 1048608 | tf_op jit(solution)/shard_map/ppermute | solution.py:555
  48.4 17.5 %all-to-all-done.proj_ref = bf16[8,136,512]{2,1,0:T(8,128)(2,1)S(1)} async-done(((bf16[8,136,512]{2,1,0:T(8,128)(2,1)}), bf16[8,136,512]{2,1,0:T(8,128)(2,1)S(1)}, u32[]{:S(2)}, u32[]{:S(2)}) %all-to-all-start) | async-done | bytes 1114144 | tf_op jit(solution)/shard_map/all_to_all | solution.py:537
  66.0 0.0 copy-done.6
  66.0 2.5 %partial_products.1 = bf16[4,288,512]{2,1,0:T(8,128)(2,1)S(1)} custom-call(s32[5]{0:T(128)S(1)} %copy-done.6, bf16[2,2,256,512]{3,2,1,0:T(8,128)(2,1)S(1)} %join.1.mine_ref, bf16[2,2,256,512]{3,2,1,0:T(8,128)(2,1)S(1)} %collective-permute-done.3.theirs_ref, bf16[8,136,512]{2,1,0:T(8,128)(2,1)S(1)} %all-to-all-done.proj_ref), custom_call_target="tpu_custom_call" | custom-call | tf_op jit(solution)/shard_map/partial_products/pallas_call | solution.py:562
  68.5 0.0 copy-start.1
  68.5 0.0 copy-start.2
  68.5 0.0 copy-start.5
  68.5 19.6 %all_to_all.20.parts_ref = bf16[4,288,512]{2,1,0:T(8,128)(2,1)S(1)} all-to-all(bf16[4,288,512]{2,1,0:T(8,128)(2,1)S(1)} %partial_products.1), channel_id=1, replica_groups=mesh['x'=4,'zh'=2,'y'=8,'zl'=4,'core'=2] {'x'}, dimensions={0} | all-to-all | bytes 2359296 | tf_op jit(solution)/shard_map/all_to_all | solution.py:574
  88.1 0.0 copy-done.1
  88.1 0.0 copy-done.2
  88.1 0.0 copy-done.5
  88.1 5.8 %local_scans.1 = (bf16[256,512]{1,0:T(8,128)(2,1)S(1)}, f32[3,128,128]{2,1,0:T(8,128)S(1)}, f32[8,128]{1,0:T(8,128)S(1)}, f32[1024,128]{1,0:T(8,128)S(1)}, f32[1...) custom-call(s32[5]{0:T(128)S(1)} %copy-done.6, ...), custom_call_target="tpu_custom_call" | custom-call | tf_op jit(solution)/shard_map/local_scans/pallas_call | solution.py:578
  94.0 0.0 copy-start.7
  94.0 17.4 %all_to_all.21.recv_ref = bf16[8,208,128]{2,1,0:T(8,128)(2,1)S(1)} all-to-all(bf16[8,208,128]{2,1,0:T(8,128)(2,1)S(1)} %get-tuple-element.21), channel_id=1, replica_groups=mesh['x'=4,'zh'=2,'y'=8,'zl'=4,'core'=2] {'y'}, dimensions={0} | all-to-all | bytes 851968 | tf_op jit(solution)/shard_map/all_to_all | solution.py:596
  111.4 1.2 chain_ring.1
  112.7 15.8 %all_to_all.22.recv_ref = bf16[8,144,128]{2,1,0:T(8,128)(2,1)S(1)} all-to-all(bf16[8,144,128]{2,1,0:T(8,128)(2,1)S(1)} %get-tuple-element.24), channel_id=1, replica_groups=mesh['x'=4,'zh'=2,'y'=8,'zl'=4,'core'=2] {'x','zh'}, dimensions={0} | all-to-all | bytes 589824 | tf_op jit(solution)/shard_map/all_to_all | solution.py:605
  128.4 0.0 copy-done.7
  128.4 4.6 %final_scan.1 = (bf16[256,512]{1,0:T(8,128)(2,1)}, bf16[256,512]{1,0:T(8,128)(2,1)}, bf16[256,512]{1,0:T(8,128)(2,1)}, f32[1,8,16]{2,1,0:T(8,128)}, f32[1,8,16]{2,1,0:T(8,128)}, /*index=5*/f32[1,8]{1,0:T(1,128)}) custom-call(s32[5]{0:T(128)S(1)} %copy-done.6, f32[3,8,128]{2,1,0:T(8,128)S(1)} %copy-done.7, bf16[8,144,128]{2,1,0:T(8,128)(2,1)S(1)} %all_to_all.22.recv_ref, ...), custom_call_target="tpu_custom_call" | custom-call | tf_op jit(solution)/shard_map/final_scan/pallas_call | solution.py:606
  (1 shorter events, 0.0 us)
Async XLA Ops:
  0.6 13.6 %collective-permute-start = (bf16[256,512]{1,0:T(8,128)(2,1)}, bf16[256,512]{1,0:T(8,128)(2,1)S(1)}, u32[]{:S(2)}, u32[]{:S(2)}) collective-permute-start(bf16[256,512]{1,0:T(8,128)(2,1)} %first_ref.1), channel_id=1, source_target_pairs={{0,1},{1,0},{2,3},{3,2},{4,5},{5,4},{6,7},{7,6},{8,9},{9,8},{10,11... | collective-permute-start | bytes 786440 | tf_op jit(solution)/shard_map/ppermute | solution.py:515
  4.3 20.3 %collective-permute-start.4 = (bf16[72,512]{1,0:T(8,128)(2,1)}, bf16[72,512]{1,0:T(8,128)(2,1)S(1)}, u32[]{:S(2)}, u32[]{:S(2)}) collective-permute-start(bf16[72,512]{1,0:T(8,128)(2,1)} %get-tuple-element.20.refs_0_.block_ref), channel_id=1, source_target_pairs={{0,64},{64,0},{1,65},{65,1},{2,66},{66,2},{3,67},{67,3},{4,68},{68... | collective-permute-start | bytes 221192 | tf_op jit(solution)/shard_map/ppermute | solution.py:514
  14.3 0.9 copy-start.3
  15.2 0.9 copy-start.4
  16.2 8.4 %copy-start = (bf16[2,256,512]{2,1,0:T(8,128)(2,1)}, bf16[2,256,512]{2,1,0:T(8,128)(2,1)S(1)}, u32[]{:S(2)}) copy-start(bf16[2,256,512]{2,1,0:T(8,128)(2,1)S(1)} %tile.1.tile_ref) | copy-start | bytes 1572868
  16.2 25.8 %collective-permute-start.2 = (bf16[2,256,512]{2,1,0:T(8,128)(2,1)S(1)}, bf16[2,256,512]{2,1,0:T(8,128)(2,1)S(1)}, u32[]{:S(2)}, u32[]{:S(2)}) collective-permute-start(bf16[2,256,512]{2,1,0:T(8,128)(2,1)S(1)} %tile.1.tile_ref), channel_id=1, source_target_pairs={{0,2},{1,7},{2,132},{3,129},{4,262},{5,259},{6,384},{7,389},{128,4... | collective-permute-start | bytes 1572872 | tf_op jit(solution)/shard_map/ppermute | solution.py:547
  20.5 21.4 %collective-permute-start.1 = (bf16[2,256,512]{2,1,0:T(8,128)(2,1)S(1)}, bf16[2,256,512]{2,1,0:T(8,128)(2,1)S(1)}, u32[]{:S(2)}, u32[]{:S(2)}) collective-permute-start(bf16[2,256,512]{2,1,0:T(8,128)(2,1)S(1)} %tile.1.tile_ref), channel_id=1, source_target_pairs={{0,0},{1,5},{2,130},{3,135},{4,260},{5,257},{6,390},{7,387},{128,2... | collective-permute-start | bytes 1572872 | tf_op jit(solution)/shard_map/ppermute | solution.py:547
  24.6 0.6 copy-start.8
  27.3 38.7 %all-to-all-start = ((bf16[8,136,512]{2,1,0:T(8,128)(2,1)}), bf16[8,136,512]{2,1,0:T(8,128)(2,1)S(1)}, u32[]{:S(2)}, u32[]{:S(2)}) async-start(bf16[8,136,512]{2,1,0:T(8,128)(2,1)} %spread.1), calls=%async_computation | async-start | bytes 2228224 | tf_op jit(solution)/shard_map/all_to_all | solution.py:537
  34.4 31.6 %copy-start.6 = (s32[5]{0:T(128)S(1)}, s32[5]{0:T(128)}, u32[]{:S(2)}) copy-start(s32[5]{0:T(128)} %stack.23.place_ref) | copy-start | bytes 64
  42.0 6.4 %collective-permute-start.3 = (bf16[2,2,256,512]{3,2,1,0:T(8,128)(2,1)S(1)}, bf16[2,2,256,512]{3,2,1,0:T(8,128)(2,1)S(1)}, u32[]{:S(2)}, u32[]{:S(2)}) collective-permute-start(bf16[2,2,256,512]{3,2,1,0:T(8,128)(2,1)S(1)} %join.1.mine_ref), channel_id=1, source_target_pairs={{0,1},{1,0},{2,3},{3,2},{4,5},{5,4},{6,7},{7,6},{8,9},{9,8},{10,11... | collective-permute-start | bytes 3145736 | tf_op jit(solution)/shard_map/ppermute | solution.py:555
  68.5 19.6 %copy-start.1 = (bf16[256,512]{1,0:T(8,128)(2,1)S(1)}, bf16[256,512]{1,0:T(8,128)(2,1)}, u32[]{:S(2)}) copy-start(bf16[256,512]{1,0:T(8,128)(2,1)} %values_ref.3) | copy-start | bytes 786436
  68.5 19.6 %copy-start.2 = (bf16[256,512]{1,0:T(8,128)(2,1)S(1)}, bf16[256,512]{1,0:T(8,128)(2,1)}, u32[]{:S(2)}) copy-start(bf16[256,512]{1,0:T(8,128)(2,1)} %gate_in_ref.3) | copy-start | bytes 786436
  68.5 19.6 %copy-start.5 = (bf16[256,512]{1,0:T(8,128)(2,1)S(1)}, bf16[256,512]{1,0:T(8,128)(2,1)}, u32[]{:S(2)}) copy-start(bf16[256,512]{1,0:T(8,128)(2,1)} %gate_out_ref.1) | copy-start | bytes 786436
  94.0 34.5 %copy-start.7 = (f32[3,8,128]{2,1,0:T(8,128)S(1)}, f32[3,8,128]{2,1,0:T(8,128)}, u32[]{:S(2)}) copy-start(f32[3,8,128]{2,1,0:T(8,128)} %get-tuple-element.19.own_ref) | copy-start | bytes 36868

commit v5 on v4

--- a/solution.py
+++ b/solution.py
@@ -223,12 +223,13 @@
         s = [decay[m] * s[m] + v for m in range(MODES)]
         return s, u
 
-    s, u = lax.fori_loop(0, half, forward, ([zero] * MODES, [zero] * MODES), unroll=4)
+    s, u = lax.fori_loop(0, half, forward, ([zero] * MODES, [zero] * MODES), unroll=32)
     for a, arrays in enumerate((s, u)):
         for m in range(MODES):
             halves[a, m] = arrays[m]
 
     blank = [zero] * GROUP
+    skip = zero
     for first in range(0, MODES, GROUP):
         decay = [tables_ref[1, mode_at(first + m), :] for m in range(GROUP)]
 
@@ -241,10 +242,10 @@
             w = [decay[m] * w[m] + g for m in range(GROUP)]
             z = [z[m] + v * w[m] for m in range(GROUP)]
             f = [f[m] + v * x[m] for m in range(GROUP)]
-            return w, x, z, f, skip + g * v
+            return w, x, z, f, skip + g * v if first == 0 else skip
 
         w, x, z, f, skip = lax.fori_loop(
-            0, half, backward, (blank, blank, blank, blank, zero), unroll=4
+            0, half, backward, (blank, blank, blank, blank, skip), unroll=32
         )
         for a, arrays in enumerate((w, x, z, f)):
             for m in range(GROUP):
@@ -420,7 +421,7 @@
         (g_rows, back_rows, w_ref, True),
     ):
         lax.fori_loop(
-            0, half, make(rows, out, reverse), [ref[mode_at(m), :] for m in range(MODES)], unroll=4
+            0, half, make(rows, out, reverse), [ref[mode_at(m), :] for m in range(MODES)], unroll=32
         )
     for h in range(2):
         for q in range(4):

time: 134 us -> 133 us (level)
  no operation moved by 1% of the time
where the time goes in v5:
time: 133 us; the launch traced here: 132 us
  blocking collectives  52.8 us (40%)
  starting transfers between devices  30.8 us (23%)
  waiting for transfers between devices  27.4 us (21%)
  Pallas kernels  16.9 us (13%)
  local copies, waits for them, and re-layouts  3.2 us (2%)
    all_to_all x1, blocking collectives, per_device(): parts = exchange(parts, 'x')  19.6 us
    all_to_all x1, waiting for transfers between devices, per_device(): proj = exchange(proj, 'y')  17.5 us
    all_to_all x1, blocking collectives, per_device(): recv = exchange(send, 'y')  17.4 us
    all_to_all x1, blocking collectives, per_device(): recv = exchange(send, ('x', 'zh'))  15.8 us
    ppermute x1, starting transfers between devices, per_device(): far = lax.ppermute(block, 'zh', swap)  10 us
    ppermute x2, starting transfers between devices, per_device(): mine.append(lax.ppermute(tile, ('x', 'zl', 'core'), moves))  7.69 us
    ppermute x2, waiting for transfers between devices, per_device(): mine.append(lax.ppermute(tile, ('x', 'zl', 'core'), moves))  7.59 us
    all_to_all x1, starting transfers between devices, per_device(): proj = exchange(proj, 'y')  7.1 us
  transfers between devices with their start and end apart: 6, of which 3 were waited for; matrix products, arithmetic and copies ran while one was open for 1% of the time, Pallas kernels for 3%

profile of v5, /device:TPU:64, one launch (start us, length us, event | category | flops | bytes accessed | tf_op | source)
XLA Modules:
  0.0 132.0 jit_solution(13117359812087253332)
XLA Ops:
  0.6 1.9 %collective-permute-start = (bf16[256,512]{1,0:T(8,128)(2,1)}, bf16[256,512]{1,0:T(8,128)(2,1)S(1)}, u32[]{:S(2)}, u32[]{:S(2)}) collective-permute-start(bf16[256,512]{1,0:T(8,128)(2,1)} %first_ref.1), channel_id=1, source_target_pairs={{0,1},{1,0},{2,3},{3,2},{4,5},{5,4},{6,7},{7,6},{8,9},{9,8},{10,11... | collective-permute-start | bytes 786440 | tf_op jit(solution)/shard_map/ppermute | solution.py:516
  2.6 1.7 %pack.1 = (bf16[72,512]{1,0:T(8,128)(2,1)}, f32[3,8,128]{2,1,0:T(8,128)}) custom-call(bf16[64,512]{1,0:T(8,128)(2,1)} %bitcast.8, f32[8,16]{1,0:T(8,128)} %bitcast.9, f32[8,16]{1,0:T(8,128)} %bitcast.10, f32[1,8]{1,0:T(1,128)} %refs_3_.1), custom_call_target="tpu_custom_call" | custom-call | tf_op jit(solution)/shard_map/pack/pallas_call | solution.py:503
  4.3 10.0 %collective-permute-start.4 = (bf16[72,512]{1,0:T(8,128)(2,1)}, bf16[72,512]{1,0:T(8,128)(2,1)S(1)}, u32[]{:S(2)}, u32[]{:S(2)}) collective-permute-start(bf16[72,512]{1,0:T(8,128)(2,1)} %get-tuple-element.20.refs_0_.block_ref), channel_id=1, source_target_pairs={{0,64},{64,0},{1,65},{65,1},{2,66},{66,2},{3,67},{67,3},{4,68},{68... | collective-permute-start | bytes 221192 | tf_op jit(solution)/shard_map/ppermute | solution.py:515
  14.3 0.0 collective-permute-done.second_ref
  14.3 0.0 copy-start.3
  14.3 0.9 copy-done.3
  15.2 0.0 copy-start.4
  15.2 0.9 copy-done.4
  16.2 0.0 copy-start
  16.2 4.3 %collective-permute-start.2 = (bf16[2,256,512]{2,1,0:T(8,128)(2,1)S(1)}, bf16[2,256,512]{2,1,0:T(8,128)(2,1)S(1)}, u32[]{:S(2)}, u32[]{:S(2)}) collective-permute-start(bf16[2,256,512]{2,1,0:T(8,128)(2,1)S(1)} %tile.1.tile_ref), channel_id=1, source_target_pairs={{0,2},{1,7},{2,132},{3,129},{4,262},{5,259},{6,384},{7,389},{128,4... | collective-permute-start | bytes 1572872 | tf_op jit(solution)/shard_map/ppermute | solution.py:548
  20.5 3.4 %collective-permute-start.1 = (bf16[2,256,512]{2,1,0:T(8,128)(2,1)S(1)}, bf16[2,256,512]{2,1,0:T(8,128)(2,1)S(1)}, u32[]{:S(2)}, u32[]{:S(2)}) collective-permute-start(bf16[2,256,512]{2,1,0:T(8,128)(2,1)S(1)} %tile.1.tile_ref), channel_id=1, source_target_pairs={{0,0},{1,5},{2,130},{3,135},{4,260},{5,257},{6,390},{7,387},{128,2... | collective-permute-start | bytes 1572872 | tf_op jit(solution)/shard_map/ppermute | solution.py:548
  23.9 0.7 stack.23.place_ref
  24.6 0.0 collective-permute-done.4.far_ref
  24.6 0.0 copy-done
  24.6 0.0 copy-start.8
  24.6 0.6 copy-done.8
  25.2 2.0 %spread.1 = bf16[8,136,512]{2,1,0:T(8,128)(2,1)} custom-call(s32[5]{0:T(128)} %stack.23.place_ref, bf16[72,512]{1,0:T(8,128)(2,1)} %get-tuple-element.20.refs_0_.block_ref, bf16[72,512]{1,0:T(8,128)(2,1)} %copy-done.8, bf16[2,256,512]{2,1,0:T(8,128)(2,1)} %copy-done), custom_call_target="tpu_custom_call" | custom-call | tf_op jit(solution)/shard_map/spread/pallas_call | solution.py:525
  27.3 7.1 %all-to-all-start = ((bf16[8,136,512]{2,1,0:T(8,128)(2,1)}), bf16[8,136,512]{2,1,0:T(8,128)(2,1)S(1)}, u32[]{:S(2)}, u32[]{:S(2)}) async-start(bf16[8,136,512]{2,1,0:T(8,128)(2,1)} %spread.1), calls=%async_computation | async-start | bytes 2228224 | tf_op jit(solution)/shard_map/all_to_all | solution.py:538
  34.4 0.0 copy-start.6
  34.4 7.6 %collective-permute-done.2.second_ref = bf16[2,256,512]{2,1,0:T(8,128)(2,1)S(1)} collective-permute-done((bf16[2,256,512]{2,1,0:T(8,128)(2,1)S(1)}, bf16[2,256,512]{2,1,0:T(8,128)(2,1)S(1)}, u32[]{:S(2)}, u32[]{:S(2)}) %collective-permute-start.2) | collective-permute-done | bytes 524320 | tf_op jit(solution)/shard_map/ppermute | solution.py:548
  42.0 0.0 collective-permute-done.1.first_ref
  42.0 0.1 join.1.mine_ref
  42.0 4.1 %collective-permute-start.3 = (bf16[2,2,256,512]{3,2,1,0:T(8,128)(2,1)S(1)}, bf16[2,2,256,512]{3,2,1,0:T(8,128)(2,1)S(1)}, u32[]{:S(2)}, u32[]{:S(2)}) collective-permute-start(bf16[2,2,256,512]{3,2,1,0:T(8,128)(2,1)S(1)} %join.1.mine_ref), channel_id=1, source_target_pairs={{0,1},{1,0},{2,3},{3,2},{4,5},{5,4},{6,7},{7,6},{8,9},{9,8},{10,11... | collective-permute-start | bytes 3145736 | tf_op jit(solution)/shard_map/ppermute | solution.py:556
  46.2 2.3 %collective-permute-done.3.theirs_ref = bf16[2,2,256,512]{3,2,1,0:T(8,128)(2,1)S(1)} collective-permute-done((bf16[2,2,256,512]{3,2,1,0:T(8,128)(2,1)S(1)}, bf16[2,2,256,512]{3,2,1,0:T(8,128)(2,1)S(1)}, u32[]{:S(2)}, u32[]{:S(2)}) %collective-permute-start.3) | collective-permute-done | bytes 1048608 | tf_op jit(solution)/shard_map/ppermute | solution.py:556
  48.4 17.5 %all-to-all-done.proj_ref = bf16[8,136,512]{2,1,0:T(8,128)(2,1)S(1)} async-done(((bf16[8,136,512]{2,1,0:T(8,128)(2,1)}), bf16[8,136,512]{2,1,0:T(8,128)(2,1)S(1)}, u32[]{:S(2)}, u32[]{:S(2)}) %all-to-all-start) | async-done | bytes 1114144 | tf_op jit(solution)/shard_map/all_to_all | solution.py:538
  66.0 0.0 copy-done.6
  66.0 2.5 %partial_products.1 = bf16[4,288,512]{2,1,0:T(8,128)(2,1)S(1)} custom-call(s32[5]{0:T(128)S(1)} %copy-done.6, bf16[2,2,256,512]{3,2,1,0:T(8,128)(2,1)S(1)} %join.1.mine_ref, bf16[2,2,256,512]{3,2,1,0:T(8,128)(2,1)S(1)} %collective-permute-done.3.theirs_ref, bf16[8,136,512]{2,1,0:T(8,128)(2,1)S(1)} %all-to-all-done.proj_ref), custom_call_target="tpu_custom_call" | custom-call | tf_op jit(solution)/shard_map/partial_products/pallas_call | solution.py:563
  68.5 0.0 copy-start.1
  68.5 0.0 copy-start.2
  68.5 0.0 copy-start.5
  68.5 19.6 %all_to_all.20.parts_ref = bf16[4,288,512]{2,1,0:T(8,128)(2,1)S(1)} all-to-all(bf16[4,288,512]{2,1,0:T(8,128)(2,1)S(1)} %partial_products.1), channel_id=1, replica_groups=mesh['x'=4,'zh'=2,'y'=8,'zl'=4,'core'=2] {'x'}, dimensions={0} | all-to-all | bytes 2359296 | tf_op jit(solution)/shard_map/all_to_all | solution.py:575
  88.1 0.0 copy-done.1
  88.1 0.0 copy-done.2
  88.1 0.0 copy-done.5
  88.1 5.1 %local_scans.1 = (bf16[256,512]{1,0:T(8,128)(2,1)S(1)}, f32[3,128,128]{2,1,0:T(8,128)S(1)}, f32[8,128]{1,0:T(8,128)S(1)}, f32[1024,128]{1,0:T(8,128)S(1)}, f32[1...) custom-call(s32[5]{0:T(128)S(1)} %copy-done.6, ...), custom_call_target="tpu_custom_call" | custom-call | tf_op jit(solution)/shard_map/local_scans/pallas_call | solution.py:579
  93.2 0.0 copy-start.7
  93.2 17.4 %all_to_all.21.recv_ref = bf16[8,208,128]{2,1,0:T(8,128)(2,1)S(1)} all-to-all(bf16[8,208,128]{2,1,0:T(8,128)(2,1)S(1)} %get-tuple-element.21), channel_id=1, replica_groups=mesh['x'=4,'zh'=2,'y'=8,'zl'=4,'core'=2] {'y'}, dimensions={0} | all-to-all | bytes 851968 | tf_op jit(solution)/shard_map/all_to_all | solution.py:597
  110.6 1.2 chain_ring.1
  111.9 15.8 %all_to_all.22.recv_ref = bf16[8,144,128]{2,1,0:T(8,128)(2,1)S(1)} all-to-all(bf16[8,144,128]{2,1,0:T(8,128)(2,1)S(1)} %get-tuple-element.24), channel_id=1, replica_groups=mesh['x'=4,'zh'=2,'y'=8,'zl'=4,'core'=2] {'x','zh'}, dimensions={0} | all-to-all | bytes 589824 | tf_op jit(solution)/shard_map/all_to_all | solution.py:606
  127.7 0.0 copy-done.7
  127.7 4.3 %final_scan.1 = (bf16[256,512]{1,0:T(8,128)(2,1)}, bf16[256,512]{1,0:T(8,128)(2,1)}, bf16[256,512]{1,0:T(8,128)(2,1)}, f32[1,8,16]{2,1,0:T(8,128)}, f32[1,8,16]{2,1,0:T(8,128)}, /*index=5*/f32[1,8]{1,0:T(1,128)}) custom-call(s32[5]{0:T(128)S(1)} %copy-done.6, f32[3,8,128]{2,1,0:T(8,128)S(1)} %copy-done.7, bf16[8,144,128]{2,1,0:T(8,128)(2,1)S(1)} %all_to_all.22.recv_ref, ...), custom_call_target="tpu_custom_call" | custom-call | tf_op jit(solution)/shard_map/final_scan/pallas_call | solution.py:607
  (1 shorter events, 0.0 us)
Async XLA Ops:
  0.6 13.6 %collective-permute-start = (bf16[256,512]{1,0:T(8,128)(2,1)}, bf16[256,512]{1,0:T(8,128)(2,1)S(1)}, u32[]{:S(2)}, u32[]{:S(2)}) collective-permute-start(bf16[256,512]{1,0:T(8,128)(2,1)} %first_ref.1), channel_id=1, source_target_pairs={{0,1},{1,0},{2,3},{3,2},{4,5},{5,4},{6,7},{7,6},{8,9},{9,8},{10,11... | collective-permute-start | bytes 786440 | tf_op jit(solution)/shard_map/ppermute | solution.py:516
  4.3 20.3 %collective-permute-start.4 = (bf16[72,512]{1,0:T(8,128)(2,1)}, bf16[72,512]{1,0:T(8,128)(2,1)S(1)}, u32[]{:S(2)}, u32[]{:S(2)}) collective-permute-start(bf16[72,512]{1,0:T(8,128)(2,1)} %get-tuple-element.20.refs_0_.block_ref), channel_id=1, source_target_pairs={{0,64},{64,0},{1,65},{65,1},{2,66},{66,2},{3,67},{67,3},{4,68},{68... | collective-permute-start | bytes 221192 | tf_op jit(solution)/shard_map/ppermute | solution.py:515
  14.3 0.9 copy-start.3
  15.2 0.9 copy-start.4
  16.2 8.4 %copy-start = (bf16[2,256,512]{2,1,0:T(8,128)(2,1)}, bf16[2,256,512]{2,1,0:T(8,128)(2,1)S(1)}, u32[]{:S(2)}) copy-start(bf16[2,256,512]{2,1,0:T(8,128)(2,1)S(1)} %tile.1.tile_ref) | copy-start | bytes 1572868
  16.2 25.8 %collective-permute-start.2 = (bf16[2,256,512]{2,1,0:T(8,128)(2,1)S(1)}, bf16[2,256,512]{2,1,0:T(8,128)(2,1)S(1)}, u32[]{:S(2)}, u32[]{:S(2)}) collective-permute-start(bf16[2,256,512]{2,1,0:T(8,128)(2,1)S(1)} %tile.1.tile_ref), channel_id=1, source_target_pairs={{0,2},{1,7},{2,132},{3,129},{4,262},{5,259},{6,384},{7,389},{128,4... | collective-permute-start | bytes 1572872 | tf_op jit(solution)/shard_map/ppermute | solution.py:548
  20.5 21.4 %collective-permute-start.1 = (bf16[2,256,512]{2,1,0:T(8,128)(2,1)S(1)}, bf16[2,256,512]{2,1,0:T(8,128)(2,1)S(1)}, u32[]{:S(2)}, u32[]{:S(2)}) collective-permute-start(bf16[2,256,512]{2,1,0:T(8,128)(2,1)S(1)} %tile.1.tile_ref), channel_id=1, source_target_pairs={{0,0},{1,5},{2,130},{3,135},{4,260},{5,257},{6,390},{7,387},{128,2... | collective-permute-start | bytes 1572872 | tf_op jit(solution)/shard_map/ppermute | solution.py:548
  24.6 0.6 copy-start.8
  27.3 38.7 %all-to-all-start = ((bf16[8,136,512]{2,1,0:T(8,128)(2,1)}), bf16[8,136,512]{2,1,0:T(8,128)(2,1)S(1)}, u32[]{:S(2)}, u32[]{:S(2)}) async-start(bf16[8,136,512]{2,1,0:T(8,128)(2,1)} %spread.1), calls=%async_computation | async-start | bytes 2228224 | tf_op jit(solution)/shard_map/all_to_all | solution.py:538
  34.4 31.6 %copy-start.6 = (s32[5]{0:T(128)S(1)}, s32[5]{0:T(128)}, u32[]{:S(2)}) copy-start(s32[5]{0:T(128)} %stack.23.place_ref) | copy-start | bytes 64
  42.0 6.4 %collective-permute-start.3 = (bf16[2,2,256,512]{3,2,1,0:T(8,128)(2,1)S(1)}, bf16[2,2,256,512]{3,2,1,0:T(8,128)(2,1)S(1)}, u32[]{:S(2)}, u32[]{:S(2)}) collective-permute-start(bf16[2,2,256,512]{3,2,1,0:T(8,128)(2,1)S(1)} %join.1.mine_ref), channel_id=1, source_target_pairs={{0,1},{1,0},{2,3},{3,2},{4,5},{5,4},{6,7},{7,6},{8,9},{9,8},{10,11... | collective-permute-start | bytes 3145736 | tf_op jit(solution)/shard_map/ppermute | solution.py:556
  68.5 19.6 %copy-start.1 = (bf16[256,512]{1,0:T(8,128)(2,1)S(1)}, bf16[256,512]{1,0:T(8,128)(2,1)}, u32[]{:S(2)}) copy-start(bf16[256,512]{1,0:T(8,128)(2,1)} %values_ref.3) | copy-start | bytes 786436
  68.5 19.6 %copy-start.2 = (bf16[256,512]{1,0:T(8,128)(2,1)S(1)}, bf16[256,512]{1,0:T(8,128)(2,1)}, u32[]{:S(2)}) copy-start(bf16[256,512]{1,0:T(8,128)(2,1)} %gate_in_ref.3) | copy-start | bytes 786436
  68.5 19.6 %copy-start.5 = (bf16[256,512]{1,0:T(8,128)(2,1)S(1)}, bf16[256,512]{1,0:T(8,128)(2,1)}, u32[]{:S(2)}) copy-start(bf16[256,512]{1,0:T(8,128)(2,1)} %gate_out_ref.1) | copy-start | bytes 786436
  93.2 34.5 %copy-start.7 = (f32[3,8,128]{2,1,0:T(8,128)S(1)}, f32[3,8,128]{2,1,0:T(8,128)}, u32[]{:S(2)}) copy-start(f32[3,8,128]{2,1,0:T(8,128)} %get-tuple-element.19.own_ref) | copy-start | bytes 36868

commit v6 on v5

--- a/solution.py
+++ b/solution.py
@@ -106,32 +106,40 @@
     return slice(8 * m, 8 * m + 8)
 
 
-def product_kernel(place_ref, mine_ref, theirs_ref, proj_ref, out_ref):
+def product_kernel(place_ref, mine_ref, theirs_ref, proj_ref, v_rows, out_ref):
+    del v_rows
     core = place_ref[0]
     ring, height, cols = proj_ref.shape
     depth = (height - 8) // 2
-    rows = mine_ref.shape[2]
+    count, rows = out_ref.shape[0], mine_ref.shape[2]
 
     def rows_of(c):
         at = pl.ds(pl.multiple_of(c * depth, depth), depth)
         return proj_ref[:, at, :].reshape(ring * depth, cols)
-
-    for k in range(4):
-        tile_ref = (mine_ref, theirs_ref)[k // 2].at[k % 2]
-        first = core if k < 2 else 1 - core
-
-        @pl.when(pl.program_id(0) == k)
-        def _():
-            total = jnp.dot(tile_ref[0], rows_of(first), preferred_element_type=jnp.float32)
-            total += jnp.dot(tile_ref[1], rows_of(1 - first), preferred_element_type=jnp.float32)
-            out_ref[0, 0:rows, :] = total.astype(jnp.bfloat16)
 
     params = [
         proj_ref[y].astype(jnp.float32)[2 * depth + 2 * z : 2 * depth + 2 * z + 2]
         for z in range(2)
         for y in range(ring)
     ]
-    out_ref[0, rows:, :] = jnp.concatenate(params, axis=0).astype(jnp.bfloat16)
+    params = jnp.concatenate(params, axis=0).astype(jnp.bfloat16)
+    for k in range(4):
+        tile_ref = (mine_ref, theirs_ref)[k // 2].at[k % 2]
+        first = core if k < 2 else 1 - core
+        total = jnp.dot(tile_ref[0], rows_of(first), preferred_element_type=jnp.float32)
+        total += jnp.dot(tile_ref[1], rows_of(1 - first), preferred_element_type=jnp.float32)
+        to = lax.rem(place_ref[3] - place_ref[4] + 2 * count - 2 * first - k % 2, count)
+        out_ref[pl.ds(to, 1), 0:rows, :] = total.astype(jnp.bfloat16)[None]
+        out_ref[pl.ds(to, 1), rows:, :] = params[None]
+
+
+def value_kernel(half, values_ref, gate_in_ref, v_rows):
+    mixed_values = (
+        (gate_in_ref[...].astype(jnp.float32) * values_ref[...].astype(jnp.float32))
+        .astype(jnp.bfloat16)
+        .astype(jnp.float32)
+    )
+    to_steps(v_rows, mixed_values, half)
 
 
 def two_terms(x, pad):
@@ -156,13 +164,11 @@
     half,
     place_ref,
     parts_ref,
-    values_ref,
-    gate_in_ref,
+    v_rows,
     gate_out_ref,
     gated_ref,
     tables_ref,
     skip_ref,
-    v_rows,
     g_rows,
     send_ref,
     edge_ref,
@@ -196,12 +202,6 @@
             tables_ref[1, at, :] = jnp.exp(-rate)
             tables_ref[2, at, :] = jnp.exp(-float(half) * rate)
             skip_ref[h * 4 + q : h * 4 + q + 1, :] = flipped[2 * MODES : 2 * MODES + 1]
-    mixed_values = (
-        (gate_in_ref[...].astype(jnp.float32) * values_ref[...].astype(jnp.float32))
-        .astype(jnp.bfloat16)
-        .astype(jnp.float32)
-    )
-    to_steps(v_rows, mixed_values, half)
     gated = parts_ref[0, 0:rows, :].astype(jnp.float32)
     for k in range(1, sources):
         gated += parts_ref[k, 0:rows, :].astype(jnp.float32)
@@ -555,34 +555,27 @@
     )(*mine)
     theirs = lax.ppermute(mine, "core", swap)
 
-    def tile_of(k, place):
-        core = jnp.where(k < 2, place[0], 1 - place[0])
-        return (lax.rem(place[3] - place[4] + 2 * nx - 2 * core - lax.rem(k, 2), nx), 0, 0)
-
+    v_rows = call(
+        functools.partial(value_kernel, half), shape((half * 8, LANES), f32), [], "value_steps"
+    )(values, gate_in)
     height = rows + nzh * ny * pencil // 4
-    parts = pl.pallas_call(
+    parts = call(
         product_kernel,
-        grid_spec=pltpu.PrefetchScalarGridSpec(
-            num_scalar_prefetch=1,
-            grid=(nx,),
-            in_specs=[whole(2, 2, rows, cols)] * 2 + [whole(*proj.shape)],
-            out_specs=pl.BlockSpec((1, height, cols), tile_of),
-        ),
-        out_shape=shape((nx, height, cols), bf16),
-        compiler_params=pltpu.CompilerParams(vmem_limit_bytes=VMEM),
-        name="partial_products",
-    )(place, mine, theirs, proj)
+        shape((nx, height, cols), bf16),
+        [],
+        "partial_products",
+        in_specs=[smem] + [vmem] * 3 + [pl.BlockSpec(memory_space=pl.ANY)],
+    )(place, mine, theirs, proj, v_rows)
     parts = exchange(parts, "x")
 
     many = 4 * MODES
     groups = nx * nzh
-    gated, tables, skip, v_rows, g_rows, send, edge, rates, own_table = call(
+    gated, tables, skip, g_rows, send, edge, rates, own_table = call(
         functools.partial(local_kernel, half),
         [
             shape((rows, cols), bf16),
             shape((3, MODES * 8, LANES), f32),
             shape((8, LANES), f32),
-            shape((half * 8, LANES), f32),
             shape((half * 8, LANES), f32),
             shape((ny, 2 * many + 8 * groups + 16, LANES), bf16),
             shape((2, MODES, 4, LANES), f32),
@@ -591,8 +584,8 @@
         ],
         [(cols, LANES), (6, MODES, 8, LANES), (4 * LANES, LANES), (cols, LANES)],
         "local_scans",
-        in_specs=[smem] + [vmem] * 4,
-    )(place, parts, values, gate_in, gate_out)
+        in_specs=[smem] + [vmem] * 3,
+    )(place, parts, v_rows, gate_out)
 
     recv = exchange(send, "y")
     send, near = call(

time: 133 us -> 133 us (level)
  local copies, waits for them, and re-layouts: 3.2 us -> 8.98 us
  waiting for transfers between devices: 27.4 us -> 23.4 us
    unnamed x18 -> x30, local copies, waits for them, and re-layouts: 2.53 us -> 8.37 us
    all_to_all x1, waiting for transfers between devices: 17.5 us -> 13.7 us  [per_device(): proj = exchange(proj, 'y')]
  transfers between devices with their start and end apart: 6 -> 6, of which waited for: 3 -> 3; matrix products, arithmetic and copies ran while one was open for 1% -> 0% of each run, Pallas kernels for 3% -> 3%
where the time goes in v6:
time: 133 us; the launch traced here: 132 us
  blocking collectives  52.8 us (40%)
  starting transfers between devices  30.1 us (23%)
  waiting for transfers between devices  23.4 us (18%)
  Pallas kernels  16.1 us (12%)
  local copies, waits for them, and re-layouts  8.98 us (7%)
    all_to_all x1, blocking collectives, per_device(): parts = exchange(parts, 'x')  19.6 us
    all_to_all x1, blocking collectives, per_device(): recv = exchange(send, 'y')  17.4 us
    all_to_all x1, blocking collectives, per_device(): recv = exchange(send, ('x', 'zh'))  15.8 us
    all_to_all x1, waiting for transfers between devices, per_device(): proj = exchange(proj, 'y')  13.7 us
    ppermute x1, starting transfers between devices, per_device(): far = lax.ppermute(block, 'zh', swap)  10 us
    unnamed x30, local copies, waits for them, and re-layouts  8.37 us
    ppermute x2, starting transfers between devices, per_device(): mine.append(lax.ppermute(tile, ('x', 'zl', 'core'), moves))  7.69 us
    ppermute x2, waiting for transfers between devices, per_device(): mine.append(lax.ppermute(tile, ('x', 'zl', 'core'), moves))  7.62 us
  transfers between devices with their start and end apart: 6, of which 3 were waited for; matrix products, arithmetic and copies ran while one was open for 0% of the time, Pallas kernels for 3%

profile of v6, /device:TPU:64, one launch (start us, length us, event | category | flops | bytes accessed | tf_op | source)
XLA Modules:
  0.0 132.2 jit_solution(1122354174405184824)
XLA Ops:
  0.6 1.9 %collective-permute-start = (bf16[256,512]{1,0:T(8,128)(2,1)}, bf16[256,512]{1,0:T(8,128)(2,1)S(1)}, u32[]{:S(2)}, u32[]{:S(2)}) collective-permute-start(bf16[256,512]{1,0:T(8,128)(2,1)} %first_ref.1), channel_id=1, source_target_pairs={{0,1},{1,0},{2,3},{3,2},{4,5},{5,4},{6,7},{7,6},{8,9},{9,8},{10,11... | collective-permute-start | bytes 786440 | tf_op jit(solution)/shard_map/ppermute | solution.py:516
  2.6 1.7 %pack.1 = (bf16[72,512]{1,0:T(8,128)(2,1)}, f32[3,8,128]{2,1,0:T(8,128)}) custom-call(bf16[64,512]{1,0:T(8,128)(2,1)} %bitcast.8, f32[8,16]{1,0:T(8,128)} %bitcast.9, f32[8,16]{1,0:T(8,128)} %bitcast.10, f32[1,8]{1,0:T(1,128)} %refs_3_.1), custom_call_target="tpu_custom_call" | custom-call | tf_op jit(solution)/shard_map/pack/pallas_call | solution.py:503
  4.3 10.0 %collective-permute-start.4 = (bf16[72,512]{1,0:T(8,128)(2,1)}, bf16[72,512]{1,0:T(8,128)(2,1)S(1)}, u32[]{:S(2)}, u32[]{:S(2)}) collective-permute-start(bf16[72,512]{1,0:T(8,128)(2,1)} %get-tuple-element.19.refs_0_.block_ref), channel_id=1, source_target_pairs={{0,64},{64,0},{1,65},{65,1},{2,66},{66,2},{3,67},{67,3},{4,68},{68... | collective-permute-start | bytes 221192 | tf_op jit(solution)/shard_map/ppermute | solution.py:515
  14.3 0.0 collective-permute-done.second_ref
  14.3 0.0 copy-start.5
  14.3 0.9 copy-done.5
  15.2 0.0 copy-start.6
  15.2 0.9 copy-done.6
  16.2 0.0 copy-start
  16.2 4.3 %collective-permute-start.2 = (bf16[2,256,512]{2,1,0:T(8,128)(2,1)S(1)}, bf16[2,256,512]{2,1,0:T(8,128)(2,1)S(1)}, u32[]{:S(2)}, u32[]{:S(2)}) collective-permute-start(bf16[2,256,512]{2,1,0:T(8,128)(2,1)S(1)} %tile.1.tile_ref), channel_id=1, source_target_pairs={{0,2},{1,7},{2,132},{3,129},{4,262},{5,259},{6,384},{7,389},{128,4... | collective-permute-start | bytes 1572872 | tf_op jit(solution)/shard_map/ppermute | solution.py:548
  20.5 3.4 %collective-permute-start.1 = (bf16[2,256,512]{2,1,0:T(8,128)(2,1)S(1)}, bf16[2,256,512]{2,1,0:T(8,128)(2,1)S(1)}, u32[]{:S(2)}, u32[]{:S(2)}) collective-permute-start(bf16[2,256,512]{2,1,0:T(8,128)(2,1)S(1)} %tile.1.tile_ref), channel_id=1, source_target_pairs={{0,0},{1,5},{2,130},{3,135},{4,260},{5,257},{6,390},{7,387},{128,2... | collective-permute-start | bytes 1572872 | tf_op jit(solution)/shard_map/ppermute | solution.py:548
  23.9 0.6 stack.23.place_ref
  24.5 0.0 collective-permute-done.4.far_ref
  24.5 0.0 copy-done
  24.5 0.0 copy-start.14
  24.5 0.6 copy-done.14
  25.2 2.0 %spread.1 = bf16[8,136,512]{2,1,0:T(8,128)(2,1)} custom-call(s32[5]{0:T(128)} %stack.23.place_ref, bf16[72,512]{1,0:T(8,128)(2,1)} %get-tuple-element.19.refs_0_.block_ref, bf16[72,512]{1,0:T(8,128)(2,1)} %copy-done.14, bf16[2,256,512]{2,1,0:T(8,128)(2,1)} %copy-done), custom_call_target="tpu_custom_call" | custom-call | tf_op jit(solution)/shard_map/spread/pallas_call | solution.py:525
  27.2 7.1 %all-to-all-start = ((bf16[8,136,512]{2,1,0:T(8,128)(2,1)}), bf16[8,136,512]{2,1,0:T(8,128)(2,1)S(1)}, u32[]{:S(2)}, u32[]{:S(2)}) async-start(bf16[8,136,512]{2,1,0:T(8,128)(2,1)} %spread.1), calls=%async_computation | async-start | bytes 2228224 | tf_op jit(solution)/shard_map/all_to_all | solution.py:538
  34.3 0.0 copy-start.3
  34.3 0.0 copy-start.4
  34.3 0.0 copy-start.8
  34.3 7.6 %collective-permute-done.2.second_ref = bf16[2,256,512]{2,1,0:T(8,128)(2,1)S(1)} collective-permute-done((bf16[2,256,512]{2,1,0:T(8,128)(2,1)S(1)}, bf16[2,256,512]{2,1,0:T(8,128)(2,1)S(1)}, u32[]{:S(2)}, u32[]{:S(2)}) %collective-permute-start.2) | collective-permute-done | bytes 524320 | tf_op jit(solution)/shard_map/ppermute | solution.py:548
  42.0 0.0 copy-start.10
  42.0 0.8 copy-done.10
  42.8 0.0 collective-permute-done.1.first_ref
  42.8 0.0 copy-start.12
  42.8 0.8 copy-done.12
  43.5 0.0 copy-start.11
  43.5 1.0 copy-done.11
  44.6 0.0 copy-start.13
  44.6 1.0 copy-done.13
  45.6 0.1 join.1.mine_ref
  45.7 3.3 %collective-permute-start.3 = (bf16[2,2,256,512]{3,2,1,0:T(8,128)(2,1)S(1)}, bf16[2,2,256,512]{3,2,1,0:T(8,128)(2,1)S(1)}, u32[]{:S(2)}, u32[]{:S(2)}) collective-permute-start(bf16[2,2,256,512]{3,2,1,0:T(8,128)(2,1)S(1)} %join.1.mine_ref), channel_id=1, source_target_pairs={{0,1},{1,0},{2,3},{3,2},{4,5},{5,4},{6,7},{7,6},{8,9},{9,8},{10,11... | collective-permute-start | bytes 3145736 | tf_op jit(solution)/shard_map/ppermute | solution.py:556
  49.0 0.0 copy-done.3
  49.0 0.0 copy-done.4
  49.1 0.1 value_steps.1.v_rows
  49.2 2.1 %collective-permute-done.3.theirs_ref = bf16[2,2,256,512]{3,2,1,0:T(8,128)(2,1)S(1)} collective-permute-done((bf16[2,2,256,512]{3,2,1,0:T(8,128)(2,1)S(1)}, bf16[2,2,256,512]{3,2,1,0:T(8,128)(2,1)S(1)}, u32[]{:S(2)}, u32[]{:S(2)}) %collective-permute-start.3) | collective-permute-done | bytes 1048608 | tf_op jit(solution)/shard_map/ppermute | solution.py:556
  51.3 0.0 copy-start.1
  51.3 1.0 copy-done.1
  52.3 13.7 %all-to-all-done.proj_ref = bf16[8,136,512]{2,1,0:T(8,128)(2,1)S(1)} async-done(((bf16[8,136,512]{2,1,0:T(8,128)(2,1)}), bf16[8,136,512]{2,1,0:T(8,128)(2,1)S(1)}, u32[]{:S(2)}, u32[]{:S(2)}) %all-to-all-start) | async-done | bytes 1114144 | tf_op jit(solution)/shard_map/all_to_all | solution.py:538
  65.9 0.0 copy-done.8
  65.9 0.0 copy-start.2
  65.9 1.2 copy-done.2
  67.2 1.8 %partial_products.1 = bf16[4,288,512]{2,1,0:T(8,128)(2,1)S(1)} custom-call(s32[5]{0:T(128)S(1)} %copy-done.8, bf16[2,2,256,512]{3,2,1,0:T(8,128)(2,1)S(1)} %join.1.mine_ref, bf16[2,2,256,512]{3,2,1,0:T(8,128)(2,1)S(1)} %copy-done.2, bf16[8,136,512]{2,1,0:T(8,128)(2,1)S(1)} %all-to-all-done.proj_ref, f32[1024,128]{1,0:T(8,128)S(1)} %value_steps.1.v_rows), custom_call_target="tpu_custom_call" | custom-call | tf_op jit(solution)/shard_map/partial_products/pallas_call | solution.py:562
  69.0 0.0 copy-start.7
  69.0 19.6 %all_to_all.20.parts_ref = bf16[4,288,512]{2,1,0:T(8,128)(2,1)S(1)} all-to-all(bf16[4,288,512]{2,1,0:T(8,128)(2,1)S(1)} %partial_products.1), channel_id=1, replica_groups=mesh['x'=4,'zh'=2,'y'=8,'zl'=4,'core'=2] {'x'}, dimensions={0} | all-to-all | bytes 2359296 | tf_op jit(solution)/shard_map/all_to_all | solution.py:569
  88.5 0.0 copy-done.7
  88.5 4.9 %local_scans.1 = (bf16[256,512]{1,0:T(8,128)(2,1)S(1)}, f32[3,128,128]{2,1,0:T(8,128)S(1)}, f32[8,128]{1,0:T(8,128)S(1)}, f32[1024,128]{1,0:T(8,128)S(1)}, bf16[...) custom-call(s32[5]{0:T(128)S(1)} %copy-done.8, ...), custom_call_target="tpu_custom_call" | custom-call | tf_op jit(solution)/shard_map/local_scans/pallas_call | solution.py:573
  93.4 0.0 copy-start.9
  93.4 17.4 %all_to_all.21.recv_ref = bf16[8,208,128]{2,1,0:T(8,128)(2,1)S(1)} all-to-all(bf16[8,208,128]{2,1,0:T(8,128)(2,1)S(1)} %get-tuple-element.20), channel_id=1, replica_groups=mesh['x'=4,'zh'=2,'y'=8,'zl'=4,'core'=2] {'y'}, dimensions={0} | all-to-all | bytes 851968 | tf_op jit(solution)/shard_map/all_to_all | solution.py:590
  110.9 1.2 chain_ring.1
  112.1 15.8 %all_to_all.22.recv_ref = bf16[8,144,128]{2,1,0:T(8,128)(2,1)S(1)} all-to-all(bf16[8,144,128]{2,1,0:T(8,128)(2,1)S(1)} %get-tuple-element.23), channel_id=1, replica_groups=mesh['x'=4,'zh'=2,'y'=8,'zl'=4,'core'=2] {'x','zh'}, dimensions={0} | all-to-all | bytes 589824 | tf_op jit(solution)/shard_map/all_to_all | solution.py:599
  127.9 0.0 copy-done.9
  127.9 4.3 %final_scan.1 = (bf16[256,512]{1,0:T(8,128)(2,1)}, bf16[256,512]{1,0:T(8,128)(2,1)}, bf16[256,512]{1,0:T(8,128)(2,1)}, f32[1,8,16]{2,1,0:T(8,128)}, f32[1,8,16]{2,1,0:T(8,128)}, /*index=5*/f32[1,8]{1,0:T(1,128)}) custom-call(s32[5]{0:T(128)S(1)} %copy-done.8, f32[3,8,128]{2,1,0:T(8,128)S(1)} %copy-done.9, bf16[8,144,128]{2,1,0:T(8,128)(2,1)S(1)} %all_to_all.22.recv_ref, ...), custom_call_target="tpu_custom_call" | custom-call | tf_op jit(solution)/shard_map/final_scan/pallas_call | solution.py:600
  (1 shorter events, 0.0 us)
Async XLA Ops:
  0.6 13.6 %collective-permute-start = (bf16[256,512]{1,0:T(8,128)(2,1)}, bf16[256,512]{1,0:T(8,128)(2,1)S(1)}, u32[]{:S(2)}, u32[]{:S(2)}) collective-permute-start(bf16[256,512]{1,0:T(8,128)(2,1)} %first_ref.1), channel_id=1, source_target_pairs={{0,1},{1,0},{2,3},{3,2},{4,5},{5,4},{6,7},{7,6},{8,9},{9,8},{10,11... | collective-permute-start | bytes 786440 | tf_op jit(solution)/shard_map/ppermute | solution.py:516
  4.3 20.3 %collective-permute-start.4 = (bf16[72,512]{1,0:T(8,128)(2,1)}, bf16[72,512]{1,0:T(8,128)(2,1)S(1)}, u32[]{:S(2)}, u32[]{:S(2)}) collective-permute-start(bf16[72,512]{1,0:T(8,128)(2,1)} %get-tuple-element.19.refs_0_.block_ref), channel_id=1, source_target_pairs={{0,64},{64,0},{1,65},{65,1},{2,66},{66,2},{3,67},{67,3},{4,68},{68... | collective-permute-start | bytes 221192 | tf_op jit(solution)/shard_map/ppermute | solution.py:515
  14.3 0.9 copy-start.5
  15.2 0.9 copy-start.6
  16.2 8.3 %copy-start = (bf16[2,256,512]{2,1,0:T(8,128)(2,1)}, bf16[2,256,512]{2,1,0:T(8,128)(2,1)S(1)}, u32[]{:S(2)}) copy-start(bf16[2,256,512]{2,1,0:T(8,128)(2,1)S(1)} %tile.1.tile_ref) | copy-start | bytes 1572868
  16.2 25.8 %collective-permute-start.2 = (bf16[2,256,512]{2,1,0:T(8,128)(2,1)S(1)}, bf16[2,256,512]{2,1,0:T(8,128)(2,1)S(1)}, u32[]{:S(2)}, u32[]{:S(2)}) collective-permute-start(bf16[2,256,512]{2,1,0:T(8,128)(2,1)S(1)} %tile.1.tile_ref), channel_id=1, source_target_pairs={{0,2},{1,7},{2,132},{3,129},{4,262},{5,259},{6,384},{7,389},{128,4... | collective-permute-start | bytes 1572872 | tf_op jit(solution)/shard_map/ppermute | solution.py:548
  20.5 22.2 %collective-permute-start.1 = (bf16[2,256,512]{2,1,0:T(8,128)(2,1)S(1)}, bf16[2,256,512]{2,1,0:T(8,128)(2,1)S(1)}, u32[]{:S(2)}, u32[]{:S(2)}) collective-permute-start(bf16[2,256,512]{2,1,0:T(8,128)(2,1)S(1)} %tile.1.tile_ref), channel_id=1, source_target_pairs={{0,0},{1,5},{2,130},{3,135},{4,260},{5,257},{6,390},{7,387},{128,2... | collective-permute-start | bytes 1572872 | tf_op jit(solution)/shard_map/ppermute | solution.py:548
  24.5 0.6 copy-start.14
  27.2 38.7 %all-to-all-start = ((bf16[8,136,512]{2,1,0:T(8,128)(2,1)}), bf16[8,136,512]{2,1,0:T(8,128)(2,1)S(1)}, u32[]{:S(2)}, u32[]{:S(2)}) async-start(bf16[8,136,512]{2,1,0:T(8,128)(2,1)} %spread.1), calls=%async_computation | async-start | bytes 2228224 | tf_op jit(solution)/shard_map/all_to_all | solution.py:538
  34.3 14.7 %copy-start.3 = (bf16[256,512]{1,0:T(8,128)(2,1)S(1)}, bf16[256,512]{1,0:T(8,128)(2,1)}, u32[]{:S(2)}) copy-start(bf16[256,512]{1,0:T(8,128)(2,1)} %values_ref.3) | copy-start | bytes 786436
  34.3 14.7 %copy-start.4 = (bf16[256,512]{1,0:T(8,128)(2,1)S(1)}, bf16[256,512]{1,0:T(8,128)(2,1)}, u32[]{:S(2)}) copy-start(bf16[256,512]{1,0:T(8,128)(2,1)} %gate_in_ref.3) | copy-start | bytes 786436
  34.3 31.6 %copy-start.8 = (s32[5]{0:T(128)S(1)}, s32[5]{0:T(128)}, u32[]{:S(2)}) copy-start(s32[5]{0:T(128)} %stack.23.place_ref) | copy-start | bytes 64
  42.0 0.8 copy-start.10
  42.8 0.8 copy-start.12
  43.5 1.0 copy-start.11
  44.6 1.0 copy-start.13
  45.7 5.6 %collective-permute-start.3 = (bf16[2,2,256,512]{3,2,1,0:T(8,128)(2,1)S(1)}, bf16[2,2,256,512]{3,2,1,0:T(8,128)(2,1)S(1)}, u32[]{:S(2)}, u32[]{:S(2)}) collective-permute-start(bf16[2,2,256,512]{3,2,1,0:T(8,128)(2,1)S(1)} %join.1.mine_ref), channel_id=1, source_target_pairs={{0,1},{1,0},{2,3},{3,2},{4,5},{5,4},{6,7},{7,6},{8,9},{9,8},{10,11... | collective-permute-start | bytes 3145736 | tf_op jit(solution)/shard_map/ppermute | solution.py:556
  51.3 1.0 copy-start.1
  65.9 1.2 copy-start.2
  69.0 19.6 %copy-start.7 = (bf16[256,512]{1,0:T(8,128)(2,1)S(1)}, bf16[256,512]{1,0:T(8,128)(2,1)}, u32[]{:S(2)}) copy-start(bf16[256,512]{1,0:T(8,128)(2,1)} %gate_out_ref.1) | copy-start | bytes 786436
  93.4 34.5 %copy-start.9 = (f32[3,8,128]{2,1,0:T(8,128)S(1)}, f32[3,8,128]{2,1,0:T(8,128)}, u32[]{:S(2)}) copy-start(f32[3,8,128]{2,1,0:T(8,128)} %get-tuple-element.18.own_ref) | copy-start | bytes 36868

commit v7 on v6

--- a/solution.py
+++ b/solution.py
@@ -106,8 +106,7 @@
     return slice(8 * m, 8 * m + 8)
 
 
-def product_kernel(place_ref, mine_ref, theirs_ref, proj_ref, v_rows, out_ref):
-    del v_rows
+def product_kernel(place_ref, mine_ref, theirs_ref, proj_ref, out_ref):
     core = place_ref[0]
     ring, height, cols = proj_ref.shape
     depth = (height - 8) // 2
@@ -555,21 +554,21 @@
     )(*mine)
     theirs = lax.ppermute(mine, "core", swap)
 
-    v_rows = call(
-        functools.partial(value_kernel, half), shape((half * 8, LANES), f32), [], "value_steps"
-    )(values, gate_in)
     height = rows + nzh * ny * pencil // 4
     parts = call(
         product_kernel,
         shape((nx, height, cols), bf16),
         [],
         "partial_products",
-        in_specs=[smem] + [vmem] * 3 + [pl.BlockSpec(memory_space=pl.ANY)],
-    )(place, mine, theirs, proj, v_rows)
+        in_specs=[smem] + [vmem] * 3,
+    )(place, mine, theirs, proj)
     parts = exchange(parts, "x")
 
     many = 4 * MODES
     groups = nx * nzh
+    v_rows = call(
+        functools.partial(value_kernel, half), shape((half * 8, LANES), f32), [], "value_steps"
+    )(values, gate_in)
     gated, tables, skip, g_rows, send, edge, rates, own_table = call(
         functools.partial(local_kernel, half),
         [

time: 133 us -> 131 us (0.985)
  waiting for transfers between devices: 23.4 us -> 44.5 us
  blocking collectives: 52.8 us -> 31.7 us
  local copies, waits for them, and re-layouts: 8.98 us -> 3.19 us
  starting transfers between devices: 30.1 us -> 33.4 us
    all_to_all x1 -> x0, blocking collectives: 19.6 us -> none  [per_device(): parts = exchange(parts, 'x')]
    all_to_all x0 -> x1, waiting for transfers between devices: none -> 16.6 us  [per_device(): parts = exchange(parts, 'x')]
    unnamed x30 -> x18, local copies, waits for them, and re-layouts: 8.37 us -> 2.52 us
    all_to_all x0 -> x1, starting transfers between devices: none -> 3.8 us  [per_device(): parts = exchange(parts, 'x')]
    all_to_all x1, waiting for transfers between devices: 13.7 us -> 17.3 us  [per_device(): proj = exchange(proj, 'y')]
    ppermute x1, starting transfers between devices: 3.33 us -> 1.92 us  [per_device(): theirs = lax.ppermute(mine, 'core', swap)]
  transfers between devices with their start and end apart: 6 -> 7, of which waited for: 3 -> 4; matrix products, arithmetic and copies ran while one was open for 0% -> 1% of each run, Pallas kernels for 3% -> 3%
where the time goes in v7:
time: 131 us
  waiting for transfers between devices  44.5 us (34%)
  starting transfers between devices  33.4 us (25%)
  blocking collectives  31.7 us (24%)
  Pallas kernels  17.2 us (13%)
  local copies, waits for them, and re-layouts  3.19 us (2%)
    all_to_all x1, waiting for transfers between devices, per_device(): proj = exchange(proj, 'y')  17.3 us
    all_to_all x1, blocking collectives, per_device(): recv = exchange(send, 'y')  17.2 us
    all_to_all x1, waiting for transfers between devices, per_device(): parts = exchange(parts, 'x')  16.6 us
    all_to_all x1, blocking collectives, per_device(): recv = exchange(send, ('x', 'zh'))  14.5 us
    ppermute x1, starting transfers between devices, per_device(): far = lax.ppermute(block, 'zh', swap)  10 us
    ppermute x2, starting transfers between devices, per_device(): mine.append(lax.ppermute(tile, ('x', 'zl', 'core'), moves))  8.62 us
    ppermute x2, waiting for transfers between devices, per_device(): mine.append(lax.ppermute(tile, ('x', 'zl', 'core'), moves))  7.99 us
    all_to_all x1, starting transfers between devices, per_device(): proj = exchange(proj, 'y')  7.1 us
  transfers between devices with their start and end apart: 7, of which 4 were waited for; matrix products, arithmetic and copies ran while one was open for 1% of the time, Pallas kernels for 3%

profile of v7, /device:TPU:64, one launch (start us, length us, event | category | flops | bytes accessed | tf_op | source)
XLA Modules:
  0.0 130.8 jit_solution(15543599029816133702)
XLA Ops:
  0.6 1.9 %collective-permute-start = (bf16[256,512]{1,0:T(8,128)(2,1)}, bf16[256,512]{1,0:T(8,128)(2,1)S(1)}, u32[]{:S(2)}, u32[]{:S(2)}) collective-permute-start(bf16[256,512]{1,0:T(8,128)(2,1)} %first_ref.1), channel_id=1, source_target_pairs={{0,1},{1,0},{2,3},{3,2},{4,5},{5,4},{6,7},{7,6},{8,9},{9,8},{10,11... | collective-permute-start | bytes 786440 | tf_op jit(solution)/shard_map/ppermute | solution.py:515
  2.6 1.7 %pack.1 = (bf16[72,512]{1,0:T(8,128)(2,1)}, f32[3,8,128]{2,1,0:T(8,128)}) custom-call(bf16[64,512]{1,0:T(8,128)(2,1)} %bitcast.8, f32[8,16]{1,0:T(8,128)} %bitcast.9, f32[8,16]{1,0:T(8,128)} %bitcast.10, f32[1,8]{1,0:T(1,128)} %refs_3_.1), custom_call_target="tpu_custom_call" | custom-call | tf_op jit(solution)/shard_map/pack/pallas_call | solution.py:502
  4.3 10.0 %collective-permute-start.4 = (bf16[72,512]{1,0:T(8,128)(2,1)}, bf16[72,512]{1,0:T(8,128)(2,1)S(1)}, u32[]{:S(2)}, u32[]{:S(2)}) collective-permute-start(bf16[72,512]{1,0:T(8,128)(2,1)} %get-tuple-element.19.refs_0_.block_ref), channel_id=1, source_target_pairs={{0,64},{64,0},{1,65},{65,1},{2,66},{66,2},{3,67},{67,3},{4,68},{68... | collective-permute-start | bytes 221192 | tf_op jit(solution)/shard_map/ppermute | solution.py:514
  14.3 0.0 collective-permute-done.second_ref
  14.3 0.0 copy-start.3
  14.3 0.9 copy-done.3
  15.2 0.0 copy-start.4
  15.2 0.9 copy-done.4
  16.2 0.0 copy-start
  16.2 3.4 %collective-permute-start.1 = (bf16[2,256,512]{2,1,0:T(8,128)(2,1)S(1)}, bf16[2,256,512]{2,1,0:T(8,128)(2,1)S(1)}, u32[]{:S(2)}, u32[]{:S(2)}) collective-permute-start(bf16[2,256,512]{2,1,0:T(8,128)(2,1)S(1)} %tile.1.tile_ref), channel_id=1, source_target_pairs={{0,0},{1,5},{2,130},{3,135},{4,260},{5,257},{6,390},{7,387},{128,2... | collective-permute-start | bytes 1572872 | tf_op jit(solution)/shard_map/ppermute | solution.py:547
  19.6 5.2 %collective-permute-start.2 = (bf16[2,256,512]{2,1,0:T(8,128)(2,1)S(1)}, bf16[2,256,512]{2,1,0:T(8,128)(2,1)S(1)}, u32[]{:S(2)}, u32[]{:S(2)}) collective-permute-start(bf16[2,256,512]{2,1,0:T(8,128)(2,1)S(1)} %tile.1.tile_ref), channel_id=1, source_target_pairs={{0,2},{1,7},{2,132},{3,129},{4,262},{5,259},{6,384},{7,389},{128,4... | collective-permute-start | bytes 1572872 | tf_op jit(solution)/shard_map/ppermute | solution.py:547
  24.9 0.7 stack.23.place_ref
  25.5 0.0 collective-permute-done.4.far_ref
  25.5 0.0 copy-done
  25.5 0.0 copy-start.8
  25.5 0.6 copy-done.8
  26.2 2.0 %spread.1 = bf16[8,136,512]{2,1,0:T(8,128)(2,1)} custom-call(s32[5]{0:T(128)} %stack.23.place_ref, bf16[72,512]{1,0:T(8,128)(2,1)} %get-tuple-element.19.refs_0_.block_ref, bf16[72,512]{1,0:T(8,128)(2,1)} %copy-done.8, bf16[2,256,512]{2,1,0:T(8,128)(2,1)} %copy-done), custom_call_target="tpu_custom_call" | custom-call | tf_op jit(solution)/shard_map/spread/pallas_call | solution.py:524
  28.2 7.1 %all-to-all-start = ((bf16[8,136,512]{2,1,0:T(8,128)(2,1)}), bf16[8,136,512]{2,1,0:T(8,128)(2,1)S(1)}, u32[]{:S(2)}, u32[]{:S(2)}) async-start(bf16[8,136,512]{2,1,0:T(8,128)(2,1)} %spread.1), calls=%async_computation | async-start | bytes 2228224 | tf_op jit(solution)/shard_map/all_to_all | solution.py:537
  35.3 0.0 copy-start.6
  35.3 0.0 collective-permute-done.1.first_ref
  35.3 8.0 %collective-permute-done.2.second_ref = bf16[2,256,512]{2,1,0:T(8,128)(2,1)S(1)} collective-permute-done((bf16[2,256,512]{2,1,0:T(8,128)(2,1)S(1)}, bf16[2,256,512]{2,1,0:T(8,128)(2,1)S(1)}, u32[]{:S(2)}, u32[]{:S(2)}) %collective-permute-start.2) | collective-permute-done | bytes 524320 | tf_op jit(solution)/shard_map/ppermute | solution.py:547
  43.3 0.1 join.1.mine_ref
  43.4 1.9 %collective-permute-start.3 = (bf16[2,2,256,512]{3,2,1,0:T(8,128)(2,1)S(1)}, bf16[2,2,256,512]{3,2,1,0:T(8,128)(2,1)S(1)}, u32[]{:S(2)}, u32[]{:S(2)}) collective-permute-start(bf16[2,2,256,512]{3,2,1,0:T(8,128)(2,1)S(1)} %join.1.mine_ref), channel_id=1, source_target_pairs={{0,1},{1,0},{2,3},{3,2},{4,5},{5,4},{6,7},{7,6},{8,9},{9,8},{10,11... | collective-permute-start | bytes 3145736 | tf_op jit(solution)/shard_map/ppermute | solution.py:555
  45.3 2.6 %collective-permute-done.3.theirs_ref = bf16[2,2,256,512]{3,2,1,0:T(8,128)(2,1)S(1)} collective-permute-done((bf16[2,2,256,512]{3,2,1,0:T(8,128)(2,1)S(1)}, bf16[2,2,256,512]{3,2,1,0:T(8,128)(2,1)S(1)}, u32[]{:S(2)}, u32[]{:S(2)}) %collective-permute-start.3) | collective-permute-done | bytes 1048608 | tf_op jit(solution)/shard_map/ppermute | solution.py:555
  47.9 17.3 %all-to-all-done.proj_ref = bf16[8,136,512]{2,1,0:T(8,128)(2,1)S(1)} async-done(((bf16[8,136,512]{2,1,0:T(8,128)(2,1)}), bf16[8,136,512]{2,1,0:T(8,128)(2,1)S(1)}, u32[]{:S(2)}, u32[]{:S(2)}) %all-to-all-start) | async-done | bytes 1114144 | tf_op jit(solution)/shard_map/all_to_all | solution.py:537
  65.2 0.0 copy-done.6
  65.2 2.8 %partial_products.1 = bf16[4,288,512]{2,1,0:T(8,128)(2,1)} custom-call(s32[5]{0:T(128)S(1)} %copy-done.6, bf16[2,2,256,512]{3,2,1,0:T(8,128)(2,1)S(1)} %join.1.mine_ref, bf16[2,2,256,512]{3,2,1,0:T(8,128)(2,1)S(1)} %collective-permute-done.3.theirs_ref, bf16[8,136,512]{2,1,0:T(8,128)(2,1)S(1)} %all-to-all-done.proj_ref), custom_call_target="tpu_custom_call" | custom-call | tf_op jit(solution)/shard_map/partial_products/pallas_call | solution.py:558
  68.0 0.0 copy-start.1
  68.0 0.0 copy-start.2
  68.0 0.0 copy-start.5
  68.0 3.8 %all-to-all-start.1 = ((bf16[4,288,512]{2,1,0:T(8,128)(2,1)}), bf16[4,288,512]{2,1,0:T(8,128)(2,1)S(1)}, u32[]{:S(2)}, u32[]{:S(2)}) async-start(bf16[4,288,512]{2,1,0:T(8,128)(2,1)} %partial_products.1), calls=%async_computation.1 | async-start | bytes 2359296 | tf_op jit(solution)/shard_map/all_to_all | solution.py:565
  71.8 0.0 copy-done.1
  71.8 0.0 copy-done.2
  71.8 0.1 value_steps.1.v_rows
  72.0 16.6 %all-to-all-done.1.parts_ref = bf16[4,288,512]{2,1,0:T(8,128)(2,1)S(1)} async-done(((bf16[4,288,512]{2,1,0:T(8,128)(2,1)}), bf16[4,288,512]{2,1,0:T(8,128)(2,1)S(1)}, u32[]{:S(2)}, u32[]{:S(2)}) %all-to-all-start.1) | async-done | bytes 1179680 | tf_op jit(solution)/shard_map/all_to_all | solution.py:565
  88.6 0.0 copy-done.5
  88.6 4.9 %local_scans.1 = (bf16[256,512]{1,0:T(8,128)(2,1)S(1)}, f32[3,128,128]{2,1,0:T(8,128)S(1)}, f32[8,128]{1,0:T(8,128)S(1)}, f32[1024,128]{1,0:T(8,128)S(1)}, bf16[...) custom-call(s32[5]{0:T(128)S(1)} %copy-done.6, ...), custom_call_target="tpu_custom_call" | custom-call | tf_op jit(solution)/shard_map/local_scans/pallas_call | solution.py:572
  93.5 0.0 copy-start.7
  93.5 17.2 %all_to_all.20.recv_ref = bf16[8,208,128]{2,1,0:T(8,128)(2,1)S(1)} all-to-all(bf16[8,208,128]{2,1,0:T(8,128)(2,1)S(1)} %get-tuple-element.20), channel_id=1, replica_groups=mesh['x'=4,'zh'=2,'y'=8,'zl'=4,'core'=2] {'y'}, dimensions={0} | all-to-all | bytes 851968 | tf_op jit(solution)/shard_map/all_to_all | solution.py:589
  110.7 1.2 chain_ring.1
  112.0 14.5 %all_to_all.21.recv_ref = bf16[8,144,128]{2,1,0:T(8,128)(2,1)S(1)} all-to-all(bf16[8,144,128]{2,1,0:T(8,128)(2,1)S(1)} %get-tuple-element.23), channel_id=1, replica_groups=mesh['x'=4,'zh'=2,'y'=8,'zl'=4,'core'=2] {'x','zh'}, dimensions={0} | all-to-all | bytes 589824 | tf_op jit(solution)/shard_map/all_to_all | solution.py:598
  126.5 0.0 copy-done.7
  126.5 4.3 %final_scan.1 = (bf16[256,512]{1,0:T(8,128)(2,1)}, bf16[256,512]{1,0:T(8,128)(2,1)}, bf16[256,512]{1,0:T(8,128)(2,1)}, f32[1,8,16]{2,1,0:T(8,128)}, f32[1,8,16]{2,1,0:T(8,128)}, /*index=5*/f32[1,8]{1,0:T(1,128)}) custom-call(s32[5]{0:T(128)S(1)} %copy-done.6, f32[3,8,128]{2,1,0:T(8,128)S(1)} %copy-done.7, bf16[8,144,128]{2,1,0:T(8,128)(2,1)S(1)} %all_to_all.21.recv_ref, ...), custom_call_target="tpu_custom_call" | custom-call | tf_op jit(solution)/shard_map/final_scan/pallas_call | solution.py:599
  (1 shorter events, 0.0 us)
Async XLA Ops:
  0.6 13.6 %collective-permute-start = (bf16[256,512]{1,0:T(8,128)(2,1)}, bf16[256,512]{1,0:T(8,128)(2,1)S(1)}, u32[]{:S(2)}, u32[]{:S(2)}) collective-permute-start(bf16[256,512]{1,0:T(8,128)(2,1)} %first_ref.1), channel_id=1, source_target_pairs={{0,1},{1,0},{2,3},{3,2},{4,5},{5,4},{6,7},{7,6},{8,9},{9,8},{10,11... | collective-permute-start | bytes 786440 | tf_op jit(solution)/shard_map/ppermute | solution.py:515
  4.3 21.3 %collective-permute-start.4 = (bf16[72,512]{1,0:T(8,128)(2,1)}, bf16[72,512]{1,0:T(8,128)(2,1)S(1)}, u32[]{:S(2)}, u32[]{:S(2)}) collective-permute-start(bf16[72,512]{1,0:T(8,128)(2,1)} %get-tuple-element.19.refs_0_.block_ref), channel_id=1, source_target_pairs={{0,64},{64,0},{1,65},{65,1},{2,66},{66,2},{3,67},{67,3},{4,68},{68... | collective-permute-start | bytes 221192 | tf_op jit(solution)/shard_map/ppermute | solution.py:514
  14.3 0.9 copy-start.3
  15.2 0.9 copy-start.4
  16.2 9.3 %copy-start = (bf16[2,256,512]{2,1,0:T(8,128)(2,1)}, bf16[2,256,512]{2,1,0:T(8,128)(2,1)S(1)}, u32[]{:S(2)}) copy-start(bf16[2,256,512]{2,1,0:T(8,128)(2,1)S(1)} %tile.1.tile_ref) | copy-start | bytes 1572868
  16.2 19.1 %collective-permute-start.1 = (bf16[2,256,512]{2,1,0:T(8,128)(2,1)S(1)}, bf16[2,256,512]{2,1,0:T(8,128)(2,1)S(1)}, u32[]{:S(2)}, u32[]{:S(2)}) collective-permute-start(bf16[2,256,512]{2,1,0:T(8,128)(2,1)S(1)} %tile.1.tile_ref), channel_id=1, source_target_pairs={{0,0},{1,5},{2,130},{3,135},{4,260},{5,257},{6,390},{7,387},{128,2... | collective-permute-start | bytes 1572872 | tf_op jit(solution)/shard_map/ppermute | solution.py:547
  19.6 23.7 %collective-permute-start.2 = (bf16[2,256,512]{2,1,0:T(8,128)(2,1)S(1)}, bf16[2,256,512]{2,1,0:T(8,128)(2,1)S(1)}, u32[]{:S(2)}, u32[]{:S(2)}) collective-permute-start(bf16[2,256,512]{2,1,0:T(8,128)(2,1)S(1)} %tile.1.tile_ref), channel_id=1, source_target_pairs={{0,2},{1,7},{2,132},{3,129},{4,262},{5,259},{6,384},{7,389},{128,4... | collective-permute-start | bytes 1572872 | tf_op jit(solution)/shard_map/ppermute | solution.py:547
  25.5 0.6 copy-start.8
  28.2 37.0 %all-to-all-start = ((bf16[8,136,512]{2,1,0:T(8,128)(2,1)}), bf16[8,136,512]{2,1,0:T(8,128)(2,1)S(1)}, u32[]{:S(2)}, u32[]{:S(2)}) async-start(bf16[8,136,512]{2,1,0:T(8,128)(2,1)} %spread.1), calls=%async_computation | async-start | bytes 2228224 | tf_op jit(solution)/shard_map/all_to_all | solution.py:537
  35.3 29.9 %copy-start.6 = (s32[5]{0:T(128)S(1)}, s32[5]{0:T(128)}, u32[]{:S(2)}) copy-start(s32[5]{0:T(128)} %stack.23.place_ref) | copy-start | bytes 64
  43.4 4.6 %collective-permute-start.3 = (bf16[2,2,256,512]{3,2,1,0:T(8,128)(2,1)S(1)}, bf16[2,2,256,512]{3,2,1,0:T(8,128)(2,1)S(1)}, u32[]{:S(2)}, u32[]{:S(2)}) collective-permute-start(bf16[2,2,256,512]{3,2,1,0:T(8,128)(2,1)S(1)} %join.1.mine_ref), channel_id=1, source_target_pairs={{0,1},{1,0},{2,3},{3,2},{4,5},{5,4},{6,7},{7,6},{8,9},{9,8},{10,11... | collective-permute-start | bytes 3145736 | tf_op jit(solution)/shard_map/ppermute | solution.py:555
  68.0 3.8 %copy-start.1 = (bf16[256,512]{1,0:T(8,128)(2,1)S(1)}, bf16[256,512]{1,0:T(8,128)(2,1)}, u32[]{:S(2)}) copy-start(bf16[256,512]{1,0:T(8,128)(2,1)} %values_ref.3) | copy-start | bytes 786436
  68.0 3.8 %copy-start.2 = (bf16[256,512]{1,0:T(8,128)(2,1)S(1)}, bf16[256,512]{1,0:T(8,128)(2,1)}, u32[]{:S(2)}) copy-start(bf16[256,512]{1,0:T(8,128)(2,1)} %gate_in_ref.3) | copy-start | bytes 786436
  68.0 20.6 %copy-start.5 = (bf16[256,512]{1,0:T(8,128)(2,1)S(1)}, bf16[256,512]{1,0:T(8,128)(2,1)}, u32[]{:S(2)}) copy-start(bf16[256,512]{1,0:T(8,128)(2,1)} %gate_out_ref.1) | copy-start | bytes 786436
  68.0 20.6 %all-to-all-start.1 = ((bf16[4,288,512]{2,1,0:T(8,128)(2,1)}), bf16[4,288,512]{2,1,0:T(8,128)(2,1)S(1)}, u32[]{:S(2)}, u32[]{:S(2)}) async-start(bf16[4,288,512]{2,1,0:T(8,128)(2,1)} %partial_products.1), calls=%async_computation.1 | async-start | bytes 2359296 | tf_op jit(solution)/shard_map/all_to_all | solution.py:565
  93.5 33.0 %copy-start.7 = (f32[3,8,128]{2,1,0:T(8,128)S(1)}, f32[3,8,128]{2,1,0:T(8,128)}, u32[]{:S(2)}) copy-start(f32[3,8,128]{2,1,0:T(8,128)} %get-tuple-element.18.own_ref) | copy-start | bytes 36868
